TPU v7x, 32 devices: a whole 2x2x4 slice. The times are simulated.
32 devices in a mesh: items: 8 (over z, x), pipe: 4 (over y, core).
Axes of the slice: x: 2, y: 2, z: 4, core: 2. Of those that a mesh axis runs over, the one named last changes fastest.
Arguments:
- text_in: bfloat16 [32, 2, 364, 768], P(('items', 'pipe')), may hold values from -6 to 6
- memory: bfloat16 [10, 768], P(None, 'pipe'), may hold values from -6 to 6
- w_qkv: bfloat16 [1536, 2304], P('pipe'), may hold values from -0.21875 to 0.21875
- w_o: bfloat16 [1536, 768], P('pipe'), may hold values from -0.875 to 0.875
- w_in: bfloat16 [1536, 3072], P('pipe'), may hold values from -0.21875 to 0.21875
- w_out: bfloat16 [6144, 768], P('pipe'), may hold values from -0.109375 to 0.109375
- gains: bfloat16 [3072], P('pipe'), may hold values from 0.5 to 1.5
- biases: bfloat16 [15360], P('pipe'), may hold values from -1.5 to 1.5
- counts: int32 [32], P('items'), may hold values from 1 to 2, as said below
- last_lengths: int32 [32], P('items'), may hold values from 91 to 364, as said below
- text_cot: bfloat16 [32, 2, 364, 768], P(('items', 'pipe')), may hold values from -6 to 6
- memory_cot: bfloat16 [32, 10, 768], P(('items', 'pipe')), may hold values from -6 to 6
Outputs:
- final_text: float32 [32, 2, 364, 768], P(('items', 'pipe'))
- final_memory: float32 [32, 10, 768], P(('items', 'pipe'))
- text_grad: float32 [32, 2, 364, 768], P(('items', 'pipe'))
- memory_grad: float32 [10, 768], P(None, 'pipe')
- qkv_grad: float32 [1536, 2304], P('pipe')
- out_proj_grad: float32 [1536, 768], P('pipe')
- up_grad: float32 [1536, 3072], P('pipe')
- down_grad: float32 [6144, 768], P('pipe')
- gains_grad: float32 [3072], P('pipe')
- biases_grad: float32 [15360], P('pipe')
Inputs may be any that keep to these rules, and one draw needn't show every extreme that they name: `counts`: some item has 2 segments and some has 1. `last_lengths`: some item reaches each end.
All inputs are finite; a program needn't handle non-finite values.
Results may differ from a plain program's by a relative error of at most 0.02.
Values may be sent and summed in bfloat16 or wider, within the bound.
A program may use at most 256 MiB of HBM per device.

v0:
```python
import jax
import jax.numpy as jnp
from jax import lax
from jax.sharding import PartitionSpec as P

D = 768
HEADS = 12
HEAD_DIM = 64
MEM = 10
TEXT = 364
MAXSEG = 2
IPD = 1
SEG = 384
MB = 2
UNITS = 4


epsilon = 1e-06
masked_score = -1000000000.0


def from_partner(x, axis, bit):
    return lax.ppermute(x, axis, [(i, i ^ 1 << bit) for i in range(lax.axis_size(axis))])


def exact_gelu(values):
    return jax.nn.gelu(values, approximate=False)


def over_rows(left, right):
    return lax.dot_general(
        left, right, (((0,), (0,)), ((), ())), preferred_element_type=jnp.float32
    )


def against(left, right):
    return lax.dot_general(
        left, right, (((1,), (1,)), ((), ())), preferred_element_type=jnp.float32
    )


def norm_parts(values):
    centre = values - jnp.mean(values, axis=-1, keepdims=True)
    inverse = lax.rsqrt(jnp.mean(centre * centre, axis=-1, keepdims=True) + epsilon)
    return (centre * inverse, inverse)


def norm_back(grad, normed, inverse, gain):
    scaled = grad * gain
    middle = jnp.mean(scaled, axis=-1, keepdims=True) + normed * jnp.mean(
        scaled * normed, axis=-1, keepdims=True
    )
    return (inverse * (scaled - middle), jnp.sum(grad * normed, axis=0), jnp.sum(grad, axis=0))


def vectors(params):
    gains, biases = (params[4], params[5])
    pieces = [biases[index * D : (index + 1) * D] for index in range(6)]
    return (gains[:D], gains[D:], pieces, biases[6 * D :])


def scores_of(packed, keymask):
    query = packed[:, :D].reshape(SEG, HEADS, HEAD_DIM)
    keyed = packed[:, D : 2 * D].reshape(SEG, HEADS, HEAD_DIM)
    raw = jnp.einsum(
        "qhd,khd->hqk", query, keyed, preferred_element_type=jnp.float32
    ) * HEAD_DIM ** (-0.5)
    return jnp.where(keymask[None, None, :], raw, masked_score)


def layer_forward(params, inputs, keymask):
    w_qkv, w_o, w_in, w_out = (params[0], params[1], params[2], params[3])
    gain_one, gain_two, pieces, up_bias = vectors(params)
    query_bias, value_bias, out_bias, shift_one, down_bias, shift_two = pieces
    mixed = jnp.dot(inputs, w_qkv, preferred_element_type=jnp.float32)
    packed = jnp.concatenate(
        [mixed[:, :D] + query_bias, mixed[:, D : 2 * D], mixed[:, 2 * D :] + value_bias], axis=1
    ).astype(jnp.bfloat16)
    scores = scores_of(packed, keymask)
    top = jnp.max(scores, axis=-1, keepdims=True)
    raised = jnp.exp(scores - top)
    total = jnp.sum(raised, axis=-1, keepdims=True)
    probs = (raised / total).astype(jnp.bfloat16)
    values = packed[:, 2 * D :].reshape(SEG, HEADS, HEAD_DIM)
    context = (
        jnp.einsum("hqk,khd->qhd", probs, values, preferred_element_type=jnp.float32)
        .reshape(SEG, D)
        .astype(jnp.bfloat16)
    )
    first_sum = (
        inputs.astype(jnp.float32)
        + jnp.dot(context, w_o, preferred_element_type=jnp.float32)
        + out_bias
    )
    normed_one, inverse_one = norm_parts(first_sum)
    hidden = normed_one * gain_one + shift_one
    upward = (
        jnp.dot(hidden.astype(jnp.bfloat16), w_in, preferred_element_type=jnp.float32) + up_bias
    )
    active = exact_gelu(upward).astype(jnp.bfloat16)
    second_sum = hidden + jnp.dot(active, w_out, preferred_element_type=jnp.float32) + down_bias
    normed_two, inverse_two = norm_parts(second_sum)
    output = normed_two * gain_two + shift_two
    cache = (
        packed,
        top + jnp.log(total),
        context,
        normed_one,
        inverse_one,
        upward,
        normed_two,
        inverse_two,
    )
    return (output, cache)


def layer_backward(params, inputs, cache, grad_out, keymask):
    w_qkv, w_o, w_in, w_out = (params[0], params[1], params[2], params[3])
    gain_one, gain_two, pieces, up_bias = vectors(params)
    shift_one = pieces[3]
    packed, log_total, context, normed_one, inverse_one, upward, normed_two, inverse_two = cache
    grad_second, grad_gain_two, grad_shift_two = norm_back(
        grad_out, normed_two, inverse_two, gain_two
    )
    grad_down = grad_second.astype(jnp.bfloat16)
    active = exact_gelu(upward).astype(jnp.bfloat16)
    grad_w_out = over_rows(active, grad_down)
    grad_active = against(grad_down, w_out)
    gelu_pull = jax.vjp(exact_gelu, upward)[1]
    grad_up = gelu_pull(grad_active)[0].astype(jnp.bfloat16)
    hidden = normed_one * gain_one + shift_one
    grad_w_in = over_rows(hidden.astype(jnp.bfloat16), grad_up)
    grad_hidden = grad_second + against(grad_up, w_in)
    grad_first, grad_gain_one, grad_shift_one = norm_back(
        grad_hidden, normed_one, inverse_one, gain_one
    )
    grad_branch = grad_first.astype(jnp.bfloat16)
    grad_w_o = over_rows(context, grad_branch)
    grad_context = against(grad_branch, w_o).astype(jnp.bfloat16).reshape(SEG, HEADS, HEAD_DIM)
    scores = scores_of(packed, keymask)
    probs = jnp.exp(scores - log_total)
    query = packed[:, :D].reshape(SEG, HEADS, HEAD_DIM)
    keyed = packed[:, D : 2 * D].reshape(SEG, HEADS, HEAD_DIM)
    values = packed[:, 2 * D :].reshape(SEG, HEADS, HEAD_DIM)
    grad_values = jnp.einsum(
        "hqk,qhd->khd", probs.astype(jnp.bfloat16), grad_context, preferred_element_type=jnp.float32
    )
    grad_probs = jnp.einsum(
        "qhd,khd->hqk", grad_context, values, preferred_element_type=jnp.float32
    )
    grad_scores = (
        probs * (grad_probs - jnp.sum(grad_probs * probs, axis=-1, keepdims=True))
    ).astype(jnp.bfloat16)
    scale = HEAD_DIM ** (-0.5)
    grad_query = (
        jnp.einsum("hqk,khd->qhd", grad_scores, keyed, preferred_element_type=jnp.float32) * scale
    )
    grad_keys = (
        jnp.einsum("hqk,qhd->khd", grad_scores, query, preferred_element_type=jnp.float32) * scale
    )
    grad_packed = jnp.concatenate(
        [grad_query.reshape(SEG, D), grad_keys.reshape(SEG, D), grad_values.reshape(SEG, D)], axis=1
    ).astype(jnp.bfloat16)
    packed_wide = grad_packed.astype(jnp.float32)
    grad_w_qkv = over_rows(inputs, grad_packed)
    grad_inputs = grad_first + against(grad_packed, w_qkv)
    grad_biases = jnp.concatenate(
        [
            jnp.sum(packed_wide[:, :D], axis=0),
            jnp.sum(packed_wide[:, 2 * D :], axis=0),
            jnp.sum(grad_branch.astype(jnp.float32), axis=0),
            grad_shift_one,
            jnp.sum(grad_down.astype(jnp.float32), axis=0),
            grad_shift_two,
            jnp.sum(grad_up.astype(jnp.float32), axis=0),
        ]
    )
    grad_gains = jnp.concatenate([grad_gain_one, grad_gain_two])
    return (grad_inputs, (grad_w_qkv, grad_w_o, grad_w_in, grad_w_out, grad_gains, grad_biases))


def split_half(array, member):
    size = array.shape[0] // 2
    lower, upper = (array[:size], array[size:])
    return (jnp.where(member == 0, lower, upper), jnp.where(member == 0, upper, lower))


def per_device(
    text_in,
    memory,
    w_qkv,
    w_o,
    w_in,
    w_out,
    gains,
    biases,
    counts,
    last_lengths,
    text_cot,
    memory_cot,
):
    place = lax.axis_index("pipe")
    first = place < 2
    member = place % 2
    owned = (w_qkv, w_o, w_in, w_out, gains, biases)
    partner_parts = from_partner((w_qkv, w_o, w_in, w_out, gains, biases), "pipe", 0)
    joined = [
        jnp.where(
            member == 0,
            jnp.concatenate([mine, other_half], 0),
            jnp.concatenate([other_half, mine], 0),
        )
        for mine, other_half in zip(owned, partner_parts)
    ]
    params = (
        joined[0],
        joined[1],
        joined[2],
        joined[3],
        joined[4].astype(jnp.float32),
        joined[5].astype(jnp.float32),
    )
    memory_full = lax.all_gather(memory, "pipe", axis=1, tiled=True)
    lower = member * IPD
    seg_counts = jnp.concatenate(
        [
            lax.dynamic_slice_in_dim(counts, lower, IPD),
            lax.dynamic_slice_in_dim(counts, lower + 2 * IPD, IPD),
        ]
    )
    tail_lengths = jnp.concatenate(
        [
            lax.dynamic_slice_in_dim(last_lengths, lower, IPD),
            lax.dynamic_slice_in_dim(last_lengths, lower + 2 * IPD, IPD),
        ]
    )
    outgoing = jnp.where(first, text_cot, text_in)
    incoming, memory_incoming = from_partner((outgoing, memory_cot), "pipe", 1)
    texts_all = jnp.concatenate([text_in, incoming], 0)
    cot_all = jnp.concatenate([incoming, text_cot], 0)
    memory_cot_all = jnp.concatenate([memory_incoming, memory_cot], 0).astype(jnp.float32)

    def unit_info(unit):
        inside = (unit >= 0) & (unit < UNITS)
        clipped = jnp.clip(unit, 0, UNITS - 1)
        item = clipped % MB
        segment = clipped // MB
        count = seg_counts[item]
        length = jnp.where(segment < count - 1, TEXT, tail_lengths[item])
        rows = jnp.arange(SEG)
        keymask = (rows < MEM) | (rows >= MEM + TEXT) | (rows - MEM < length)
        textmask = jnp.arange(TEXT) < length
        return (clipped, item, segment, keymask, textmask, inside & (segment < count), inside)

    slots = UNITS + 1
    empty_cache = ()

    def forward_turn(turn, carry):
        received, memory_state, stored, caches, final_all = carry
        unit = jnp.where(first, turn, turn - 1)
        clipped, item, segment, keymask, textmask, valid, inside = unit_info(unit)
        memory_now = memory_state[item]
        fresh = jnp.concatenate([memory_now, texts_all[item, segment], memory_now], 0)
        inputs = jnp.where(first, fresh, received)
        output, cache = layer_forward(params, inputs, keymask)
        sent = output.astype(jnp.bfloat16)
        slot = jnp.where(inside, clipped, UNITS)
        stored = lax.dynamic_update_index_in_dim(stored, inputs, slot, 0)
        text_rows = jnp.where(
            textmask[:, None] & valid, sent[MEM : MEM + TEXT].astype(jnp.float32), 0.0
        )
        update = jnp.where(first, final_all[item, segment], text_rows)
        final_all = lax.dynamic_update_slice(final_all, update[None, None], (item, segment, 0, 0))
        received = from_partner(sent, "pipe", 1)
        prior_clip, prior_item, prior_seg, prior_keys, prior_text, prior_valid, prior_inside = (
            unit_info(turn - 1)
        )
        source = jnp.where(first, received, sent)
        kept_memory = jnp.where(prior_valid, source[MEM + TEXT :], memory_state[prior_item])
        memory_state = lax.dynamic_update_index_in_dim(memory_state, kept_memory, prior_item, 0)
        return (received, memory_state, stored, caches, final_all)

    start = (
        jnp.zeros((SEG, D), jnp.bfloat16),
        jnp.broadcast_to(memory_full, (MB, MEM, D)),
        jnp.zeros((slots, SEG, D), jnp.bfloat16),
        empty_cache,
        jnp.zeros((MB, MAXSEG, TEXT, D), jnp.float32),
    )
    received, memory_state, stored, caches, final_all = lax.fori_loop(0, slots, forward_turn, start)

    def backward_turn(turn, carry):
        received, memory_grads, text_grads, memory_total, totals = carry
        unit = jnp.where(first, UNITS - turn, UNITS - 1 - turn)
        clipped, item, segment, keymask, textmask, valid, inside = unit_info(unit)
        text_rows = jnp.where(textmask[:, None], cot_all[item, segment].astype(jnp.float32), 0.0)
        upper = jnp.concatenate(
            [jnp.zeros((MEM, D), jnp.float32), text_rows, memory_grads[item]], 0
        )
        grad_out = jnp.where(valid, jnp.where(first, received.astype(jnp.float32), upper), 0.0)
        inputs = stored[clipped]
        cache = layer_forward(params, inputs, keymask)[1]
        grad_inputs, grads = layer_backward(params, inputs, cache, grad_out, keymask)
        totals = tuple((total + grad for total, grad in zip(totals, grads)))
        back = grad_inputs.astype(jnp.bfloat16)
        back_wide = back.astype(jnp.float32)
        write = first & valid
        update = jnp.where(write, back_wide[MEM : MEM + TEXT], text_grads[item, segment])
        text_grads = lax.dynamic_update_slice(text_grads, update[None, None], (item, segment, 0, 0))
        memory_total = memory_total + jnp.where(
            write & (segment == 0), back_wide[:MEM] + back_wide[MEM + TEXT :], 0.0
        )
        received = from_partner(back, "pipe", 1)
        done_clip, done_item, done_seg, done_keys, done_text, done_valid, done_inside = unit_info(
            UNITS - turn
        )
        arrived = received.astype(jnp.float32)
        newer = jnp.where(
            done_valid & jnp.logical_not(first),
            arrived[:MEM] + arrived[MEM + TEXT :],
            memory_grads[done_item],
        )
        memory_grads = lax.dynamic_update_index_in_dim(memory_grads, newer, done_item, 0)
        return (received, memory_grads, text_grads, memory_total, totals)

    zero_grads = tuple((jnp.zeros(part.shape, jnp.float32) for part in params))
    start = (
        jnp.zeros((SEG, D), jnp.bfloat16),
        memory_cot_all,
        jnp.zeros((MB, MAXSEG, TEXT, D), jnp.float32),
        jnp.zeros((MEM, D), jnp.float32),
        zero_grads,
    )
    received, memory_grads, text_grads, memory_total, totals = lax.fori_loop(
        0, slots, backward_turn, start
    )
    results_out = jnp.where(first, text_grads[IPD:], final_all[:IPD])
    returned = from_partner(results_out.astype(jnp.bfloat16), "pipe", 1).astype(results_out.dtype)
    final_text = jnp.where(first, returned, final_all[IPD:])
    text_grad = jnp.where(first, text_grads[:IPD], returned)
    final_memory = jnp.where(first, memory_state[:IPD], memory_state[IPD:]).astype(jnp.float32)
    memory_part = lax.psum_scatter(
        jnp.where(first, memory_total, 0.0), "pipe", scatter_dimension=1, tiled=True
    )
    split = [split_half(part, member) for part in totals]
    handed = [pair[1] for pair in split]
    partner_sums = (
        from_partner(handed[0].astype(jnp.bfloat16), "pipe", 0).astype(jnp.float32),
        from_partner(handed[1].astype(jnp.bfloat16), "pipe", 0).astype(jnp.float32),
        from_partner(handed[2].astype(jnp.bfloat16), "pipe", 0).astype(jnp.float32),
        from_partner(handed[3].astype(jnp.bfloat16), "pipe", 0).astype(jnp.float32),
        from_partner(handed[4].astype(jnp.bfloat16), "pipe", 0).astype(jnp.float32),
        from_partner(handed[5].astype(jnp.bfloat16), "pipe", 0).astype(jnp.float32),
    )
    summed = [pair[0] + other_sum for pair, other_sum in zip(split, partner_sums)]
    reduced = lax.psum(
        (summed[0], summed[1], summed[2], summed[3], summed[4], summed[5], memory_part), "items"
    )
    return (
        final_text,
        final_memory,
        text_grad,
        reduced[6],
        reduced[0],
        reduced[1],
        reduced[2],
        reduced[3],
        reduced[4],
        reduced[5],
    )


def solution(mesh):
    placed = (
        P(("items", "pipe"), None, None, None),
        P(None, "pipe"),
        P("pipe", None),
        P("pipe", None),
        P("pipe", None),
        P("pipe", None),
        P("pipe"),
        P("pipe"),
        P("items"),
        P("items"),
        P(("items", "pipe"), None, None, None),
        P(("items", "pipe"), None, None),
    )
    return jax.shard_map(
        per_device,
        mesh=mesh,
        in_specs=placed,
        out_specs=(
            P(("items", "pipe"), None, None, None),
            P(("items", "pipe"), None, None),
            P(("items", "pipe"), None, None, None),
            P(None, "pipe"),
            P("pipe", None),
            P("pipe", None),
            P("pipe", None),
            P("pipe", None),
            P("pipe"),
            P("pipe"),
        ),
        check_vma=False,
    )
```

profile of v0, /device:TPU:0, one launch (start us, length us, event | category | flops | bytes accessed | tf_op | source)
XLA Modules:
  0.0 1752.3 jit_solution(3370617535803006957)
XLA Ops:
  19.0 20.6 %collective-permute-done.2 = bf16[1,10,768]{2,1,0:T(8,128)(2,1)S(1)} collective-permute-done((bf16[1,10,768]{2,1,0:T(8,128)(2,1)}, bf16[1,10,768]{2,1,0:T(8,128)(2,1)S(1)}, u32[]{:S(2)}, u32[]{:S(2)}) %collective-permute-start.2) | collective-permute-done | bytes 15392 | tf_op jit(solution)/shard_map/ppermute | solution.py:23
  84.8 365.4 %while.57 = (s32[]{:T(128)}, bf16[384,768]{1,0:T(8,128)(2,1)}, bf16[2,10,768]{2,1,0:T(8,128)(2,1)S(1)}, bf16[5,384,768]{2,1,0:T(8,128)(2,1)}, f32[2,2,364,768]{3...) while((s32[]{:T(128)}, bf16[384,768]{1,0:T(8,128)(2,1)}, ...), condition=%wide.region_7.8_spmd, body=%wide.region_0.7_spmd.sunk | while | flops 5989635584 | bytes 72845008 | solution.py:290
  122.6 17.4 fusion.273
  149.2 20.6 %dynamic_update_slice.70 = f32[2,2,364,768]{3,1,2,0:T(2,128)} dynamic-update-slice(f32[2,2,364,768]{3,1,2,0:T(2,128)} %get-tuple-element.1746, f32[1,1,364,768]{3,1,2,0:T(1,128)S(1)} %copy.124, s32[]{:T(128)S(6)} %select_n.904, s32[]{:T(128)S(6)} %select_n.906, s32[]{:T(128)} %constant.1093.clone.1..sunk, s32[]{:T(128)} %constant.1093.clone.1..sunk) | dynamic-update-slice | bytes 2236420 | tf_op jit(solution)/shard_map/while/body/eval_jaxpr/dynamic_update_slice | solution.py:273
  193.3 17.4 fusion.273
  218.5 20.5 %dynamic_update_slice.70 = f32[2,2,364,768]{3,1,2,0:T(2,128)} dynamic-update-slice(f32[2,2,364,768]{3,1,2,0:T(2,128)} %get-tuple-element.1746, f32[1,1,364,768]{3,1,2,0:T(1,128)S(1)} %copy.124, s32[]{:T(128)S(6)} %select_n.904, s32[]{:T(128)S(6)} %select_n.906, s32[]{:T(128)} %constant.1093.clone.1..sunk, s32[]{:T(128)} %constant.1093.clone.1..sunk) | dynamic-update-slice | bytes 2236420 | tf_op jit(solution)/shard_map/while/body/eval_jaxpr/dynamic_update_slice | solution.py:273
  262.6 17.4 fusion.273
  288.7 20.6 %dynamic_update_slice.70 = f32[2,2,364,768]{3,1,2,0:T(2,128)} dynamic-update-slice(f32[2,2,364,768]{3,1,2,0:T(2,128)} %get-tuple-element.1746, f32[1,1,364,768]{3,1,2,0:T(1,128)S(1)} %copy.124, s32[]{:T(128)S(6)} %select_n.904, s32[]{:T(128)S(6)} %select_n.906, s32[]{:T(128)} %constant.1093.clone.1..sunk, s32[]{:T(128)} %constant.1093.clone.1..sunk) | dynamic-update-slice | bytes 2236420 | tf_op jit(solution)/shard_map/while/body/eval_jaxpr/dynamic_update_slice | solution.py:273
  332.8 17.4 fusion.273
  358.0 20.5 %dynamic_update_slice.70 = f32[2,2,364,768]{3,1,2,0:T(2,128)} dynamic-update-slice(f32[2,2,364,768]{3,1,2,0:T(2,128)} %get-tuple-element.1746, f32[1,1,364,768]{3,1,2,0:T(1,128)S(1)} %copy.124, s32[]{:T(128)S(6)} %select_n.904, s32[]{:T(128)S(6)} %select_n.906, s32[]{:T(128)} %constant.1093.clone.1..sunk, s32[]{:T(128)} %constant.1093.clone.1..sunk) | dynamic-update-slice | bytes 2236420 | tf_op jit(solution)/shard_map/while/body/eval_jaxpr/dynamic_update_slice | solution.py:273
  402.1 17.4 fusion.273
  428.2 20.5 %dynamic_update_slice.70 = f32[2,2,364,768]{3,1,2,0:T(2,128)} dynamic-update-slice(f32[2,2,364,768]{3,1,2,0:T(2,128)} %get-tuple-element.1746, f32[1,1,364,768]{3,1,2,0:T(1,128)S(1)} %copy.124, s32[]{:T(128)S(6)} %select_n.904, s32[]{:T(128)S(6)} %select_n.906, s32[]{:T(128)} %constant.1093.clone.1..sunk, s32[]{:T(128)} %constant.1093.clone.1..sunk) | dynamic-update-slice | bytes 2236420 | tf_op jit(solution)/shard_map/while/body/eval_jaxpr/dynamic_update_slice | solution.py:273
  454.4 792.7 %while.58 = (s32[]{:T(128)}, bf16[384,768]{1,0:T(8,128)(2,1)}, f32[2,10,768]{2,1,0:T(8,128)S(1)}, f32[2,2,364,768]{3,1,2,0:T(2,128)}, f32[10,768]{1,0:T(8,128)},...) while((s32[]{:T(128)}, bf16[384,768]{1,0:T(8,128)(2,1)}, ...), condition=%wide.region_29.30_spmd.clone, body=%wide.region_8.29_spmd.clone.sunk | while | flops 17851322368 | bytes 523644352 | solution.py:334
  497.6 14.7 multiply_convert_fusion.4
  579.8 20.6 %dynamic_update_slice.72 = f32[2,2,364,768]{3,1,2,0:T(2,128)} dynamic-update-slice(f32[2,2,364,768]{3,1,2,0:T(2,128)} %get-tuple-element.1820, f32[1,1,364,768]{3,1,2,0:T(1,128)} %copy.130, s32[]{:T(128)S(6)} %select_n.921, s32[]{:T(128)S(6)} %select_n.923, s32[]{:T(128)} %constant.1093.clone.1..sunk.1, s32[]{:T(128)} %constant.1093.clone.1..sunk.1) | dynamic-update-slice | bytes 2236420 | tf_op jit(solution)/shard_map/while/body/eval_jaxpr/dynamic_update_slice | solution.py:309
  733.0 20.6 %dynamic_update_slice.72 = f32[2,2,364,768]{3,1,2,0:T(2,128)} dynamic-update-slice(f32[2,2,364,768]{3,1,2,0:T(2,128)} %get-tuple-element.1820, f32[1,1,364,768]{3,1,2,0:T(1,128)} %copy.130, s32[]{:T(128)S(6)} %select_n.921, s32[]{:T(128)S(6)} %select_n.923, s32[]{:T(128)} %constant.1093.clone.1..sunk.1, s32[]{:T(128)} %constant.1093.clone.1..sunk.1) | dynamic-update-slice | bytes 2236420 | tf_op jit(solution)/shard_map/while/body/eval_jaxpr/dynamic_update_slice | solution.py:309
  798.8 14.7 multiply_convert_fusion.4
  886.5 20.6 %dynamic_update_slice.72 = f32[2,2,364,768]{3,1,2,0:T(2,128)} dynamic-update-slice(f32[2,2,364,768]{3,1,2,0:T(2,128)} %get-tuple-element.1820, f32[1,1,364,768]{3,1,2,0:T(1,128)} %copy.130, s32[]{:T(128)S(6)} %select_n.921, s32[]{:T(128)S(6)} %select_n.923, s32[]{:T(128)} %constant.1093.clone.1..sunk.1, s32[]{:T(128)} %constant.1093.clone.1..sunk.1) | dynamic-update-slice | bytes 2236420 | tf_op jit(solution)/shard_map/while/body/eval_jaxpr/dynamic_update_slice | solution.py:309
  952.3 14.7 multiply_convert_fusion.4
  1042.0 20.6 %dynamic_update_slice.72 = f32[2,2,364,768]{3,1,2,0:T(2,128)} dynamic-update-slice(f32[2,2,364,768]{3,1,2,0:T(2,128)} %get-tuple-element.1820, f32[1,1,364,768]{3,1,2,0:T(1,128)} %copy.130, s32[]{:T(128)S(6)} %select_n.921, s32[]{:T(128)S(6)} %select_n.923, s32[]{:T(128)} %constant.1093.clone.1..sunk.1, s32[]{:T(128)} %constant.1093.clone.1..sunk.1) | dynamic-update-slice | bytes 2236420 | tf_op jit(solution)/shard_map/while/body/eval_jaxpr/dynamic_update_slice | solution.py:309
  1107.7 14.7 multiply_convert_fusion.4
  1195.5 20.6 %dynamic_update_slice.72 = f32[2,2,364,768]{3,1,2,0:T(2,128)} dynamic-update-slice(f32[2,2,364,768]{3,1,2,0:T(2,128)} %get-tuple-element.1820, f32[1,1,364,768]{3,1,2,0:T(1,128)} %copy.130, s32[]{:T(128)S(6)} %select_n.921, s32[]{:T(128)S(6)} %select_n.923, s32[]{:T(128)} %constant.1093.clone.1..sunk.1, s32[]{:T(128)} %constant.1093.clone.1..sunk.1) | dynamic-update-slice | bytes 2236420 | tf_op jit(solution)/shard_map/while/body/eval_jaxpr/dynamic_update_slice | solution.py:309
  1299.1 40.8 %all-reduce = (f32[10,192]{1,0:T(8,128)}, f32[768]{0:T(1024)}, f32[3840]{0:T(1024)}) all-reduce(f32[10,192]{1,0:T(8,128)S(1)} %copy.94, f32[768]{0:T(1024)S(1)} %convert_add_fusion.5, f32[3840]{0:T(1024)S(1)} %convert_add_fusion.4), channel_id=1, replica_groups=mesh['items'=8,'pipe'=4] {'items'}, use_global_device_ids=true, to_apply=%region_31.32 | all-reduce | flops 6528 | bytes 52224 | tf_op jit(solution)/shard_map/psum | solution.py:356
  1344.9 388.8 %all-reduce.4.cloned.1.call-done = (f32[384,2304]{1,0:T(8,128)}, f32[384,768]{1,0:T(8,128)}, f32[384,3072]{1,0:T(8,128)}, f32[1536,768]{1,0:T(8,128)}) async-done(((f32[384,2304]{1,0:T(8,128)}, f32[384,768]{1,0:T(8,128)}, f32[384,3072]{1,0:T(8,128)}, f32[1536,768]{1,0:T(8,128)}), (f32[384,2304]{1,0:T(8,128)}, f32[384,768]{1,0:T(8,128)}, f32[384,3072]{1,0:T(8,128)}, ...) | async-done | bytes 14155792 | tf_op jit(solution)/shard_map/psum | solution.py:356
  (1322 shorter events, 859.2 us)
Async XLA Ops:
  8.1 1290.1 %reduce-scatter.4.cloned.1.call-start = ((), (), s32[]{:S(2)}) async-start(), calls=%async_computation.1 | async-start | bytes 491520
  8.1 58.0 %collective-permute-start.8 = (bf16[384,3072]{1,0:T(8,128)(2,1)}, bf16[384,3072]{1,0:T(8,128)(2,1)}, u32[]{:S(2)}, u32[]{:S(2)}) collective-permute-start(bf16[384,3072]{1,0:T(8,128)(2,1)} %param.20), channel_id=1, source_target_pairs={{0,1},{1,0},{2,3},{3,2},{4,5},{5,4},{6,7},{7,6},{8,9},{9,8},{10,11... | collective-permute-start | bytes 7077896 | tf_op jit(solution)/shard_map/ppermute | solution.py:23
  11.1 40.0 %collective-permute-start.3 = (bf16[1,2,364,768]{3,1,2,0:T(2,128)(2,1)}, bf16[1,2,364,768]{3,1,2,0:T(2,128)(2,1)}, u32[]{:S(2)}, u32[]{:S(2)}) collective-permute-start(bf16[1,2,364,768]{3,1,2,0:T(2,128)(2,1)} %bitcast.116), channel_id=1, source_target_pairs={{0,2},{1,3},{2,0},{3,1},{4,6},{5,7},{6,4},{7,5},{8,10},{9,11},{10,... | collective-permute-start | bytes 3354632 | tf_op jit(solution)/shard_map/ppermute | solution.py:23
  13.7 48.6 %collective-permute-start.4 = (bf16[384,2304]{1,0:T(8,128)(2,1)}, bf16[384,2304]{1,0:T(8,128)(2,1)}, u32[]{:S(2)}, u32[]{:S(2)}) collective-permute-start(bf16[384,2304]{1,0:T(8,128)(2,1)} %param.18), channel_id=1, source_target_pairs={{0,1},{1,0},{2,3},{3,2},{4,5},{5,4},{6,7},{7,6},{8,9},{9,8},{10,11... | collective-permute-start | bytes 5308424 | tf_op jit(solution)/shard_map/ppermute | solution.py:23
  13.7 3.9 collective-permute-start.5
  17.3 31.9 %collective-permute-start.6 = (bf16[384,768]{1,0:T(8,128)(2,1)}, bf16[384,768]{1,0:T(8,128)(2,1)}, u32[]{:S(2)}, u32[]{:S(2)}) collective-permute-start(bf16[384,768]{1,0:T(8,128)(2,1)} %param.19), channel_id=1, source_target_pairs={{0,1},{1,0},{2,3},{3,2},{4,5},{5,4},{6,7},{7,6},{8,9},{9,8},{10,11... | collective-permute-start | bytes 1769480 | tf_op jit(solution)/shard_map/ppermute | solution.py:23
  17.6 21.9 %collective-permute-start.2 = (bf16[1,10,768]{2,1,0:T(8,128)(2,1)}, bf16[1,10,768]{2,1,0:T(8,128)(2,1)S(1)}, u32[]{:S(2)}, u32[]{:S(2)}) collective-permute-start(bf16[1,10,768]{2,1,0:T(8,128)(2,1)} %param.27), channel_id=1, source_target_pairs={{0,2},{1,3},{2,0},{3,1},{4,6},{5,7},{6,4},{7,5},{8,10},{9,11},{10,... | collective-permute-start | bytes 46088 | tf_op jit(solution)/shard_map/ppermute | solution.py:23
  39.6 33.2 %collective-permute-start.9 = (bf16[1536,768]{1,0:T(8,128)(2,1)}, bf16[1536,768]{1,0:T(8,128)(2,1)}, u32[]{:S(2)}, u32[]{:S(2)}) collective-permute-start(bf16[1536,768]{1,0:T(8,128)(2,1)} %param.21), channel_id=1, source_target_pairs={{0,1},{1,0},{2,3},{3,2},{4,5},{5,4},{6,7},{7,6},{8,9},{9,8},{10,11... | collective-permute-start | bytes 7077896 | tf_op jit(solution)/shard_map/ppermute | solution.py:23
  141.9 28.5 %collective-permute-start = (bf16[384,768]{1,0:T(8,128)(2,1)S(1)}, bf16[384,768]{1,0:T(8,128)(2,1)}, u32[]{:S(2)}, u32[]{:S(2)}) collective-permute-start(bf16[384,768]{1,0:T(8,128)(2,1)S(1)} %add_convert_fusion.3), channel_id=1, source_target_pairs={{0,2},{1,3},{2,0},{3,1},{4,6},{5,7},{6,4},{7,5},{8,10},{9,11},{10,... | collective-permute-start | bytes 1769480 | tf_op jit(solution)/shard_map/while/body/eval_jaxpr/ppermute | solution.py:23
  212.6 27.0 %collective-permute-start = (bf16[384,768]{1,0:T(8,128)(2,1)S(1)}, bf16[384,768]{1,0:T(8,128)(2,1)}, u32[]{:S(2)}, u32[]{:S(2)}) collective-permute-start(bf16[384,768]{1,0:T(8,128)(2,1)S(1)} %add_convert_fusion.3), channel_id=1, source_target_pairs={{0,2},{1,3},{2,0},{3,1},{4,6},{5,7},{6,4},{7,5},{8,10},{9,11},{10,... | collective-permute-start | bytes 1769480 | tf_op jit(solution)/shard_map/while/body/eval_jaxpr/ppermute | solution.py:23
  281.9 27.9 %collective-permute-start = (bf16[384,768]{1,0:T(8,128)(2,1)S(1)}, bf16[384,768]{1,0:T(8,128)(2,1)}, u32[]{:S(2)}, u32[]{:S(2)}) collective-permute-start(bf16[384,768]{1,0:T(8,128)(2,1)S(1)} %add_convert_fusion.3), channel_id=1, source_target_pairs={{0,2},{1,3},{2,0},{3,1},{4,6},{5,7},{6,4},{7,5},{8,10},{9,11},{10,... | collective-permute-start | bytes 1769480 | tf_op jit(solution)/shard_map/while/body/eval_jaxpr/ppermute | solution.py:23
  352.1 27.1 %collective-permute-start = (bf16[384,768]{1,0:T(8,128)(2,1)S(1)}, bf16[384,768]{1,0:T(8,128)(2,1)}, u32[]{:S(2)}, u32[]{:S(2)}) collective-permute-start(bf16[384,768]{1,0:T(8,128)(2,1)S(1)} %add_convert_fusion.3), channel_id=1, source_target_pairs={{0,2},{1,3},{2,0},{3,1},{4,6},{5,7},{6,4},{7,5},{8,10},{9,11},{10,... | collective-permute-start | bytes 1769480 | tf_op jit(solution)/shard_map/while/body/eval_jaxpr/ppermute | solution.py:23
  421.4 27.9 %collective-permute-start = (bf16[384,768]{1,0:T(8,128)(2,1)S(1)}, bf16[384,768]{1,0:T(8,128)(2,1)}, u32[]{:S(2)}, u32[]{:S(2)}) collective-permute-start(bf16[384,768]{1,0:T(8,128)(2,1)S(1)} %add_convert_fusion.3), channel_id=1, source_target_pairs={{0,2},{1,3},{2,0},{3,1},{4,6},{5,7},{6,4},{7,5},{8,10},{9,11},{10,... | collective-permute-start | bytes 1769480 | tf_op jit(solution)/shard_map/while/body/eval_jaxpr/ppermute | solution.py:23
  555.8 66.0 %collective-permute-start.1 = (bf16[384,768]{1,0:T(8,128)(2,1)}, bf16[384,768]{1,0:T(8,128)(2,1)}, u32[]{:S(2)}, u32[]{:S(2)}) collective-permute-start(bf16[384,768]{1,0:T(8,128)(2,1)} %get-tuple-element.1707), channel_id=1, source_target_pairs={{0,2},{1,3},{2,0},{3,1},{4,6},{5,7},{6,4},{7,5},{8,10},{9,11},{10,... | collective-permute-start | bytes 1769480 | tf_op jit(solution)/shard_map/while/body/eval_jaxpr/ppermute | solution.py:23
  701.6 75.6 %collective-permute-start.1 = (bf16[384,768]{1,0:T(8,128)(2,1)}, bf16[384,768]{1,0:T(8,128)(2,1)}, u32[]{:S(2)}, u32[]{:S(2)}) collective-permute-start(bf16[384,768]{1,0:T(8,128)(2,1)} %get-tuple-element.1707), channel_id=1, source_target_pairs={{0,2},{1,3},{2,0},{3,1},{4,6},{5,7},{6,4},{7,5},{8,10},{9,11},{10,... | collective-permute-start | bytes 1769480 | tf_op jit(solution)/shard_map/while/body/eval_jaxpr/ppermute | solution.py:23
  857.0 73.7 %collective-permute-start.1 = (bf16[384,768]{1,0:T(8,128)(2,1)}, bf16[384,768]{1,0:T(8,128)(2,1)}, u32[]{:S(2)}, u32[]{:S(2)}) collective-permute-start(bf16[384,768]{1,0:T(8,128)(2,1)} %get-tuple-element.1707), channel_id=1, source_target_pairs={{0,2},{1,3},{2,0},{3,1},{4,6},{5,7},{6,4},{7,5},{8,10},{9,11},{10,... | collective-permute-start | bytes 1769480 | tf_op jit(solution)/shard_map/while/body/eval_jaxpr/ppermute | solution.py:23
  1010.5 75.7 %collective-permute-start.1 = (bf16[384,768]{1,0:T(8,128)(2,1)}, bf16[384,768]{1,0:T(8,128)(2,1)}, u32[]{:S(2)}, u32[]{:S(2)}) collective-permute-start(bf16[384,768]{1,0:T(8,128)(2,1)} %get-tuple-element.1707), channel_id=1, source_target_pairs={{0,2},{1,3},{2,0},{3,1},{4,6},{5,7},{6,4},{7,5},{8,10},{9,11},{10,... | collective-permute-start | bytes 1769480 | tf_op jit(solution)/shard_map/while/body/eval_jaxpr/ppermute | solution.py:23
  1166.0 73.6 %collective-permute-start.1 = (bf16[384,768]{1,0:T(8,128)(2,1)}, bf16[384,768]{1,0:T(8,128)(2,1)}, u32[]{:S(2)}, u32[]{:S(2)}) collective-permute-start(bf16[384,768]{1,0:T(8,128)(2,1)} %get-tuple-element.1707), channel_id=1, source_target_pairs={{0,2},{1,3},{2,0},{3,1},{4,6},{5,7},{6,4},{7,5},{8,10},{9,11},{10,... | collective-permute-start | bytes 1769480 | tf_op jit(solution)/shard_map/while/body/eval_jaxpr/ppermute | solution.py:23
  1251.7 16.2 collective-permute-start.11
  1257.5 16.4 collective-permute-start.13
  1258.1 8.6 collective-permute-start.12
  1263.8 18.4 %collective-permute-start.14 = (bf16[1536,768]{1,0:T(8,128)(2,1)}, bf16[1536,768]{1,0:T(8,128)(2,1)}, u32[]{:S(2)}, u32[]{:S(2)}) collective-permute-start(bf16[1536,768]{1,0:T(8,128)(2,1)} %select_convert_fusion), channel_id=1, source_target_pairs={{0,1},{1,0},{2,3},{3,2},{4,5},{5,4},{6,7},{7,6},{8,9},{9,8},{10,11... | collective-permute-start | bytes 7077896 | tf_op jit(solution)/shard_map/ppermute | solution.py:23
  1266.6 467.2 %all-reduce.4.cloned.1.call-start = ((), (), s32[]{:S(2)}) async-start(), calls=%async_computation.2 | async-start | bytes 28311552 | tf_op jit(solution)/shard_map/psum | solution.py:356
  1293.9 46.0 %collective-permute-start.10 = (bf16[1,2,364,768]{3,1,2,0:T(2,128)(2,1)S(1)}, bf16[1,2,364,768]{3,1,2,0:T(2,128)(2,1)S(1)}, u32[]{:S(2)}, u32[]{:S(2)}) collective-permute-start(bf16[1,2,364,768]{3,1,2,0:T(2,128)(2,1)S(1)} %select_convert_fusion.3), channel_id=1, source_target_pairs={{0,2},{1,3},{2,0},{3,1},{4,6},{5,7},{6,4},{7,5},{8,10},{9,11},{10,... | collective-permute-start | bytes 3354632 | tf_op jit(solution)/shard_map/ppermute | solution.py:23
  (359 other events, 3298.1 us)
Sparse Core Ops, SparseCore 0:
  1266.7 22.5 reduce-scatter.3
Sparse Core Ops, SparseCore 1:
  1289.7 444.0 all-reduce.3
where the time goes:
time: 1780 us; the launch traced here: 1750 us
  matrix products  543 us (31%)
  waiting for transfers between devices  413 us (23%)
  local copies, waits for them, and re-layouts  398 us (22%)
  other arithmetic  240 us (13%)
  loops' own time  75.4 us (4%)
  blocking collectives  46.4 us (3%)
  starting transfers between devices  21.1 us (1%)
    psum x1, waiting for transfers between devices, per_device(): lax.psum((summed[0], summed[1], summed[2], summed[3], summed[4], summed[5...  389 us
    dot_general x20, matrix products, over_rows(): lax.dot_general(left, right, (((0,), (0,)), ((), ())), preferred_element_...  135 us
    dynamic_update_slice x10, local copies, waits for them, and re-layouts, backward_turn(): lax.dynamic_update_slice(text_grads, update[None, None], (item, segment,...  114 us
    dynamic_update_slice x10, local copies, waits for them, and re-layouts, forward_turn(): lax.dynamic_update_slice(final_all, update[None, None], (item, segment, 0...  108 us
    dot_general x10, matrix products, layer_forward(): jnp.dot(active, w_out, preferred_element_type=jnp.float32)  97.8 us
    dot_general x5, matrix products, layer_forward(): jnp.dot(hidden.astype(jnp.bfloat16), w_in, preferred_element_type=jnp.flo...  73.4 us
    dot_general x20, matrix products, against(): lax.dot_general(left, right, (((1,), (1,)), ((), ())), preferred_element_...  70.6 us
    while x700, local copies, waits for them, and re-layouts  57.4 us
  transfers between devices with their start and end apart: 27, of which 4 were waited for; matrix products, arithmetic and copies ran while one was open for 32% of the time, Pallas kernels for 0%

commit v1 on v0

v1 whole, which is shorter than its diff:
```python
import functools

import jax
import jax.numpy as jnp
from jax import lax
from jax.experimental import pallas as pl
from jax.experimental.pallas import tpu as pltpu
from jax.sharding import PartitionSpec as P

D = 768
FF = 3072
MEM = 10
TEXT = 364
SEG = 384
PAIRS = 6
LANE = 128
TAIL = 32
UNITS = 4
LOG2E = 1.4426950408889634
MASKED = -1.0e9
EPS = 1e-6
MESH = pl.DeviceIdType.MESH
BF = jnp.bfloat16
F32 = jnp.float32
G1, BQ, BV, BO, N1, BD, G2, N2, BI = 0, 1, 2, 3, 4, 5, 8, 9, 10
BLOCKS = [slice(128 * b, 128 * b + 128) for b in range(3)]


def nn(left, right):
    return jnp.dot(left, right, preferred_element_type=F32)


def nt(left, right):
    return lax.dot_general(left, right, (((1,), (1,)), ((), ())), preferred_element_type=F32)


def tn(left, right):
    return lax.dot_general(left, right, (((0,), (0,)), ((), ())), preferred_element_type=F32)


def gelu_parts(up):
    t = pl.reciprocal(1.0 + (0.3275911 * 0.7071067811865476) * jnp.abs(up), approx=True)
    poly = t * (
        0.127414796
        + t * (-0.142248368 + t * (0.7107068705 + t * (-0.7265760135 + t * 0.5307027145)))
    )
    bell = jnp.exp2(up * up * (-0.5 * LOG2E))
    half = poly * bell
    phi = jnp.where(up >= 0, 1.0 - half, half)
    return up * phi, phi + up * bell * 0.3989422804014327


def norm_parts(values):
    centre = values - jnp.mean(values, axis=-1, keepdims=True)
    inverse = lax.rsqrt(jnp.mean(centre * centre, axis=-1, keepdims=True) + EPS)
    return centre * inverse, inverse


def norm_back(grad, normed, inverse, gain):
    scaled = grad * gain
    middle = jnp.mean(scaled, axis=-1, keepdims=True)
    along = jnp.mean(scaled * normed, axis=-1, keepdims=True)
    return inverse * (scaled - middle - normed * along)


def row_sum(values):
    return jnp.sum(values, axis=0, keepdims=True)


def split_stack(dst, src):
    low = lax.broadcasted_iota(jnp.int32, (SEG, LANE), 1) < 64
    zero = jnp.zeros((SEG, LANE), BF)
    dst[:SEG, :LANE] = jnp.where(low, src, zero)
    dst[SEG:, :LANE] = jnp.where(low, zero, src)


def tail_matrix(spread):
    row = lax.broadcasted_iota(jnp.int32, (TAIL, TAIL), 0)
    col = lax.broadcasted_iota(jnp.int32, (TAIL, TAIL), 1)
    if spread:
        keep = ((row >= 22) & (col == row)) | ((row >= 12) & (row < 22) & (col == row + 10))
    else:
        keep = (row >= 22) & ((col == row) | (col == row - 10))
    return jnp.where(keep, 1.0, 0.0).astype(BF)


def relay_kernel(
    x_own,
    c_own,
    mem0,
    mc_own,
    flags,
    kmask,
    w_qkv,
    w_o,
    w_in,
    w_out,
    vec_own,
    xs,
    ctxs,
    hids,
    acts,
    tops,
    gds,
    gus,
    gbs,
    gps,
    backs,
    vecg,
    wq,
    wo,
    wi,
    wd,
    vec,
    xin,
    gsl,
    mcs,
    trx,
    packed,
    st,
    n1s,
    n2s,
    dgs,
    ctx,
    sc,
    sd,
    big,
    stk,
    stv,
    rhs,
    hid,
    outb,
    gdb,
    delta,
    w_local,
    w_send,
    w_recv,
    e_local,
    e_send,
    e_recv,
    mid_send,
    mid_recv,
    tail_send,
    tail_recv,
    grad_send,
    grad_recv,
    x_sem,
    ctx_sem,
    gu_sem,
    gp_sem,
    hid_sem,
    act_sem,
    gd_sem,
    out_sem,
):
    place = lax.axis_index("pipe")
    first = place < 2
    member = lax.rem(place, 2)
    twin = {"pipe": place + 1 - 2 * member}
    other = {"pipe": lax.rem(place + 2, 4)}

    barrier = pltpu.get_barrier_semaphore()
    pl.semaphore_signal(barrier, inc=1, device_id=twin, device_id_type=MESH)
    pl.semaphore_signal(barrier, inc=1, device_id=other, device_id_type=MESH)
    pl.semaphore_wait(barrier, 2)

    def remote(src, dst, send, recv, to):
        return pltpu.make_async_remote_copy(
            src_ref=src, dst_ref=dst, send_sem=send, recv_sem=recv, device_id=to, device_id_type=MESH
        )

    halves = (
        (vec_own, vec, 8),
        (w_qkv, wq, D // 2),
        (w_o, wo, D // 2),
        (w_in, wi, D // 2),
        (w_out, wd, FF // 2),
    )
    locals_, sends, recvs = [], [], []
    for index, (src, dst, rows) in enumerate(halves):
        mine = dst.at[pl.ds(pl.multiple_of(member * rows, rows), rows)]
        theirs = dst.at[pl.ds(pl.multiple_of((1 - member) * rows, rows), rows)]
        locals_.append(pltpu.make_async_copy(src, mine, w_local.at[index]))
        sends.append(remote(src, mine, w_send.at[index], w_recv.at[index], twin))
        recvs.append(remote(src, theirs, w_send.at[index], w_recv.at[index], twin))
    x_home = [pltpu.make_async_copy(x_own.at[k], xin.at[2 * k], e_local.at[k]) for k in range(2)]
    x_away = [
        remote(x_own.at[k], xin.at[2 * k + 1], e_send.at[k], e_recv.at[k], other) for k in range(2)
    ]
    c_home = [
        pltpu.make_async_copy(c_own.at[k], gsl.at[2 * k + 1], e_local.at[k]) for k in range(2)
    ]
    c_away = [
        remote(c_own.at[k], gsl.at[2 * k], e_send.at[k], e_recv.at[k], other) for k in range(2)
    ]
    m_home = pltpu.make_async_copy(mc_own, mcs.at[1], e_local.at[2])
    m_away = remote(mc_own, mcs.at[0], e_send.at[2], e_recv.at[2], other)

    @pl.when(first)
    def _():
        for copy in x_home:
            copy.start()

    for index in (0, 1):
        locals_[index].start()
        sends[index].start()
    for index in (2, 3, 4):
        locals_[index].start()
        sends[index].start()

    @pl.when(first)
    def _():
        for copy in c_away:
            copy.start()
        m_away.start()

    @pl.when(jnp.logical_not(first))
    def _():
        for copy in x_away:
            copy.start()
        for copy in c_home:
            copy.start()
        m_home.start()

    rhs[...] = jnp.zeros_like(rhs)
    ones_row = lax.broadcasted_iota(jnp.int32, (2 * SEG, LANE), 0)
    ones_col = lax.broadcasted_iota(jnp.int32, (2 * SEG, LANE), 1)
    ones = jnp.where(ones_col == jnp.where(ones_row < SEG, 0, 1), 1.0, 0.0).astype(BF)
    for b in range(2):
        stv[b, :, LANE:] = ones
    vecg[...] = jnp.zeros_like(vecg)
    low = lax.broadcasted_iota(jnp.int32, (SEG, LANE), 1) < 64

    def v(row):
        return vec[row : row + 1, :]

    def out_copies(u, buf, results):
        return pltpu.make_async_copy(outb.at[buf], results.at[u], out_sem.at[buf])

    def mid_copy(u, buf):
        return remote(outb.at[buf], xin.at[u], mid_send.at[buf], mid_recv.at[u], other)

    def grad_copy(u, buf):
        return remote(outb.at[buf], gsl.at[u], grad_send.at[buf], grad_recv.at[u], other)

    def tail_copy(item, buf):
        src = outb.at[buf, pl.ds(SEG - TAIL, TAIL)]
        return remote(src, trx.at[item], tail_send.at[item], tail_recv.at[item], other)

    def wait_weights(index):
        locals_[index].wait()
        sends[index].wait_send()
        recvs[index].wait_recv()

    def forward_turn(u, carry):
        item = lax.rem(u, 2)
        buf = lax.rem(u, 2)

        @pl.when(first & (u == 0))
        def _():
            for copy in x_home:
                copy.wait()

        @pl.when(first & (u == 1))
        def _():
            for copy in x_away:
                copy.wait_recv()

        @pl.when(first & (u < 2))
        def _():
            xin[u, SEG - TAIL :, :] = xin[u, SEG - TAIL :, :] + mem0[...]

        @pl.when(first & (u >= 2))
        def _():
            tail_copy(item, buf).wait_recv()
            spread = nn(tail_matrix(True), trx[item]).astype(BF)
            xin[u, SEG - TAIL :, :] = xin[u, SEG - TAIL :, :] + spread

        @pl.when(jnp.logical_not(first))
        def _():
            mid_copy(u, buf).wait_recv()

        pltpu.make_async_copy(xin.at[u], xs.at[u], x_sem.at[u]).start()

        @pl.when(u == 0)
        def _():
            wait_weights(0)
            wait_weights(1)

        mask = kmask[u]
        x = xin[u]
        packed[u, :, :D] = (nn(x, wq[:, :D]) + v(BQ)).astype(BF) * 0.125
        packed[u, :, D : 2 * D] = nn(x, wq[:, D : 2 * D]).astype(BF)
        packed[u, :, 2 * D :] = (nn(x, wq[:, 2 * D :]) + v(BV)).astype(BF)

        @pl.when(u > 0)
        def _():
            hid_copy(u).wait()
            act_copy(u).wait()

        def scores(p):
            b = p % 2
            split_stack(stk.at[b], packed[u, :, D + p * LANE : D + (p + 1) * LANE])
            split_stack(stv.at[b], packed[u, :, 2 * D + p * LANE : 2 * D + (p + 1) * LANE])
            sc[b] = nt(packed[u, :, p * LANE : (p + 1) * LANE], stk[b])

        scores(0)
        for p in range(PAIRS):
            b = p % 2
            if p + 1 < PAIRS:
                scores(p + 1)
            for rows in BLOCKS:
                for h in range(2):
                    cols = slice(h * SEG, (h + 1) * SEG)
                    scaled = sc[b, rows, cols] * LOG2E + mask
                    top = jnp.max(scaled, axis=-1, keepdims=True)
                    big[b * 2 * SEG + rows.start : b * 2 * SEG + rows.stop, cols] = jnp.exp2(
                        scaled - top
                    ).astype(BF)
                    st[u, rows, 2 * p + h : 2 * p + h + 1] = top
            mixed = nn(big[b * 2 * SEG : b * 2 * SEG + SEG, :], stv[b])
            total = mixed[:, LANE : LANE + 2]
            share = 1.0 / total
            ctx[u, :, p * LANE : (p + 1) * LANE] = (
                mixed[:, :LANE] * jnp.where(low, share[:, :1], share[:, 1:])
            ).astype(BF)
            st[u, :, 2 * p : 2 * p + 2] = st[u, :, 2 * p : 2 * p + 2] + jnp.log2(total)
        pltpu.make_async_copy(ctx.at[u], ctxs.at[u], ctx_sem.at[u]).start()

        @pl.when(u == 0)
        def _():
            wait_weights(2)

        sd[0] = nn(ctx[u], wo[...])
        for rows in BLOCKS:
            normed, inverse = norm_parts(xin[u, rows, :].astype(F32) + sd[0, rows, :] + v(BO))
            n1s[u, rows, :] = normed
            st[u, rows, 12:13] = inverse
            hid[rows, :] = (normed * v(G1) + v(N1)).astype(BF)
        hid_copy(u).start()

        @pl.when(u == 0)
        def _():
            wait_weights(3)
            wait_weights(4)

        def up(j):
            sd[j % 2] = nn(hid[...], wi[:, j * D : (j + 1) * D])

        up(0)
        for j in range(4):
            if j + 1 < 4:
                up(j + 1)
            for rows in BLOCKS:
                act, slope = gelu_parts(sd[j % 2, rows, :] + v(BI + j))
                big[j * SEG + rows.start : j * SEG + rows.stop, :] = act.astype(BF)
                dgs[u, rows, j * D : (j + 1) * D] = slope.astype(BF)
            part = nn(big[j * SEG : (j + 1) * SEG, :], wd[j * D : (j + 1) * D, :])
            sc[0] = part if j == 0 else sc[0] + part
        act_copy(u).start()

        @pl.when(u >= 2)
        def _():
            out_copies(u, buf, tops).wait()

        @pl.when((u >= 2) & first)
        def _():
            mid_copy(u, buf).wait_send()

        @pl.when((u >= 2) & jnp.logical_not(first))
        def _():
            tail_copy(item, buf).wait_send()

        for rows in BLOCKS:
            hidden = n1s[u, rows, :] * v(G1) + v(N1)
            normed, inverse = norm_parts(hidden + sc[0, rows, :] + v(BD))
            n2s[u, rows, :] = normed
            st[u, rows, 13:14] = inverse
            outb[buf, rows, :] = (normed * v(G2) + v(N2)).astype(BF)

        @pl.when(first)
        def _():
            mid_copy(u, buf).start()

        @pl.when(jnp.logical_not(first) & (u < 2))
        def _():
            tail_copy(item, buf).start()

        out_copies(u, buf, tops).start()
        return carry

    def hid_copy(u):
        return pltpu.make_async_copy(hid, hids.at[u], hid_sem)

    def act_copy(u):
        return pltpu.make_async_copy(big, acts.at[u], act_sem)

    lax.fori_loop(0, UNITS, forward_turn, 0)

    hid_copy(0).wait()
    act_copy(0).wait()
    for u in range(UNITS):
        pltpu.make_async_copy(ctx.at[u], ctxs.at[u], ctx_sem.at[u]).wait()
    for buf in range(2):
        out_copies(2 + buf, buf, tops).wait()

    @pl.when(first)
    def _():
        for buf in range(2):
            mid_copy(2 + buf, buf).wait_send()
        for copy in c_away:
            copy.wait_send()
        m_away.wait_send()

    @pl.when(jnp.logical_not(first))
    def _():
        for copy in x_away:
            copy.wait_send()
        for copy in c_home:
            copy.wait()
        for copy in c_away:
            copy.wait_recv()
        m_home.wait()
        m_away.wait_recv()

    def gd_copy(u):
        return pltpu.make_async_copy(gdb.at[0], gds.at[u], gd_sem.at[0])

    def gb_copy(u):
        return pltpu.make_async_copy(gdb.at[1], gbs.at[u], gd_sem.at[1])

    def backward_turn(turn, carry):
        u = UNITS - 1 - turn
        item = lax.rem(u, 2)
        buf = lax.rem(u, 2)

        @pl.when(first)
        def _():
            grad_copy(u, buf).wait_recv()

        sd[0] = gsl[u].astype(F32)

        @pl.when(jnp.logical_not(first) & (u >= 2))
        def _():
            sd[0, SEG - TAIL :, :] = sd[0, SEG - TAIL :, :] + mcs[item, 0]

        @pl.when(jnp.logical_not(first) & (u < 2))
        def _():
            tail_copy(item, buf).wait_recv()
            arrived = nn(tail_matrix(False), trx[item])
            sd[0, SEG - TAIL :, :] = (
                sd[0, SEG - TAIL :, :] + arrived * flags[item] + mcs[item, 1]
            )

        @pl.when(turn > 0)
        def _():
            gd_copy(u).wait()
            gb_copy(u).wait()

        for rows in BLOCKS:
            grad = sd[0, rows, :]
            normed = n2s[u, rows, :]
            second = norm_back(grad, normed, st[u, rows, 13:14], v(G2))
            sc[0, rows, :] = second
            down = second.astype(BF)
            gdb[0, rows, :] = down
            vecg[G2 : G2 + 1, :] += row_sum(grad * normed)
            vecg[N2 : N2 + 1, :] += row_sum(grad)
            vecg[BD : BD + 1, :] += row_sum(down.astype(F32))
        gd_copy(u).start()
        for j in range(4):
            sd[j % 2] = nt(gdb[0], wd[j * D : (j + 1) * D, :])
            for rows in BLOCKS:
                cols = slice(j * D, (j + 1) * D)
                lifted = (sd[j % 2, rows, :] * dgs[u, rows, cols].astype(F32)).astype(BF)
                dgs[u, rows, cols] = lifted
                vecg[BI + j : BI + j + 1, :] += row_sum(lifted.astype(F32))
        pltpu.make_async_copy(dgs.at[u], gus.at[u], gu_sem.at[u]).start()
        sd[0] = nt(dgs[u], wi[...])
        for rows in BLOCKS:
            grad = sc[0, rows, :] + sd[0, rows, :]
            normed = n1s[u, rows, :]
            first_grad = norm_back(grad, normed, st[u, rows, 12:13], v(G1))
            branch = first_grad.astype(BF)
            gdb[1, rows, :] = branch
            vecg[G1 : G1 + 1, :] += row_sum(grad * normed)
            vecg[N1 : N1 + 1, :] += row_sum(grad)
            vecg[BO : BO + 1, :] += row_sum(branch.astype(F32))
            n1s[u, rows, :] = first_grad
        gb_copy(u).start()
        head = lax.broadcasted_iota(jnp.int32, (D, LANE), 0) // 64
        heads = (head == lax.broadcasted_iota(jnp.int32, (D, LANE), 1)).astype(F32).astype(BF)
        grad_ctx = nt(gdb[1], wo[...]).astype(BF)
        product = grad_ctx.astype(F32) * ctx[u].astype(F32)
        high = product.astype(BF)
        rest = (product - high.astype(F32)).astype(BF)
        delta[...] = nn(high, heads) + nn(rest, heads)
        ctx[u] = grad_ctx
        mask = kmask[u]

        def scores(p):
            b = p % 2
            query = packed[u, :, p * LANE : (p + 1) * LANE]
            grad = ctx[u, :, p * LANE : (p + 1) * LANE]
            split_stack(stk.at[b], packed[u, :, D + p * LANE : D + (p + 1) * LANE])
            split_stack(stv.at[b], packed[u, :, 2 * D + p * LANE : 2 * D + (p + 1) * LANE])
            rhs[b, :SEG, :LANE] = grad
            rhs[b, SEG:, LANE:] = query
            sc[b] = nt(query, stk[b])
            sd[b] = nt(grad, stv[b, :, :LANE])

        scores(0)
        for p in range(PAIRS):
            b = p % 2
            base = b * 2 * SEG
            if p + 1 < PAIRS:
                scores(p + 1)
            for rows in BLOCKS:
                for h in range(2):
                    cols = slice(h * SEG, (h + 1) * SEG)
                    one = slice(2 * p + h, 2 * p + h + 1)
                    probs = jnp.exp2(sc[b, rows, cols] * LOG2E + mask - st[u, rows, one])
                    big[base + rows.start : base + rows.stop, cols] = probs.astype(BF)
                    big[base + SEG + rows.start : base + SEG + rows.stop, cols] = (
                        probs * (sd[b, rows, cols] - delta[rows, one])
                    ).astype(BF)
            packed[u, :, p * LANE : (p + 1) * LANE] = (
                nn(big[base + SEG : base + 2 * SEG, :], stk[b]) * 0.125
            ).astype(BF)
            both = tn(big[base : base + 2 * SEG, :], rhs[b])
            packed[u, :, D + p * LANE : D + (p + 1) * LANE] = jnp.where(
                low, both[:SEG, LANE:], both[SEG:, LANE:]
            ).astype(BF)
            packed[u, :, 2 * D + p * LANE : 2 * D + (p + 1) * LANE] = jnp.where(
                low, both[:SEG, :LANE], both[SEG:, :LANE]
            ).astype(BF)
        pltpu.make_async_copy(packed.at[u], gps.at[u], gp_sem.at[u]).start()
        for rows in BLOCKS:
            vecg[BQ : BQ + 1, :] += row_sum(packed[u, rows, :D].astype(F32))
            vecg[BV : BV + 1, :] += row_sum(packed[u, rows, 2 * D :].astype(F32))
        sd[0] = nt(packed[u], wq[...])

        @pl.when(turn >= 2)
        def _():
            out_copies(u, buf, backs).wait()

        @pl.when((turn >= 2) & first)
        def _():
            tail_copy(item, buf).wait_send()

        @pl.when((turn >= 2) & jnp.logical_not(first))
        def _():
            grad_copy(u, buf).wait_send()

        for rows in BLOCKS:
            outb[buf, rows, :] = (n1s[u, rows, :] + sd[0, rows, :]).astype(BF)

        @pl.when(jnp.logical_not(first))
        def _():
            grad_copy(u, buf).start()

        @pl.when(first & (u >= 2))
        def _():
            tail_copy(item, buf).start()

        out_copies(u, buf, backs).start()
        return carry

    lax.fori_loop(0, UNITS, backward_turn, 0)

    gd_copy(0).wait()
    gb_copy(0).wait()
    for u in range(UNITS):
        pltpu.make_async_copy(xin.at[u], xs.at[u], x_sem.at[u]).wait()
        pltpu.make_async_copy(dgs.at[u], gus.at[u], gu_sem.at[u]).wait()
        pltpu.make_async_copy(packed.at[u], gps.at[u], gp_sem.at[u]).wait()
    for buf in range(2):
        out_copies(buf, buf, backs).wait()

    @pl.when(jnp.logical_not(first))
    def _():
        for buf in range(2):
            grad_copy(buf, buf).wait_send()


def relay(operands):
    rows = (UNITS, SEG, D)
    shape = jax.ShapeDtypeStruct
    hbm = pl.BlockSpec(memory_space=pl.ANY)
    vmem = pl.BlockSpec(memory_space=pltpu.VMEM)
    results = (
        shape(rows, BF),
        shape(rows, BF),
        shape(rows, BF),
        shape((UNITS, 4 * SEG, D), BF),
        shape(rows, BF),
        shape(rows, BF),
        shape((UNITS, SEG, FF), BF),
        shape(rows, BF),
        shape((UNITS, SEG, 3 * D), BF),
        shape(rows, BF),
        shape((16, D), F32),
    )
    scratch = [
        pltpu.VMEM((D, 3 * D), BF),
        pltpu.VMEM((D, D), BF),
        pltpu.VMEM((D, FF), BF),
        pltpu.VMEM((FF, D), BF),
        pltpu.VMEM((16, D), F32),
        pltpu.VMEM(rows, BF),
        pltpu.VMEM(rows, BF),
        pltpu.VMEM((2, 2, TAIL, D), F32),
        pltpu.VMEM((2, TAIL, D), BF),
        pltpu.VMEM((UNITS, SEG, 3 * D), BF),
        pltpu.VMEM((UNITS, SEG, LANE), F32),
        pltpu.VMEM(rows, F32),
        pltpu.VMEM(rows, F32),
        pltpu.VMEM((UNITS, SEG, FF), BF),
        pltpu.VMEM(rows, BF),
        pltpu.VMEM((2, SEG, D), F32),
        pltpu.VMEM((2, SEG, D), F32),
        pltpu.VMEM((4 * SEG, D), BF),
        pltpu.VMEM((2, 2 * SEG, LANE), BF),
        pltpu.VMEM((2, 2 * SEG, 2 * LANE), BF),
        pltpu.VMEM((2, 2 * SEG, 2 * LANE), BF),
        pltpu.VMEM((SEG, D), BF),
        pltpu.VMEM((2, SEG, D), BF),
        pltpu.VMEM((2, SEG, D), BF),
        pltpu.VMEM((SEG, LANE), F32),
    ]
    counts = [5, 5, 5, 3, 3, 3, 2, 4, 2, 2, 2, 4, 4, 4, 4, 4, 0, 0, 2, 2]
    scratch += [pltpu.SemaphoreType.DMA((n,)) if n else pltpu.SemaphoreType.DMA for n in counts]
    in_specs = [hbm, hbm, vmem, hbm, vmem, vmem, hbm, hbm, hbm, hbm, hbm]
    return pl.pallas_call(
        relay_kernel,
        out_shape=results,
        in_specs=in_specs,
        out_specs=tuple([hbm] * 10 + [vmem]),
        scratch_shapes=scratch,
        compiler_params=pltpu.CompilerParams(
            collective_id=0, has_side_effects=True, vmem_limit_bytes=63 * 2**20
        ),
        cost_estimate=pl.CostEstimate(flops=80 * 10**9, bytes_accessed=80 * 2**20, transcendentals=0),
    )(*operands)


def from_partner(x, axis, bit):
    return lax.ppermute(x, axis, [(i, i ^ 1 << bit) for i in range(lax.axis_size(axis))])


def over_rows(left, right):
    return lax.dot_general(
        left, right, (((0, 1), (0, 1)), ((), ())), preferred_element_type=F32
    )


def per_device(
    text_in,
    memory,
    w_qkv,
    w_o,
    w_in,
    w_out,
    gains,
    biases,
    counts,
    last_lengths,
    text_cot,
    memory_cot,
):
    place = lax.axis_index("pipe")
    first = place < 2
    member = place % 2
    pad = ((0, 0), (0, SEG - TEXT), (0, 0))

    count = counts[place]
    lengths = jnp.stack([jnp.where(count > 1, TEXT, last_lengths[place]), last_lengths[place]])
    two = count > 1
    valid = jnp.stack([jnp.bool_(True), two])
    shown = (jnp.arange(TEXT)[None, :] < lengths[:, None]) & valid[:, None]
    x_own = jnp.pad(text_in[0], pad)
    c_own = jnp.pad(jnp.where(shown[:, :, None], text_cot[0], jnp.zeros_like(text_cot[0])), pad)
    memory_full = lax.all_gather(memory, "pipe", axis=1, tiled=True)
    mem0 = jnp.pad(jnp.concatenate([memory_full, memory_full], 0), ((TAIL - 2 * MEM, 0), (0, 0)))
    placed = jnp.pad(memory_cot[0].astype(F32), ((TAIL - MEM, 0), (0, 0)))
    mc_own = jnp.stack([jnp.where(two, placed, 0.0), jnp.where(two, 0.0, placed)])
    pair_counts = jnp.stack([counts[member], counts[member + 2]])
    pair_last = jnp.stack([last_lengths[member], last_lengths[member + 2]])
    flags = jnp.broadcast_to((pair_counts > 1).astype(F32)[:, None, None], (2, 1, D))
    unit_lengths = jnp.concatenate([jnp.where(pair_counts > 1, TEXT, pair_last), pair_last])
    rows = jnp.arange(SEG)
    keep = (rows[None, :] >= TEXT) | (rows[None, :] < unit_lengths[:, None])
    kmask = jnp.where(keep, 0.0, MASKED).astype(F32)[:, None, :]
    vec_own = jnp.concatenate(
        [gains[None], biases.reshape(5, D), jnp.zeros((2, D), gains.dtype)], 0
    ).astype(F32)

    xs, ctxs, hids, acts, tops, gds, gus, gbs, gps, backs, vecg = relay(
        (x_own, c_own, mem0, mc_own, flags, kmask, w_qkv, w_o, w_in, w_out, vec_own)
    )

    outgoing = jnp.where(first, backs[1::2], tops[0::2])
    returned = from_partner(outgoing, "pipe", 1)
    own_top = jnp.where(first, returned, tops[1::2])
    own_back = jnp.where(first, backs[0::2], returned)
    final_text = jnp.where(shown[:, :, None], own_top[:, :TEXT].astype(F32), 0.0)[None]
    text_grad = own_back[:, :TEXT].astype(F32)[None]
    ends = own_top[:, SEG - MEM :].astype(F32)
    final_memory = jnp.where(two, ends[1], ends[0])[None]

    starts = backs[:2, TEXT:].astype(F32)
    memory_part = jnp.where(first, jnp.sum(starts[:, :MEM] + starts[:, MEM:], axis=0), 0.0)
    memory_part = lax.psum_scatter(memory_part, "pipe", scatter_dimension=1, tiled=True)

    def halves(left, right):
        size = left.shape[-1] // 2
        mine = lax.dynamic_slice_in_dim(left, member * size, size, 2)
        theirs = lax.dynamic_slice_in_dim(left, (1 - member) * size, size, 2)
        return over_rows(mine, right), over_rows(theirs, right).astype(BF)

    parts = [halves(xs, gps), halves(ctxs, gbs), halves(hids, gus)]
    blocks = acts.reshape(UNITS, 4, SEG, D)
    mine = lax.dynamic_slice_in_dim(blocks, member * 2, 2, 1)
    theirs = lax.dynamic_slice_in_dim(blocks, (1 - member) * 2, 2, 1)
    parts.append(
        (
            jnp.concatenate([over_rows(mine[:, i], gds) for i in range(2)], 0),
            jnp.concatenate([over_rows(theirs[:, i], gds) for i in range(2)], 0).astype(BF),
        )
    )
    sums = [keep_part + from_partner(sent, "pipe", 0).astype(F32) for keep_part, sent in parts]
    vec_mine = lax.dynamic_slice_in_dim(vecg, member * 8, 8, 0)
    vec_theirs = lax.dynamic_slice_in_dim(vecg, (1 - member) * 8, 8, 0)
    vec_sum = vec_mine + from_partner(vec_theirs, "pipe", 0)
    reduced = lax.psum((*sums, vec_sum, memory_part), "items")
    return (
        final_text,
        final_memory,
        text_grad,
        reduced[5],
        reduced[0],
        reduced[1],
        reduced[2],
        reduced[3],
        reduced[4][0],
        reduced[4][1:6].reshape(5 * D),
    )


def solution(mesh):
    placed = (
        P(("items", "pipe"), None, None, None),
        P(None, "pipe"),
        P("pipe", None),
        P("pipe", None),
        P("pipe", None),
        P("pipe", None),
        P("pipe"),
        P("pipe"),
        P("items"),
        P("items"),
        P(("items", "pipe"), None, None, None),
        P(("items", "pipe"), None, None),
    )
    return jax.shard_map(
        per_device,
        mesh=mesh,
        in_specs=placed,
        out_specs=(
            P(("items", "pipe"), None, None, None),
            P(("items", "pipe"), None, None),
            P(("items", "pipe"), None, None, None),
            P(None, "pipe"),
            P("pipe", None),
            P("pipe", None),
            P("pipe", None),
            P("pipe", None),
            P("pipe"),
            P("pipe"),
        ),
        check_vma=False,
    )
```

time: 1780 us -> 799 us (0.45)
  matrix products: 543 us -> 51.5 us
  local copies, waits for them, and re-layouts: 398 us -> 33.5 us
  Pallas kernels: 0 us -> 232 us
  other arithmetic: 240 us -> 21 us
  loops' own time: 75.4 us -> 0 us
  waiting for transfers between devices: 413 us -> 384 us
  starting transfers between devices: 21.1 us -> 1.25 us
    dot_general x110 -> x10, matrix products: 520 us -> 51.5 us  [over_rows(): lax.dot_general(left, right, (((0, 1), (0, 1)), ((), ())), preferred_elem...]
    pallas_call x0 -> x1, Pallas kernels: none -> 232 us  [relay(): pl.pallas_call(relay_kernel, out_shape=results, in_specs=in_specs, out_sp...]
    dynamic_update_slice x20 -> x0, local copies, waits for them, and re-layouts: 222 us -> none  [the longest x10 114 us: backward_turn(): lax.dynamic_update_slice(text_grads, update[None, None], (item, segment,...]
    another operation x2 -> x0, loops' own time: 75.4 us -> none  [the longest x1 45.6 us: per_device(): lax.fori_loop(0, slots, backward_turn, start)]
    convert_element_type x31 -> x4, other arithmetic: 64.3 us -> 2.97 us  [the longest x1 1.37 us: per_device(): (pair_counts > 1).astype(F32)[:, None, None]]
    while x702 -> x0, local copies, waits for them, and re-layouts: 59.1 us -> none
    dynamic_slice x41 -> x3, local copies, waits for them, and re-layouts: 50.9 us -> 4.08 us  [the longest x1 1.37 us: per_device(): pair_counts = jnp.stack([counts[member], counts[member + 2]])]
    reduce_sum x45 -> x1, other arithmetic: 44.3 us -> 0.02 us  [per_device(): jnp.sum(starts[:, :MEM] + starts[:, MEM:], axis=0)]
  transfers between devices with their start and end apart: 27 -> 8, of which waited for: 4 -> 2; matrix products, arithmetic and copies ran while one was open for 32% -> 9% of each run, Pallas kernels for 0% -> 0%
where the time goes in v1:
time: 799 us; the launch traced here: 788 us
  waiting for transfers between devices  384 us (48%)
  Pallas kernels  232 us (29%)
  matrix products  51.5 us (6%)
  blocking collectives  47.2 us (6%)
  local copies, waits for them, and re-layouts  33.5 us (4%)
  other arithmetic  21 us (3%)
  between operations  17.5 us (2%)
    psum x1, waiting for transfers between devices, per_device(): reduced = lax.psum((*sums, vec_sum, memory_part), 'items')  383 us
    pallas_call x1, Pallas kernels, relay(): pl.pallas_call(relay_kernel, out_shape=results, in_specs=in_specs, out_sp...  232 us
    dot_general x10, matrix products, over_rows(): lax.dot_general(left, right, (((0, 1), (0, 1)), ((), ())), preferred_elem...  51.5 us
    psum x1, blocking collectives, per_device(): reduced = lax.psum((*sums, vec_sum, memory_part), 'items')  40.8 us
    unnamed x49, local copies, waits for them, and re-layouts  21.1 us
  transfers between devices with their start and end apart: 8, of which 2 were waited for; matrix products, arithmetic and copies ran while one was open for 9% of the time, Pallas kernels for 0%

profile of v1, /device:TPU:0, one launch (start us, length us, event | category | flops | bytes accessed | tf_op | source)
XLA Modules:
  0.0 788.1 jit_solution(7260204146995540902)
XLA Ops:
  13.5 3.3 compare_select_fusion
  19.7 6.4 all-gather
  34.2 231.8 %shard_map.195 = (bf16[4,384,768]{2,1,0:T(8,128)(2,1)}, bf16[4,384,768]{2,1,0:T(8,128)(2,1)}, bf16[4,384,768]{2,1,0:T(8,128)(2,1)}, bf16[4,1536,768]{2,1,0:T(8,1...) custom-call(bf16[2,384,768]{2,1,0:T(8,128)(2,1)} %pad.18.x_own, ...), custom_call_target="tpu_custom_call" | custom-call | flops 80000000000 | bytes 83886080 | tf_op jit(solution)/shard_map/pallas_call | solution.py:634
  268.0 3.3 fusion.7
  271.4 7.4 fusion
  279.3 5.2 bitcast_convert_fusion
  284.5 3.7 bitcast_convert_fusion.2
  288.2 3.7 bitcast_convert_fusion.1
  291.9 1.6 pad_maximum_fusion
  294.0 5.1 fusion.5
  299.1 3.9 fusion.6
  303.0 3.6 convert_add_fusion.1
  306.6 8.4 %convert_add_fusion = f32[384,2304]{1,0:T(8,128)} fusion(bf16[384,2304]{1,0:T(8,128)(2,1)} %collective-permute-done.1, bf16[4,384,2304]{2,1,0:T(8,128)(2,1)} %get-tuple-element.24, bf16[4,384,768]{2,1,0:T(8,128)(2,1)S(1)} %copy-done.11, s32[]{:T(128)S(6)} %select_n.136), kind=kOutput, calls=%fused_computation.6 | convolution fusion | flops 2719678464 | bytes 13565956 | tf_op jit(solution)/shard_map/dot_general | solution.py:652
  315.1 7.2 bitcast_add_fusion
  322.2 4.4 maximum_add_fusion
  326.7 2.2 fusion.36
  330.4 1.4 collective-permute-done.5
  334.2 40.8 %all-reduce.4 = (f32[10,192]{1,0:T(8,128)}, f32[8,768]{1,0:T(8,128)}) all-reduce(f32[10,192]{1,0:T(8,128)S(1)} %copy.57, f32[8,768]{1,0:T(8,128)} %dynamic-slice_add_fusion), channel_id=1, replica_groups=mesh['items'=8,'pipe'=4] {'items'}, use_global_device_ids=true, to_apply=%region_2.3 | all-reduce | flops 8064 | bytes 64512 | tf_op jit(solution)/shard_map/psum | solution.py:735
  379.2 3.1 copy.49
  383.4 3.1 copy.47
  386.5 382.9 %all-reduce.8.cloned.1.call-done = (f32[384,2304]{1,0:T(8,128)}, f32[384,768]{1,0:T(8,128)}, f32[384,3072]{1,0:T(8,128)}, f32[1536,768]{1,0:T(8,128)}) async-done(((f32[384,2304]{1,0:T(8,128)}, f32[384,768]{1,0:T(8,128)}, f32[384,3072]{1,0:T(8,128)}, f32[1536,768]{1,0:T(8,128)}), (f32[384,2304]{1,0:T(8,128)}, f32[384,768]{1,0:T(8,128)}, f32[384,3072]{1,0:T(8,128)}, ...) | async-done | bytes 14155792 | tf_op jit(solution)/shard_map/psum | solution.py:735
  769.4 4.2 copy.71
  774.6 2.4 copy.73
  778.1 2.2 copy.74
  (96 shorter events, 29.3 us)
Async XLA Ops:
  8.0 21.0 %copy-start.7 = (bf16[1,2,364,768]{3,1,2,0:T(2,128)(2,1)S(1)}, bf16[1,2,364,768]{3,1,2,0:T(2,128)(2,1)}, u32[]{:S(2)}) copy-start(bf16[1,2,364,768]{3,1,2,0:T(2,128)(2,1)} %param.22) | copy-start | bytes 3354628
  8.0 325.2 %reduce-scatter.4.cloned.1.call-start = ((), (), s32[]{:S(2)}) async-start(), calls=%async_computation.1 | async-start | bytes 491520
  267.9 501.5 %all-reduce.8.cloned.1.call-start = ((), (), s32[]{:S(2)}) async-start(), calls=%async_computation.2 | async-start | bytes 28311552 | tf_op jit(solution)/shard_map/psum | solution.py:735
  268.0 3.4 copy-start.10
  268.0 11.3 %copy-start.8 = (bf16[4,384,768]{2,1,0:T(8,128)(2,1)S(1)}, bf16[4,384,768]{2,1,0:T(8,128)(2,1)}, u32[]{:S(2)}) copy-start(bf16[4,384,768]{2,1,0:T(8,128)(2,1)} %get-tuple-element.27) | copy-start | bytes 7077892
  271.3 31.7 %collective-permute-start.2 = (bf16[384,768]{1,0:T(8,128)(2,1)S(1)}, bf16[384,768]{1,0:T(8,128)(2,1)S(1)}, u32[]{:S(2)}, u32[]{:S(2)}) collective-permute-start(bf16[384,768]{1,0:T(8,128)(2,1)S(1)} %fusion.7), channel_id=1, source_target_pairs={{0,1},{1,0},{2,3},{3,2},{4,5},{5,4},{6,7},{7,6},{8,9},{9,8},{10,11... | collective-permute-start | bytes 1769480 | tf_op jit(solution)/shard_map/ppermute | solution.py:648
  271.4 7.9 %copy-start.2 = (bf16[4,384,3072]{2,1,0:T(8,128)(2,1)S(1)}, bf16[4,384,3072]{2,1,0:T(8,128)(2,1)}, u32[]{:S(2)}) copy-start(bf16[4,384,3072]{2,1,0:T(8,128)(2,1)} %get-tuple-element.28) | copy-start | bytes 28311556
  278.8 27.8 %collective-permute-start.1 = (bf16[384,2304]{1,0:T(8,128)(2,1)}, bf16[384,2304]{1,0:T(8,128)(2,1)}, u32[]{:S(2)}, u32[]{:S(2)}) collective-permute-start(bf16[384,2304]{1,0:T(8,128)(2,1)} %fusion), channel_id=1, source_target_pairs={{0,1},{1,0},{2,3},{3,2},{4,5},{5,4},{6,7},{7,6},{8,9},{9,8},{10,11... | collective-permute-start | bytes 5308424 | tf_op jit(solution)/shard_map/ppermute | solution.py:648
  279.3 5.2 copy-start.1
  284.4 30.6 %collective-permute-start.3 = (bf16[384,3072]{1,0:T(8,128)(2,1)}, bf16[384,3072]{1,0:T(8,128)(2,1)}, u32[]{:S(2)}, u32[]{:S(2)}) collective-permute-start(bf16[384,3072]{1,0:T(8,128)(2,1)} %bitcast_convert_fusion), channel_id=1, source_target_pairs={{0,1},{1,0},{2,3},{3,2},{4,5},{5,4},{6,7},{7,6},{8,9},{9,8},{10,11... | collective-permute-start | bytes 7077896 | tf_op jit(solution)/shard_map/ppermute | solution.py:648
  293.5 28.7 %collective-permute-start.4 = (bf16[1536,768]{1,0:T(8,128)(2,1)}, bf16[1536,768]{1,0:T(8,128)(2,1)}, u32[]{:S(2)}, u32[]{:S(2)}) collective-permute-start(bf16[1536,768]{1,0:T(8,128)(2,1)} %pad_maximum_fusion), channel_id=1, source_target_pairs={{0,1},{1,0},{2,3},{3,2},{4,5},{5,4},{6,7},{7,6},{8,9},{9,8},{10,11... | collective-permute-start | bytes 7077896 | tf_op jit(solution)/shard_map/ppermute | solution.py:648
  299.1 3.9 copy-start
  299.1 7.5 copy-start.11
  299.1 15.9 %slice-start = ((s8[9437184]{0:T(1024)(128)(4,1)}), s8[4194304]{0:T(1024)(128)(4,1)S(1)}, s32[]{:S(2)}) async-start(s8[9437184]{0:T(1024)(128)(4,1)} %bitcast.91), calls=%async_computation.3 | async-start | bytes 8388608
  303.0 12.0 %slice-start.1 = ((s8[9437184]{0:T(1024)(128)(4,1)}), s8[4194304]{0:T(1024)(128)(4,1)S(1)}, s32[]{:S(2)}) async-start(s8[9437184]{0:T(1024)(128)(4,1)} %bitcast.91), calls=%async_computation.4 | async-start | bytes 8388608
  306.6 8.4 %slice-start.2 = ((s8[9437184]{0:T(1024)(128)(4,1)}), s8[1048576]{0:T(1024)(128)(4,1)S(1)}, s32[]{:S(2)}) async-start(s8[9437184]{0:T(1024)(128)(4,1)} %bitcast.91), calls=%async_computation.5 | async-start | bytes 2097152
  306.6 8.4 %copy-start.9 = (bf16[4,384,768]{2,1,0:T(8,128)(2,1)S(1)}, bf16[4,384,768]{2,1,0:T(8,128)(2,1)}, u32[]{:S(2)}) copy-start(bf16[4,384,768]{2,1,0:T(8,128)(2,1)} %get-tuple-element.27) | copy-start | bytes 7077892
  315.0 7.2 copy-start.3
  328.9 50.2 %collective-permute-start = (bf16[2,384,768]{2,1,0:T(8,128)(2,1)S(1)}, bf16[2,384,768]{2,1,0:T(8,128)(2,1)S(1)}, u32[]{:S(2)}, u32[]{:S(2)}) collective-permute-start(bf16[2,384,768]{2,1,0:T(8,128)(2,1)S(1)} %get-tuple-element.59), channel_id=1, source_target_pairs={{0,2},{1,3},{2,0},{3,1},{4,6},{5,7},{6,4},{7,5},{8,10},{9,11},{10,... | collective-permute-start | bytes 3538952 | tf_op jit(solution)/shard_map/ppermute | solution.py:648
  330.3 1.5 collective-permute-start.5
  769.4 4.2 copy-start.6
  769.4 5.2 copy-start.4
  773.6 4.2 slice-start.3
  774.6 3.4 slice-start.4
  (3 other events, 6.3 us)
Sparse Core Ops, SparseCore 0:
  268.0 21.1 reduce-scatter.3
Sparse Core Ops, SparseCore 1:
  326.8 442.6 all-reduce.7

commit v2 on v1

--- a/solution.py
+++ b/solution.py
@@ -107,6 +107,7 @@
     gps,
     backs,
     vecg,
+    memg,
     wq,
     wo,
     wi,
@@ -229,6 +230,7 @@
     for b in range(2):
         stv[b, :, LANE:] = ones
     vecg[...] = jnp.zeros_like(vecg)
+    memg[...] = jnp.zeros_like(memg)
     low = lax.broadcasted_iota(jnp.int32, (SEG, LANE), 1) < 64
 
     def v(row):
@@ -243,9 +245,9 @@
     def grad_copy(u, buf):
         return remote(outb.at[buf], gsl.at[u], grad_send.at[buf], grad_recv.at[u], other)
 
-    def tail_copy(item, buf):
+    def tail_copy(slot, buf):
         src = outb.at[buf, pl.ds(SEG - TAIL, TAIL)]
-        return remote(src, trx.at[item], tail_send.at[item], tail_recv.at[item], other)
+        return remote(src, trx.at[slot], tail_send.at[slot], tail_recv.at[slot], other)
 
     def wait_weights(index):
         locals_[index].wait()
@@ -446,8 +448,8 @@
 
         @pl.when(jnp.logical_not(first) & (u < 2))
         def _():
-            tail_copy(item, buf).wait_recv()
-            arrived = nn(tail_matrix(False), trx[item])
+            tail_copy(u + 2, buf).wait_recv()
+            arrived = nn(tail_matrix(False), trx[u + 2])
             sd[0, SEG - TAIL :, :] = (
                 sd[0, SEG - TAIL :, :] + arrived * flags[item] + mcs[item, 1]
             )
@@ -546,7 +548,7 @@
 
         @pl.when((turn >= 2) & first)
         def _():
-            tail_copy(item, buf).wait_send()
+            tail_copy(u + 2, buf).wait_send()
 
         @pl.when((turn >= 2) & jnp.logical_not(first))
         def _():
@@ -559,9 +561,13 @@
         def _():
             grad_copy(u, buf).start()
 
-        @pl.when(first & (u >= 2))
-        def _():
-            tail_copy(item, buf).start()
+        @pl.when(first)
+        def _():
+            tail_copy(u, buf).start()
+
+        @pl.when(first & (u < 2))
+        def _():
+            memg[...] += nn(tail_matrix(False), outb[buf, SEG - TAIL :, :])
 
         out_copies(u, buf, backs).start()
         return carry
@@ -577,10 +583,17 @@
     for buf in range(2):
         out_copies(buf, buf, backs).wait()
 
+    @pl.when(first)
+    def _():
+        for buf in range(2):
+            tail_copy(buf, buf).wait_send()
+
     @pl.when(jnp.logical_not(first))
     def _():
         for buf in range(2):
             grad_copy(buf, buf).wait_send()
+            tail_copy(buf, buf).wait_recv()
+            memg[...] += nn(tail_matrix(False), trx[buf])
 
 
 def relay(operands):
@@ -600,6 +613,7 @@
         shape((UNITS, SEG, 3 * D), BF),
         shape(rows, BF),
         shape((16, D), F32),
+        shape((TAIL, D), F32),
     )
     scratch = [
         pltpu.VMEM((D, 3 * D), BF),
@@ -610,7 +624,7 @@
         pltpu.VMEM(rows, BF),
         pltpu.VMEM(rows, BF),
         pltpu.VMEM((2, 2, TAIL, D), F32),
-        pltpu.VMEM((2, TAIL, D), BF),
+        pltpu.VMEM((UNITS, TAIL, D), BF),
         pltpu.VMEM((UNITS, SEG, 3 * D), BF),
         pltpu.VMEM((UNITS, SEG, LANE), F32),
         pltpu.VMEM(rows, F32),
@@ -628,14 +642,14 @@
         pltpu.VMEM((2, SEG, D), BF),
         pltpu.VMEM((SEG, LANE), F32),
     ]
-    counts = [5, 5, 5, 3, 3, 3, 2, 4, 2, 2, 2, 4, 4, 4, 4, 4, 0, 0, 2, 2]
+    counts = [5, 5, 5, 3, 3, 3, 2, 4, 4, 4, 2, 4, 4, 4, 4, 4, 0, 0, 2, 2]
     scratch += [pltpu.SemaphoreType.DMA((n,)) if n else pltpu.SemaphoreType.DMA for n in counts]
     in_specs = [hbm, hbm, vmem, hbm, vmem, vmem, hbm, hbm, hbm, hbm, hbm]
     return pl.pallas_call(
         relay_kernel,
         out_shape=results,
         in_specs=in_specs,
-        out_specs=tuple([hbm] * 10 + [vmem]),
+        out_specs=tuple([hbm] * 10 + [vmem, vmem]),
         scratch_shapes=scratch,
         compiler_params=pltpu.CompilerParams(
             collective_id=0, has_side_effects=True, vmem_limit_bytes=63 * 2**20
@@ -644,6 +658,309 @@
     )(*operands)
 
 
+BLOCKS_G = 12
+CHUNK = SEG // 8
+STAGES = 15
+SMALL = 8 + TAIL
+
+
+def reduce_kernel(
+    xs,
+    ctxs,
+    hids,
+    acts,
+    gps,
+    gbs,
+    gus,
+    gds,
+    vecg,
+    mem_part,
+    f_qkv,
+    f_o,
+    f_in,
+    f_out,
+    small,
+    xt,
+    xm,
+    gg,
+    own,
+    sent,
+    tw,
+    ring0,
+    ring,
+    fin,
+    sm_tw,
+    sm_rx,
+    sm_tx,
+    load_sem,
+    tw_send,
+    tw_recv,
+    ring_send,
+    ring_recv,
+    fin_sem,
+    sm_send,
+    sm_recv,
+):
+    item = lax.axis_index("items")
+    place = lax.axis_index("pipe")
+    member = lax.rem(place, 2)
+    twin = {"pipe": place + 1 - 2 * member}
+    x_at, z_at = lax.rem(item, 2), item // 2
+    at = x_at * (7 - z_at) + (1 - x_at) * z_at
+    turn = 1 - 2 * member
+    logical = (1 - member) * at + member * (7 - at)
+
+    def item_of(position):
+        p = lax.rem(position + 8, 8)
+        up = p // 4
+        return up * (2 * (7 - p) + 1) + (1 - up) * 2 * p
+
+    ahead = {"items": item_of(at + turn)}
+    behind = {"items": item_of(at - turn)}
+    rounds = [
+        {"items": item + 1 - 2 * x_at},
+        {"items": item + 2 - 4 * lax.rem(z_at, 2)},
+        {"items": item + 4 - 8 * (z_at // 2)},
+    ]
+
+    barrier = pltpu.get_barrier_semaphore()
+    for to in [twin, ahead, behind, *rounds]:
+        pl.semaphore_signal(barrier, inc=1, device_id=to, device_id_type=MESH)
+    pl.semaphore_wait(barrier, 6)
+
+    def remote(src, dst, send, recv, to):
+        return pltpu.make_async_remote_copy(
+            src_ref=src, dst_ref=dst, send_sem=send, recv_sem=recv, device_id=to, device_id_type=MESH
+        )
+
+    def loads(left, right, theirs_rows, mine_rows, cols, slot):
+        rows_t, col_t = theirs_rows
+        rows_m, col_m = mine_rows
+        return [
+            pltpu.make_async_copy(left.at[:, rows_t, col_t], xt.at[slot], load_sem.at[slot, 0]),
+            pltpu.make_async_copy(left.at[:, rows_m, col_m], xm.at[slot], load_sem.at[slot, 1]),
+            pltpu.make_async_copy(right.at[:, :, cols], gg.at[slot], load_sem.at[slot, 2]),
+        ]
+
+    def aligned(start, size):
+        return pl.ds(pl.multiple_of(start, SEG), size)
+
+    def start_loads(b, slot):
+        def go(left, right, pick, col):
+            for copy in loads(left, right, pick(1 - member), pick(member), aligned(col * D, D), slot):
+                copy.start()
+
+        def flat(who):
+            return aligned(0, SEG), aligned(who * SEG, SEG)
+
+        @pl.when(b < 4)
+        def _():
+            def pick(who):
+                return aligned((2 * who + b // 2) * SEG, SEG), aligned(lax.rem(b, 2) * SEG, SEG)
+
+            go(acts, gds, pick, 0)
+
+        @pl.when((b >= 4) & (b < 8))
+        def _():
+            go(hids, gus, flat, b - 4)
+
+        @pl.when(b == 8)
+        def _():
+            go(ctxs, gbs, flat, 0)
+
+        @pl.when(b >= 9)
+        def _():
+            go(xs, gps, flat, b - 9)
+
+    def wait_loads(slot):
+        zero = aligned(0, SEG)
+        for copy in loads(xs, gds, (zero, zero), (zero, zero), aligned(0, D), slot):
+            copy.wait()
+
+    def twin_copy(b, slot):
+        return remote(sent.at[slot], tw.at[b], tw_send.at[slot], tw_recv.at[b], twin)
+
+    def rows_of(c):
+        return pl.ds(pl.multiple_of(c * CHUNK, 16), CHUNK)
+
+    def ring_copy(b, s, src, dst):
+        return remote(src, dst, ring_send.at[b, s], ring_recv.at[b, s], ahead)
+
+    def ring_wait(b, s):
+        ring_copy(b, s, ring0.at[b], ring0.at[b]).wait_recv()
+
+    def out_copy(b, go):
+        @pl.when(b < 4)
+        def _():
+            go(f_out.at[aligned(b * SEG, SEG)])
+
+        @pl.when((b >= 4) & (b < 8))
+        def _():
+            go(f_in.at[:, aligned((b - 4) * D, D)])
+
+        @pl.when(b == 8)
+        def _():
+            go(f_o.at[...])
+
+        @pl.when(b >= 9)
+        def _():
+            go(f_qkv.at[:, aligned((b - 9) * D, D)])
+
+    def stage(b, s):
+        c = lax.rem(logical - s + 16, 8)
+        rows = rows_of(c)
+
+        def part():
+            return own[b, rows, :] + tw[b, rows, :].astype(F32)
+
+        @pl.when(s == 0)
+        def _():
+            twin_copy(b, 0).wait_recv()
+            ring0[b] = part().astype(BF)
+            ring_copy(b, 0, ring0.at[b], ring.at[b, 0]).start()
+
+        @pl.when(s > 0)
+        def _():
+            ring_wait(b, s - 1)
+
+        @pl.when((s > 0) & (s < 7))
+        def _():
+            total = ring[b, s - 1].astype(F32) + part()
+            ring[b, s - 1] = total.astype(BF)
+            ring_copy(b, s, ring.at[b, s - 1], ring.at[b, s]).start()
+
+        @pl.when(s == 7)
+        def _():
+            fin[b, rows, :] = (ring[b, 6].astype(F32) + part()).astype(BF)
+
+        @pl.when((s >= 7) & (s < STAGES - 1))
+        def _():
+            ring_copy(b, s, fin.at[b, rows], fin.at[b, rows]).start()
+
+        @pl.when(s == STAGES - 1)
+        def _():
+            out_copy(b, lambda dst: pltpu.make_async_copy(fin.at[b], dst, fin_sem.at[b]).start())
+
+    def small_twin():
+        return remote(sm_tx.at[0], sm_tw, sm_send.at[0], sm_recv.at[0], twin)
+
+    def small_round(k):
+        return remote(small, sm_rx.at[k], sm_send.at[k + 1], sm_recv.at[k + 1], rounds[k])
+
+    start_loads(0, 0)
+    eight = pl.ds(pl.multiple_of((1 - member) * 8, 8), 8)
+    mine8 = pl.ds(pl.multiple_of(member * 8, 8), 8)
+    sm_tx[0, :8, :] = vecg[eight, :]
+    sm_tx[0, 8:, :] = mem_part[...]
+    small[:8, :] = vecg[mine8, :]
+    small[8:, :] = mem_part[...]
+    small_twin().start()
+
+    def step(i, carry):
+        slot = lax.rem(i, 2)
+
+        @pl.when(i < BLOCKS_G)
+        def _():
+            wait_loads(slot)
+
+            @pl.when(i + 1 < BLOCKS_G)
+            def _():
+                start_loads(i + 1, 1 - slot)
+
+            @pl.when(i >= 2)
+            def _():
+                twin_copy(i - 2, slot).wait_send()
+
+            right = gg[slot].reshape(UNITS * SEG, D)
+            sent[slot] = tn(xt[slot].reshape(UNITS * SEG, SEG), right).astype(BF)
+            twin_copy(i, slot).start()
+            own[i] = tn(xm[slot].reshape(UNITS * SEG, SEG), right)
+
+        for k in range(4):
+
+            @pl.when(i == 2 * k + 2)
+            def _():
+                if k == 0:
+                    small_twin().wait()
+                    small[...] = small[...] + sm_tw[...]
+                else:
+                    small_round(k - 1).wait()
+                    small[...] = small[...] + sm_rx[k - 1]
+                if k < 3:
+                    small_round(k).start()
+
+        first_b = jnp.maximum(i - STAGES, 0)
+        last_b = jnp.minimum(i, BLOCKS_G)
+
+        def serve(b, inner):
+            stage(b, i - 1 - b)
+            return inner
+
+        lax.fori_loop(first_b, last_b, serve, 0)
+        return carry
+
+    lax.fori_loop(0, BLOCKS_G + STAGES, step, 0)
+
+    twin_copy(0, 0).wait_send()
+    twin_copy(1, 1).wait_send()
+
+    def drain(b, carry):
+        def one(s, inner):
+            ring_copy(b, s, ring0.at[b], ring0.at[b]).wait_send()
+            return inner
+
+        lax.fori_loop(0, STAGES - 1, one, 0)
+        out_copy(b, lambda dst: pltpu.make_async_copy(fin.at[b], dst, fin_sem.at[b]).wait())
+        return carry
+
+    lax.fori_loop(0, BLOCKS_G, drain, 0)
+
+
+def reduce_grads(operands):
+    shape = jax.ShapeDtypeStruct
+    hbm = pl.BlockSpec(memory_space=pl.ANY)
+    vmem = pl.BlockSpec(memory_space=pltpu.VMEM)
+    dma = pltpu.SemaphoreType.DMA
+    return pl.pallas_call(
+        reduce_kernel,
+        out_shape=(
+            shape((SEG, 3 * D), BF),
+            shape((SEG, D), BF),
+            shape((SEG, FF), BF),
+            shape((FF // 2, D), BF),
+            shape((SMALL, D), F32),
+        ),
+        in_specs=[hbm] * 8 + [vmem, vmem],
+        out_specs=(hbm, hbm, hbm, hbm, vmem),
+        scratch_shapes=[
+            pltpu.VMEM((2, UNITS, SEG, SEG), BF),
+            pltpu.VMEM((2, UNITS, SEG, SEG), BF),
+            pltpu.VMEM((2, UNITS, SEG, D), BF),
+            pltpu.VMEM((BLOCKS_G, SEG, D), F32),
+            pltpu.VMEM((2, SEG, D), BF),
+            pltpu.VMEM((BLOCKS_G, SEG, D), BF),
+            pltpu.VMEM((BLOCKS_G, CHUNK, D), BF),
+            pltpu.VMEM((BLOCKS_G, 7, CHUNK, D), BF),
+            pltpu.VMEM((BLOCKS_G, SEG, D), BF),
+            pltpu.VMEM((SMALL, D), F32),
+            pltpu.VMEM((3, SMALL, D), F32),
+            pltpu.VMEM((1, SMALL, D), F32),
+            dma((2, 3)),
+            dma((2,)),
+            dma((BLOCKS_G,)),
+            dma((BLOCKS_G, STAGES - 1)),
+            dma((BLOCKS_G, STAGES - 1)),
+            dma((BLOCKS_G,)),
+            dma((4,)),
+            dma((4,)),
+        ],
+        compiler_params=pltpu.CompilerParams(
+            collective_id=1, has_side_effects=True, vmem_limit_bytes=60 * 2**20
+        ),
+        cost_estimate=pl.CostEstimate(flops=22 * 10**9, bytes_accessed=64 * 2**20, transcendentals=0),
+    )(*operands)
+
+
 def from_partner(x, axis, bit):
     return lax.ppermute(x, axis, [(i, i ^ 1 << bit) for i in range(lax.axis_size(axis))])
 
@@ -652,6 +969,32 @@
     return lax.dot_general(
         left, right, (((0, 1), (0, 1)), ((), ())), preferred_element_type=F32
     )
+
+
+def sum_grads(member, xs, ctxs, hids, acts, gps, gbs, gus, gds, vecg, memg):
+    def halves(left, right):
+        size = left.shape[-1] // 2
+        mine = lax.dynamic_slice_in_dim(left, member * size, size, 2)
+        theirs = lax.dynamic_slice_in_dim(left, (1 - member) * size, size, 2)
+        return over_rows(mine, right), over_rows(theirs, right).astype(BF)
+
+    parts = [halves(xs, gps), halves(ctxs, gbs), halves(hids, gus)]
+    blocks = acts.reshape(UNITS, 4, SEG, D)
+    mine = lax.dynamic_slice_in_dim(blocks, member * 2, 2, 1)
+    theirs = lax.dynamic_slice_in_dim(blocks, (1 - member) * 2, 2, 1)
+    parts.append(
+        (
+            jnp.concatenate([over_rows(mine[:, i], gds) for i in range(2)], 0),
+            jnp.concatenate([over_rows(theirs[:, i], gds) for i in range(2)], 0).astype(BF),
+        )
+    )
+    sums = [kept + from_partner(sent, "pipe", 0).astype(F32) for kept, sent in parts]
+    vec_mine = lax.dynamic_slice_in_dim(vecg, member * 8, 8, 0)
+    vec_theirs = lax.dynamic_slice_in_dim(vecg, (1 - member) * 8, 8, 0)
+    mine_small = jnp.concatenate([vec_mine, memg], 0)
+    small = mine_small + from_partner(jnp.concatenate([vec_theirs, memg], 0), "pipe", 0)
+    *grads, small = lax.psum((*sums, small), "items")
+    return grads, small
 
 
 def per_device(
@@ -695,55 +1038,33 @@
         [gains[None], biases.reshape(5, D), jnp.zeros((2, D), gains.dtype)], 0
     ).astype(F32)
 
-    xs, ctxs, hids, acts, tops, gds, gus, gbs, gps, backs, vecg = relay(
+    xs, ctxs, hids, acts, tops, gds, gus, gbs, gps, backs, vecg, memg = relay(
         (x_own, c_own, mem0, mc_own, flags, kmask, w_qkv, w_o, w_in, w_out, vec_own)
     )
 
     outgoing = jnp.where(first, backs[1::2], tops[0::2])
     returned = from_partner(outgoing, "pipe", 1)
+    if lax.axis_size("items") == 8:
+        *grads, small = reduce_grads((xs, ctxs, hids, acts, gps, gbs, gus, gds, vecg, memg))
+        grads = [grad.astype(F32) for grad in grads]
+    else:
+        grads, small = sum_grads(member, xs, ctxs, hids, acts, gps, gbs, gus, gds, vecg, memg)
     own_top = jnp.where(first, returned, tops[1::2])
     own_back = jnp.where(first, backs[0::2], returned)
     final_text = jnp.where(shown[:, :, None], own_top[:, :TEXT].astype(F32), 0.0)[None]
     text_grad = own_back[:, :TEXT].astype(F32)[None]
     ends = own_top[:, SEG - MEM :].astype(F32)
     final_memory = jnp.where(two, ends[1], ends[0])[None]
-
-    starts = backs[:2, TEXT:].astype(F32)
-    memory_part = jnp.where(first, jnp.sum(starts[:, :MEM] + starts[:, MEM:], axis=0), 0.0)
-    memory_part = lax.psum_scatter(memory_part, "pipe", scatter_dimension=1, tiled=True)
-
-    def halves(left, right):
-        size = left.shape[-1] // 2
-        mine = lax.dynamic_slice_in_dim(left, member * size, size, 2)
-        theirs = lax.dynamic_slice_in_dim(left, (1 - member) * size, size, 2)
-        return over_rows(mine, right), over_rows(theirs, right).astype(BF)
-
-    parts = [halves(xs, gps), halves(ctxs, gbs), halves(hids, gus)]
-    blocks = acts.reshape(UNITS, 4, SEG, D)
-    mine = lax.dynamic_slice_in_dim(blocks, member * 2, 2, 1)
-    theirs = lax.dynamic_slice_in_dim(blocks, (1 - member) * 2, 2, 1)
-    parts.append(
-        (
-            jnp.concatenate([over_rows(mine[:, i], gds) for i in range(2)], 0),
-            jnp.concatenate([over_rows(theirs[:, i], gds) for i in range(2)], 0).astype(BF),
-        )
-    )
-    sums = [keep_part + from_partner(sent, "pipe", 0).astype(F32) for keep_part, sent in parts]
-    vec_mine = lax.dynamic_slice_in_dim(vecg, member * 8, 8, 0)
-    vec_theirs = lax.dynamic_slice_in_dim(vecg, (1 - member) * 8, 8, 0)
-    vec_sum = vec_mine + from_partner(vec_theirs, "pipe", 0)
-    reduced = lax.psum((*sums, vec_sum, memory_part), "items")
+    width = D // 4
+    memory_grad = lax.dynamic_slice(small, (SMALL - MEM, place * width), (MEM, width))
     return (
         final_text,
         final_memory,
         text_grad,
-        reduced[5],
-        reduced[0],
-        reduced[1],
-        reduced[2],
-        reduced[3],
-        reduced[4][0],
-        reduced[4][1:6].reshape(5 * D),
+        memory_grad,
+        *grads,
+        small[0],
+        small[1:6].reshape(5 * D),
     )
 
 

time: 799 us -> 449 us (0.56); the launches traced: 788 us -> 448 us
  waiting for transfers between devices: 384 us -> 0.01 us
  Pallas kernels: 232 us -> 393 us
  matrix products: 51.5 us -> 0 us
  blocking collectives: 47.2 us -> 6.42 us
  between operations: 17.5 us -> 2.06 us
  local copies, waits for them, and re-layouts: 33.5 us -> 20.3 us
    psum x1 -> x0, waiting for transfers between devices: 383 us -> none  [per_device(): reduced = lax.psum((*sums, vec_sum, memory_part), 'items')]
    pallas_call x0 -> x1, Pallas kernels: none -> 172 us  [reduce_grads(): pl.pallas_call(reduce_kernel, out_shape=(shape((SEG, 3 * D), BF), shape((...]
    dot_general x10 -> x0, matrix products: 51.5 us -> none  [over_rows(): lax.dot_general(left, right, (((0, 1), (0, 1)), ((), ())), preferred_elem...]
    psum x1 -> x0, blocking collectives: 40.8 us -> none  [per_device(): reduced = lax.psum((*sums, vec_sum, memory_part), 'items')]
    unnamed x49 -> x13, local copies, waits for them, and re-layouts: 21.1 us -> 9.09 us
    pallas_call x1, Pallas kernels: 232 us -> 221 us  [relay(): pl.pallas_call(relay_kernel, out_shape=results, in_specs=in_specs, out_sp...]
    convert_element_type x1 -> x4, other arithmetic: 0.91 us -> 9.61 us  [per_device(): grads = [grad.astype(F32) for grad in grads]]
  transfers between devices with their start and end apart: 8 -> 1, of which waited for: 2 -> 0; matrix products, arithmetic and copies ran while one was open for 9% -> 3% of each run, Pallas kernels for 0% -> 38%
where the time goes in v2:
time: 449 us; the launch traced here: 448 us
  Pallas kernels  393 us (88%)
  other arithmetic  23.6 us (5%)
  local copies, waits for them, and re-layouts  20.3 us (5%)
  blocking collectives  6.42 us (1%)
    pallas_call x1, Pallas kernels, relay(): pl.pallas_call(relay_kernel, out_shape=results, in_specs=in_specs, out_sp...  221 us
    pallas_call x1, Pallas kernels, reduce_grads(): pl.pallas_call(reduce_kernel, out_shape=(shape((SEG, 3 * D), BF), shape((...  172 us
    convert_element_type x4, other arithmetic, per_device(): grads = [grad.astype(F32) for grad in grads]  9.61 us
    unnamed x13, local copies, waits for them, and re-layouts  9.09 us
  transfers between devices with their start and end apart: 1, of which 0 were waited for; matrix products, arithmetic and copies ran while one was open for 3% of the time, Pallas kernels for 38%

profile of v2, /device:TPU:0, one launch (start us, length us, event | category | flops | bytes accessed | tf_op | source)
XLA Modules:
  0.0 448.2 jit_solution(17991581668520728602)
XLA Ops:
  0.7 1.4 fusion.8
  4.1 1.4 compare_convert_fusion
  5.5 2.7 compare_select_fusion
  8.2 1.4 pad_add_fusion.3
  11.0 6.4 %all-gather = bf16[4,192,10]{1,2,0:T(8,128)(2,1)S(1)} all-gather(bf16[1,192,10]{1,2,0:T(8,128)(2,1)} %bitcast.29), channel_id=1, replica_groups=mesh['items'=8,'pipe'=4] {'pipe'}, dimensions={0}, use_global_device_ids=true | all-gather | bytes 19200 | tf_op jit(solution)/shard_map/all_gather | solution.py:1026
  19.0 1.4 copy.36
  20.6 1.1 pad.19.c_own
  21.7 1.1 pad.18.x_own
  25.6 221.4 %shard_map.195 = (bf16[4,384,768]{2,1,0:T(8,128)(2,1)}, bf16[4,384,768]{2,1,0:T(8,128)(2,1)}, bf16[4,384,768]{2,1,0:T(8,128)(2,1)}, bf16[4,1536,768]{2,1,0:T(8,1...) custom-call(bf16[2,384,768]{2,1,0:T(8,128)(2,1)} %pad.18.x_own, ...), custom_call_target="tpu_custom_call" | custom-call | flops 80000000000 | bytes 83886080 | tf_op jit(solution)/shard_map/pallas_call | solution.py:648
  247.0 2.2 fusion.7
  249.2 2.7 collective-permute-start
  251.9 171.7 %shard_map.196 = (bf16[384,2304]{1,0:T(8,128)(2,1)}, bf16[384,768]{1,0:T(8,128)(2,1)}, bf16[384,3072]{1,0:T(8,128)(2,1)}, bf16[1536,768]{1,0:T(8,128)(2,1)}, f32[40,768]{1,0:T(8,128)}) custom-call(bf16[4,384,768]{2,1,0:T(8,128)(2,1)} %get-tuple-element.29.xs, bf16[4,384,768]{2,1,0:T(8,128)(2,1)} %get-tuple-element.30.ctxs, ...), custom_call_target="tpu_custom_call" | custom-call | flops 22000001024 | bytes 67108864 | tf_op jit(solution)/shard_map/pallas_call | solution.py:924
  423.6 1.3 slice.43
  425.0 1.3 reshape.143
  426.3 2.3 convert_element_type.46
  428.6 2.0 convert_element_type.45
  430.6 0.8 copy-done.1
  431.4 2.8 convert_element_type.47
  434.2 2.5 convert_element_type.48
  436.7 1.4 constant_dynamic-slice_fusion
  438.1 1.3 slice_reduce_fusion
  439.5 1.4 slice_select_fusion
  441.4 3.1 copy.33
  445.1 3.1 copy.31
  (30 shorter events, 7.9 us)
Async XLA Ops:
  0.6 19.8 %copy-start.3 = (bf16[1,2,364,768]{3,1,2,0:T(2,128)(2,1)S(1)}, bf16[1,2,364,768]{3,1,2,0:T(2,128)(2,1)}, u32[]{:S(2)}) copy-start(bf16[1,2,364,768]{3,1,2,0:T(2,128)(2,1)} %param.22) | copy-start | bytes 3354628
  249.2 190.3 %collective-permute-start = (bf16[2,384,768]{2,1,0:T(8,128)(2,1)S(1)}, bf16[2,384,768]{2,1,0:T(8,128)(2,1)S(1)}, u32[]{:S(2)}, u32[]{:S(2)}) collective-permute-start(bf16[2,384,768]{2,1,0:T(8,128)(2,1)S(1)} %get-tuple-element.65), channel_id=1, source_target_pairs={{0,2},{1,3},{2,0},{3,1},{4,6},{5,7},{6,4},{7,5},{8,10},{9,11},{10,... | collective-permute-start | bytes 3538952 | tf_op jit(solution)/shard_map/ppermute | solution.py:965
  426.3 2.3 copy-start.2
  428.6 2.8 copy-start.1
  431.4 2.8 copy-start

commit v3 on v2

--- a/solution.py
+++ b/solution.py
@@ -87,10 +87,10 @@
 def relay_kernel(
     x_own,
     c_own,
-    mem0,
-    mc_own,
-    flags,
-    kmask,
+    mem_own,
+    mcot_own,
+    counts,
+    lasts,
     w_qkv,
     w_o,
     w_in,
@@ -100,12 +100,13 @@
     ctxs,
     hids,
     acts,
-    tops,
+    own_top,
     gds,
     gus,
     gbs,
     gps,
-    backs,
+    own_back,
+    slopes,
     vecg,
     memg,
     wq,
@@ -116,12 +117,15 @@
     xin,
     gsl,
     mcs,
+    mem_rx,
+    mem0,
     trx,
     packed,
     st,
     n1s,
     n2s,
-    dgs,
+    dgf,
+    gub,
     ctx,
     sc,
     sd,
@@ -133,6 +137,7 @@
     outb,
     gdb,
     delta,
+    parts,
     w_local,
     w_send,
     w_recv,
@@ -152,18 +157,28 @@
     hid_sem,
     act_sem,
     gd_sem,
-    out_sem,
+    dg_sem,
+    mem_send,
+    mem_recv,
+    top_send,
+    top_recv,
+    back_send,
+    back_recv,
+    res_sem,
+    lag,
 ):
     place = lax.axis_index("pipe")
     first = place < 2
     member = lax.rem(place, 2)
     twin = {"pipe": place + 1 - 2 * member}
     other = {"pipe": lax.rem(place + 2, 4)}
+    across = {"pipe": 3 - place}
+    second = jnp.logical_not(first)
 
     barrier = pltpu.get_barrier_semaphore()
-    pl.semaphore_signal(barrier, inc=1, device_id=twin, device_id_type=MESH)
-    pl.semaphore_signal(barrier, inc=1, device_id=other, device_id_type=MESH)
-    pl.semaphore_wait(barrier, 2)
+    for to in (twin, other, across):
+        pl.semaphore_signal(barrier, inc=1, device_id=to, device_id_type=MESH)
+    pl.semaphore_wait(barrier, 3)
 
     def remote(src, dst, send, recv, to):
         return pltpu.make_async_remote_copy(
@@ -194,50 +209,99 @@
     c_away = [
         remote(c_own.at[k], gsl.at[2 * k], e_send.at[k], e_recv.at[k], other) for k in range(2)
     ]
-    m_home = pltpu.make_async_copy(mc_own, mcs.at[1], e_local.at[2])
-    m_away = remote(mc_own, mcs.at[0], e_send.at[2], e_recv.at[2], other)
+    m_home = pltpu.make_async_copy(mcot_own, mcs.at[1], e_local.at[2])
+    m_away = remote(mcot_own, mcs.at[0], e_send.at[2], e_recv.at[2], other)
+    mem_twin = remote(mem_own, mem_rx.at[place], mem_send.at[0], mem_recv.at[place], twin)
+    mem_other = remote(mem_own, mem_rx.at[place], mem_send.at[0], mem_recv.at[place], other)
+    mem_across = remote(mem_own, mem_rx.at[place], mem_send.at[1], mem_recv.at[place], across)
+
+    def start_weights(index):
+        locals_[index].start()
+        sends[index].start()
+
+    def wait_weights(index):
+        locals_[index].wait()
+        recvs[index].wait_recv()
+
+    start_weights(0)
+    start_weights(1)
 
     @pl.when(first)
     def _():
         for copy in x_home:
             copy.start()
-
-    for index in (0, 1):
-        locals_[index].start()
-        sends[index].start()
-    for index in (2, 3, 4):
-        locals_[index].start()
-        sends[index].start()
-
-    @pl.when(first)
+        mem_twin.start()
+
+    @pl.when(second)
     def _():
-        for copy in c_away:
-            copy.start()
-        m_away.start()
-
-    @pl.when(jnp.logical_not(first))
-    def _():
-        for copy in x_away:
-            copy.start()
+        mem_other.start()
+        mem_across.start()
+        x_away[0].start()
         for copy in c_home:
             copy.start()
         m_home.start()
 
     rhs[...] = jnp.zeros_like(rhs)
-    ones_row = lax.broadcasted_iota(jnp.int32, (2 * SEG, LANE), 0)
-    ones_col = lax.broadcasted_iota(jnp.int32, (2 * SEG, LANE), 1)
-    ones = jnp.where(ones_col == jnp.where(ones_row < SEG, 0, 1), 1.0, 0.0).astype(BF)
-    for b in range(2):
-        stv[b, :, LANE:] = ones
+    ones = jnp.ones((2 * LANE, LANE), BF)
     vecg[...] = jnp.zeros_like(vecg)
     memg[...] = jnp.zeros_like(memg)
     low = lax.broadcasted_iota(jnp.int32, (SEG, LANE), 1) < 64
 
+    @pl.when(first)
+    def _():
+        mem_twin.wait_send()
+        for index in range(4):
+
+            @pl.when(index != place)
+            def _():
+                remote(mem_own, mem_rx.at[index], mem_send.at[0], mem_recv.at[index], twin).wait_recv()
+
+            @pl.when(index == place)
+            def _():
+                mem_rx[index] = mem_own[...]
+
+        row = lax.broadcasted_iota(jnp.int32, (TAIL, 16), 0)
+        col = lax.broadcasted_iota(jnp.int32, (TAIL, 16), 1)
+        twice = ((col == row - 12) | (col == row - 22)) & (col < MEM)
+        spread = jnp.where(twice, 1.0, 0.0).astype(BF)
+        total = jnp.zeros((TAIL, D), F32)
+        for index in range(4):
+            source = lax.broadcasted_iota(jnp.int32, (2 * LANE, D), 0)
+            target = lax.broadcasted_iota(jnp.int32, (2 * LANE, D), 1)
+            move = (target == source + index * (D // 4)) & (source < D // 4)
+            rows = nn(spread, mem_rx[index]).astype(BF)
+            total = total + nn(rows, jnp.where(move, 1.0, 0.0).astype(BF))
+        mem0[...] = total.astype(BF)
+
+    def unit_scalars(u):
+        item = lax.rem(u, 2)
+        count = counts[member + 2 * item]
+        last = lasts[member + 2 * item]
+        length = jnp.where((u < 2) & (count > 1), TEXT, last)
+        return count, length
+
+    def key_mask(length):
+        key = lax.broadcasted_iota(jnp.int32, (1, SEG), 1)
+        return jnp.where((key >= TEXT) | (key < length), 0.0, MASKED)
+
     def v(row):
         return vec[row : row + 1, :]
 
-    def out_copies(u, buf, results):
-        return pltpu.make_async_copy(outb.at[buf], results.at[u], out_sem.at[buf])
+    def top_copy(u):
+        return remote(
+            outb.at[0], own_top.at[u // 2], top_send.at[0], top_recv.at[u // 2], other
+        )
+
+    def top_here(u):
+        return pltpu.make_async_copy(outb.at[1], own_top.at[u // 2], res_sem.at[0])
+
+    def back_copy(u):
+        return remote(
+            outb.at[1], own_back.at[u // 2], back_send.at[0], back_recv.at[u // 2], other
+        )
+
+    def back_here(u):
+        return pltpu.make_async_copy(outb.at[0], own_back.at[u // 2], res_sem.at[1])
 
     def mid_copy(u, buf):
         return remote(outb.at[buf], xin.at[u], mid_send.at[buf], mid_recv.at[u], other)
@@ -249,24 +313,38 @@
         src = outb.at[buf, pl.ds(SEG - TAIL, TAIL)]
         return remote(src, trx.at[slot], tail_send.at[slot], tail_recv.at[slot], other)
 
-    def wait_weights(index):
-        locals_[index].wait()
-        sends[index].wait_send()
-        recvs[index].wait_recv()
-
     def forward_turn(u, carry):
         item = lax.rem(u, 2)
         buf = lax.rem(u, 2)
 
+        @pl.when(u == 0)
+        def _():
+            wait_weights(0)
+            wait_weights(1)
+            for index in (2, 3, 4):
+                start_weights(index)
+
         @pl.when(first & (u == 0))
         def _():
             for copy in x_home:
                 copy.wait()
 
+        @pl.when(first & (member == 1) & (u == 0))
+        def _():
+            pl.semaphore_wait(lag, 1)
+
         @pl.when(first & (u == 1))
         def _():
-            for copy in x_away:
-                copy.wait_recv()
+            x_away[0].wait_recv()
+
+        @pl.when(first & (u == 3))
+        def _():
+            x_away[1].wait_recv()
+
+        @pl.when(second & (u == 0))
+        def _():
+            x_away[0].wait_send()
+            x_away[1].start()
 
         @pl.when(first & (u < 2))
         def _():
@@ -278,18 +356,14 @@
             spread = nn(tail_matrix(True), trx[item]).astype(BF)
             xin[u, SEG - TAIL :, :] = xin[u, SEG - TAIL :, :] + spread
 
-        @pl.when(jnp.logical_not(first))
+        @pl.when(second)
         def _():
             mid_copy(u, buf).wait_recv()
 
         pltpu.make_async_copy(xin.at[u], xs.at[u], x_sem.at[u]).start()
 
-        @pl.when(u == 0)
-        def _():
-            wait_weights(0)
-            wait_weights(1)
-
-        mask = kmask[u]
+        count, length = unit_scalars(u)
+        mask = key_mask(length)
         x = xin[u]
         packed[u, :, :D] = (nn(x, wq[:, :D]) + v(BQ)).astype(BF) * 0.125
         packed[u, :, D : 2 * D] = nn(x, wq[:, D : 2 * D]).astype(BF)
@@ -299,6 +373,7 @@
         def _():
             hid_copy(u).wait()
             act_copy(u).wait()
+            slope_out(u - 1).wait()
 
         def scores(p):
             b = p % 2
@@ -316,18 +391,20 @@
                     cols = slice(h * SEG, (h + 1) * SEG)
                     scaled = sc[b, rows, cols] * LOG2E + mask
                     top = jnp.max(scaled, axis=-1, keepdims=True)
-                    big[b * 2 * SEG + rows.start : b * 2 * SEG + rows.stop, cols] = jnp.exp2(
-                        scaled - top
+                    raised = jnp.exp2(scaled - top)
+                    total = jnp.sum(raised, axis=-1, keepdims=True)
+                    big[b * 2 * SEG + rows.start : b * 2 * SEG + rows.stop, cols] = (
+                        raised * (1.0 / total)
                     ).astype(BF)
-                    st[u, rows, 2 * p + h : 2 * p + h + 1] = top
-            mixed = nn(big[b * 2 * SEG : b * 2 * SEG + SEG, :], stv[b])
-            total = mixed[:, LANE : LANE + 2]
-            share = 1.0 / total
-            ctx[u, :, p * LANE : (p + 1) * LANE] = (
-                mixed[:, :LANE] * jnp.where(low, share[:, :1], share[:, 1:])
+                    st[u, rows, 2 * p + h : 2 * p + h + 1] = top + jnp.log2(total)
+            ctx[u, :, p * LANE : (p + 1) * LANE] = nn(
+                big[b * 2 * SEG : b * 2 * SEG + SEG, :], stv[b]
             ).astype(BF)
-            st[u, :, 2 * p : 2 * p + 2] = st[u, :, 2 * p : 2 * p + 2] + jnp.log2(total)
         pltpu.make_async_copy(ctx.at[u], ctxs.at[u], ctx_sem.at[u]).start()
+
+        @pl.when(first & (member == 0) & (u == 0))
+        def _():
+            pl.semaphore_signal(lag, inc=1, device_id=twin, device_id_type=MESH)
 
         @pl.when(u == 0)
         def _():
@@ -356,20 +433,28 @@
             for rows in BLOCKS:
                 act, slope = gelu_parts(sd[j % 2, rows, :] + v(BI + j))
                 big[j * SEG + rows.start : j * SEG + rows.stop, :] = act.astype(BF)
-                dgs[u, rows, j * D : (j + 1) * D] = slope.astype(BF)
+                dgf[rows, j * D : (j + 1) * D] = slope
             part = nn(big[j * SEG : (j + 1) * SEG, :], wd[j * D : (j + 1) * D, :])
             sc[0] = part if j == 0 else sc[0] + part
         act_copy(u).start()
 
-        @pl.when(u >= 2)
-        def _():
-            out_copies(u, buf, tops).wait()
+        @pl.when(u < UNITS - 1)
+        def _():
+            slope_out(u).start()
+
+        @pl.when(second & (u == 2))
+        def _():
+            top_copy(u).wait_send()
+
+        @pl.when(second & (u == 3))
+        def _():
+            top_here(u).wait()
 
         @pl.when((u >= 2) & first)
         def _():
             mid_copy(u, buf).wait_send()
 
-        @pl.when((u >= 2) & jnp.logical_not(first))
+        @pl.when((u >= 2) & second)
         def _():
             tail_copy(item, buf).wait_send()
 
@@ -384,11 +469,18 @@
         def _():
             mid_copy(u, buf).start()
 
-        @pl.when(jnp.logical_not(first) & (u < 2))
+        @pl.when(second & (u < 2))
         def _():
             tail_copy(item, buf).start()
 
-        out_copies(u, buf, tops).start()
+        @pl.when(second & (item == 0))
+        def _():
+            top_copy(u).start()
+
+        @pl.when(second & (item == 1))
+        def _():
+            top_here(u).start()
+
         return carry
 
     def hid_copy(u):
@@ -396,6 +488,12 @@
 
     def act_copy(u):
         return pltpu.make_async_copy(big, acts.at[u], act_sem)
+
+    def slope_out(u):
+        return pltpu.make_async_copy(dgf, slopes.at[u], dg_sem.at[0])
+
+    def slope_in(u):
+        return pltpu.make_async_copy(slopes.at[u], dgf, dg_sem.at[1])
 
     lax.fori_loop(0, UNITS, forward_turn, 0)
 
@@ -403,33 +501,39 @@
     act_copy(0).wait()
     for u in range(UNITS):
         pltpu.make_async_copy(ctx.at[u], ctxs.at[u], ctx_sem.at[u]).wait()
-    for buf in range(2):
-        out_copies(2 + buf, buf, tops).wait()
+    for index in range(5):
+        sends[index].wait_send()
 
     @pl.when(first)
     def _():
         for buf in range(2):
             mid_copy(2 + buf, buf).wait_send()
-        for copy in c_away:
-            copy.wait_send()
-        m_away.wait_send()
-
-    @pl.when(jnp.logical_not(first))
+        pl.semaphore_signal(lag, inc=1, device_id=twin, device_id_type=MESH)
+        pl.semaphore_wait(lag, 1)
+        c_away[1].start()
+        m_away.start()
+        c_away[1].wait_send()
+        c_away[0].start()
+
+    @pl.when(second)
     def _():
-        for copy in x_away:
-            copy.wait_send()
+        top_copy(2).wait_send()
+        top_here(3).wait()
+        x_away[1].wait_send()
+        mem_other.wait_send()
+        mem_across.wait_send()
         for copy in c_home:
             copy.wait()
-        for copy in c_away:
-            copy.wait_recv()
         m_home.wait()
-        m_away.wait_recv()
 
     def gd_copy(u):
         return pltpu.make_async_copy(gdb.at[0], gds.at[u], gd_sem.at[0])
 
     def gb_copy(u):
         return pltpu.make_async_copy(gdb.at[1], gbs.at[u], gd_sem.at[1])
+
+    def gu_copy(u):
+        return pltpu.make_async_copy(gub, gus.at[u], gu_sem)
 
     def backward_turn(turn, carry):
         u = UNITS - 1 - turn
@@ -440,31 +544,48 @@
         def _():
             grad_copy(u, buf).wait_recv()
 
-        sd[0] = gsl[u].astype(F32)
-
-        @pl.when(jnp.logical_not(first) & (u >= 2))
-        def _():
-            sd[0, SEG - TAIL :, :] = sd[0, SEG - TAIL :, :] + mcs[item, 0]
-
-        @pl.when(jnp.logical_not(first) & (u < 2))
+        @pl.when(second & (u == 2))
+        def _():
+            c_away[1].wait_recv()
+            m_away.wait_recv()
+
+        @pl.when(second & (u == 0))
+        def _():
+            c_away[0].wait_recv()
+
+        count, length = unit_scalars(u)
+        limit = jnp.where(first, SEG, jnp.where((u < 2) | (count > 1), length, 0))
+        row = lax.broadcasted_iota(jnp.int32, (SEG, D), 0)
+        sd[0] = jnp.where(row < limit, gsl[u].astype(F32), 0.0)
+        both_live = jnp.where(count > 1, 1.0, 0.0)
+
+        @pl.when(second & (u >= 2))
+        def _():
+            sd[0, SEG - TAIL :, :] = sd[0, SEG - TAIL :, :] + mcs[item].astype(F32) * both_live
+
+        @pl.when(second & (u < 2))
         def _():
             tail_copy(u + 2, buf).wait_recv()
             arrived = nn(tail_matrix(False), trx[u + 2])
             sd[0, SEG - TAIL :, :] = (
-                sd[0, SEG - TAIL :, :] + arrived * flags[item] + mcs[item, 1]
+                sd[0, SEG - TAIL :, :]
+                + arrived * both_live
+                + mcs[item].astype(F32) * (1.0 - both_live)
             )
 
         @pl.when(turn > 0)
         def _():
             gd_copy(u).wait()
             gb_copy(u).wait()
+            gu_copy(u).wait()
+            slope_in(u).wait()
 
         for rows in BLOCKS:
             grad = sd[0, rows, :]
             normed = n2s[u, rows, :]
-            second = norm_back(grad, normed, st[u, rows, 13:14], v(G2))
-            sc[0, rows, :] = second
-            down = second.astype(BF)
+            second_grad = norm_back(grad, normed, st[u, rows, 13:14], v(G2))
+            sc[0, rows, :] = second_grad
+            down = second_grad.astype(BF)
             gdb[0, rows, :] = down
             vecg[G2 : G2 + 1, :] += row_sum(grad * normed)
             vecg[N2 : N2 + 1, :] += row_sum(grad)
@@ -474,11 +595,16 @@
             sd[j % 2] = nt(gdb[0], wd[j * D : (j + 1) * D, :])
             for rows in BLOCKS:
                 cols = slice(j * D, (j + 1) * D)
-                lifted = (sd[j % 2, rows, :] * dgs[u, rows, cols].astype(F32)).astype(BF)
-                dgs[u, rows, cols] = lifted
+                lifted = (sd[j % 2, rows, :] * dgf[rows, cols]).astype(BF)
+                gub[rows, cols] = lifted
                 vecg[BI + j : BI + j + 1, :] += row_sum(lifted.astype(F32))
-        pltpu.make_async_copy(dgs.at[u], gus.at[u], gu_sem.at[u]).start()
-        sd[0] = nt(dgs[u], wi[...])
+        gu_copy(u).start()
+
+        @pl.when(u > 0)
+        def _():
+            slope_in(u - 1).start()
+
+        sd[0] = nt(gub[...], wi[...])
         for rows in BLOCKS:
             grad = sc[0, rows, :] + sd[0, rows, :]
             normed = n1s[u, rows, :]
@@ -490,15 +616,9 @@
             vecg[BO : BO + 1, :] += row_sum(branch.astype(F32))
             n1s[u, rows, :] = first_grad
         gb_copy(u).start()
-        head = lax.broadcasted_iota(jnp.int32, (D, LANE), 0) // 64
-        heads = (head == lax.broadcasted_iota(jnp.int32, (D, LANE), 1)).astype(F32).astype(BF)
         grad_ctx = nt(gdb[1], wo[...]).astype(BF)
-        product = grad_ctx.astype(F32) * ctx[u].astype(F32)
-        high = product.astype(BF)
-        rest = (product - high.astype(F32)).astype(BF)
-        delta[...] = nn(high, heads) + nn(rest, heads)
         ctx[u] = grad_ctx
-        mask = kmask[u]
+        mask = key_mask(length)
 
         def scores(p):
             b = p % 2
@@ -509,7 +629,7 @@
             rhs[b, :SEG, :LANE] = grad
             rhs[b, SEG:, LANE:] = query
             sc[b] = nt(query, stk[b])
-            sd[b] = nt(grad, stv[b, :, :LANE])
+            sd[b] = nt(grad, stv[b])
 
         scores(0)
         for p in range(PAIRS):
@@ -523,9 +643,22 @@
                     one = slice(2 * p + h, 2 * p + h + 1)
                     probs = jnp.exp2(sc[b, rows, cols] * LOG2E + mask - st[u, rows, one])
                     big[base + rows.start : base + rows.stop, cols] = probs.astype(BF)
-                    big[base + SEG + rows.start : base + SEG + rows.stop, cols] = (
-                        probs * (sd[b, rows, cols] - delta[rows, one])
-                    ).astype(BF)
+                    sc[b, rows, cols] = probs
+                    product = probs * sd[b, rows, cols]
+                    third = product[:, :LANE] + product[:, LANE : 2 * LANE] + product[:, 2 * LANE :]
+                    high = third.astype(BF)
+                    at = 2 * h * LANE
+                    parts[b, rows, at : at + LANE] = high
+                    parts[b, rows, at + LANE : at + 2 * LANE] = (third - high.astype(F32)).astype(BF)
+            for h in range(2):
+                delta[b, h] = nn(parts[b, :, 2 * h * LANE : 2 * (h + 1) * LANE], ones)
+            for rows in BLOCKS:
+                for h in range(2):
+                    for third in range(3):
+                        cols = slice(h * SEG + third * LANE, h * SEG + (third + 1) * LANE)
+                        big[base + SEG + rows.start : base + SEG + rows.stop, cols] = (
+                            sc[b, rows, cols] * (sd[b, rows, cols] - delta[b, h, rows, :])
+                        ).astype(BF)
             packed[u, :, p * LANE : (p + 1) * LANE] = (
                 nn(big[base + SEG : base + 2 * SEG, :], stk[b]) * 0.125
             ).astype(BF)
@@ -542,22 +675,26 @@
             vecg[BV : BV + 1, :] += row_sum(packed[u, rows, 2 * D :].astype(F32))
         sd[0] = nt(packed[u], wq[...])
 
-        @pl.when(turn >= 2)
-        def _():
-            out_copies(u, buf, backs).wait()
+        @pl.when((turn == 2) & first)
+        def _():
+            back_copy(u).wait_send()
+
+        @pl.when((turn == 3) & first)
+        def _():
+            back_here(u).wait()
 
         @pl.when((turn >= 2) & first)
         def _():
             tail_copy(u + 2, buf).wait_send()
 
-        @pl.when((turn >= 2) & jnp.logical_not(first))
+        @pl.when((turn >= 2) & second)
         def _():
             grad_copy(u, buf).wait_send()
 
         for rows in BLOCKS:
             outb[buf, rows, :] = (n1s[u, rows, :] + sd[0, rows, :]).astype(BF)
 
-        @pl.when(jnp.logical_not(first))
+        @pl.when(second)
         def _():
             grad_copy(u, buf).start()
 
@@ -569,31 +706,42 @@
         def _():
             memg[...] += nn(tail_matrix(False), outb[buf, SEG - TAIL :, :])
 
-        out_copies(u, buf, backs).start()
+        @pl.when(first & (item == 1))
+        def _():
+            back_copy(u).start()
+
+        @pl.when(first & (item == 0))
+        def _():
+            back_here(u).start()
+
         return carry
 
     lax.fori_loop(0, UNITS, backward_turn, 0)
 
     gd_copy(0).wait()
     gb_copy(0).wait()
+    gu_copy(0).wait()
     for u in range(UNITS):
         pltpu.make_async_copy(xin.at[u], xs.at[u], x_sem.at[u]).wait()
-        pltpu.make_async_copy(dgs.at[u], gus.at[u], gu_sem.at[u]).wait()
         pltpu.make_async_copy(packed.at[u], gps.at[u], gp_sem.at[u]).wait()
-    for buf in range(2):
-        out_copies(buf, buf, backs).wait()
 
     @pl.when(first)
     def _():
         for buf in range(2):
             tail_copy(buf, buf).wait_send()
-
-    @pl.when(jnp.logical_not(first))
+            top_copy(2 * buf).wait_recv()
+        back_copy(1).wait_send()
+        back_here(0).wait()
+        c_away[0].wait_send()
+        m_away.wait_send()
+
+    @pl.when(second)
     def _():
         for buf in range(2):
             grad_copy(buf, buf).wait_send()
             tail_copy(buf, buf).wait_recv()
             memg[...] += nn(tail_matrix(False), trx[buf])
+            back_copy(2 * buf + 1).wait_recv()
 
 
 def relay(operands):
@@ -606,12 +754,13 @@
         shape(rows, BF),
         shape(rows, BF),
         shape((UNITS, 4 * SEG, D), BF),
-        shape(rows, BF),
+        shape((2, SEG, D), BF),
         shape(rows, BF),
         shape((UNITS, SEG, FF), BF),
         shape(rows, BF),
         shape((UNITS, SEG, 3 * D), BF),
-        shape(rows, BF),
+        shape((2, SEG, D), BF),
+        shape((UNITS - 1, SEG, FF), F32),
         shape((16, D), F32),
         shape((TAIL, D), F32),
     )
@@ -623,33 +772,39 @@
         pltpu.VMEM((16, D), F32),
         pltpu.VMEM(rows, BF),
         pltpu.VMEM(rows, BF),
-        pltpu.VMEM((2, 2, TAIL, D), F32),
+        pltpu.VMEM((2, TAIL, D), BF),
+        pltpu.VMEM((4, 16, 2 * LANE), BF),
+        pltpu.VMEM((TAIL, D), BF),
         pltpu.VMEM((UNITS, TAIL, D), BF),
         pltpu.VMEM((UNITS, SEG, 3 * D), BF),
         pltpu.VMEM((UNITS, SEG, LANE), F32),
         pltpu.VMEM(rows, F32),
         pltpu.VMEM(rows, F32),
-        pltpu.VMEM((UNITS, SEG, FF), BF),
+        pltpu.VMEM((SEG, FF), F32),
+        pltpu.VMEM((SEG, FF), BF),
         pltpu.VMEM(rows, BF),
         pltpu.VMEM((2, SEG, D), F32),
         pltpu.VMEM((2, SEG, D), F32),
         pltpu.VMEM((4 * SEG, D), BF),
         pltpu.VMEM((2, 2 * SEG, LANE), BF),
-        pltpu.VMEM((2, 2 * SEG, 2 * LANE), BF),
+        pltpu.VMEM((2, 2 * SEG, LANE), BF),
         pltpu.VMEM((2, 2 * SEG, 2 * LANE), BF),
         pltpu.VMEM((SEG, D), BF),
         pltpu.VMEM((2, SEG, D), BF),
         pltpu.VMEM((2, SEG, D), BF),
-        pltpu.VMEM((SEG, LANE), F32),
+        pltpu.VMEM((2, 2, SEG, LANE), F32),
+        pltpu.VMEM((2, SEG, 4 * LANE), BF),
     ]
-    counts = [5, 5, 5, 3, 3, 3, 2, 4, 4, 4, 2, 4, 4, 4, 4, 4, 0, 0, 2, 2]
+    counts = [5, 5, 5, 3, 3, 3, 2, 4, 4, 4, 2, 4, 4, 4, 0, 4, 0, 0, 2, 2, 2, 4, 1, 2, 1, 2, 2]
     scratch += [pltpu.SemaphoreType.DMA((n,)) if n else pltpu.SemaphoreType.DMA for n in counts]
-    in_specs = [hbm, hbm, vmem, hbm, vmem, vmem, hbm, hbm, hbm, hbm, hbm]
+    scratch += [pltpu.SemaphoreType.REGULAR]
+    smem = pl.BlockSpec(memory_space=pltpu.SMEM)
+    in_specs = [hbm, hbm, vmem, vmem, smem, smem, hbm, hbm, hbm, hbm, hbm]
     return pl.pallas_call(
         relay_kernel,
         out_shape=results,
         in_specs=in_specs,
-        out_specs=tuple([hbm] * 10 + [vmem, vmem]),
+        out_specs=tuple([hbm] * 11 + [vmem, vmem]),
         scratch_shapes=scratch,
         compiler_params=pltpu.CompilerParams(
             collective_id=0, has_side_effects=True, vmem_limit_bytes=63 * 2**20
@@ -961,6 +1116,91 @@
     )(*operands)
 
 
+def finish_kernel(
+    counts, lasts, tops, backs, tail, f_qkv, f_o, f_in, f_out, small, text, text_g, memory, mem_g, qkv_g, o_g, in_g, out_g, gains_g, biases_g
+):
+    step = pl.program_id(0)
+    place = lax.axis_index("pipe")
+    count, last = counts[place], lasts[place]
+    rows = tops.shape[1]
+    row = lax.broadcasted_iota(jnp.int32, (rows, D), 0) + step * rows
+    for k in range(2):
+        limit = jnp.where(count > 1, TEXT if k == 0 else last, last if k == 0 else 0)
+        text[:, k, :] = jnp.where(row < limit, tops[k].astype(F32), 0.0)
+        text_g[:, k, :] = backs[k].astype(F32)
+    qkv_g[...] = f_qkv[...].astype(F32)
+    o_g[...] = f_o[...].astype(F32)
+    in_g[...] = f_in[...].astype(F32)
+    out_g[...] = f_out[...].astype(F32)
+
+    @pl.when(step == 0)
+    def _():
+        ends = tail[...].astype(F32)
+        memory[0] = jnp.where(count > 1, ends[1], ends[0])[TAIL - MEM :, :]
+        width = D // 4
+        for index in range(4):
+
+            @pl.when(place == index)
+            def _():
+                mem_g[...] = small[SMALL - MEM :, index * width : (index + 1) * width]
+
+        gains_g[...] = small[0:1, :]
+        biases_g[...] = small[1:6, :]
+
+
+def finish(operands):
+    shape = jax.ShapeDtypeStruct
+    smem = pl.BlockSpec(memory_space=pltpu.SMEM)
+    steps = 8
+    row = SEG // steps
+
+    def split(rows, cols):
+        return pl.BlockSpec((rows, cols), lambda i: (i, 0))
+
+    def whole(*size):
+        return pl.BlockSpec(size, lambda i: (0,) * len(size))
+
+    pair = pl.BlockSpec((2, row, D), lambda i: (0, i, 0))
+    pair_out = pl.BlockSpec((row, 2, D), lambda i: (i, 0, 0))
+    grads = [split(row, 3 * D), split(row, D), split(row, FF), split(4 * row, D)]
+    counts, lasts, tops, backs, *rest = operands
+    return pl.pallas_call(
+        finish_kernel,
+        grid=(steps,),
+        out_shape=(
+            shape((TEXT, 2, D), F32),
+            shape((TEXT, 2, D), F32),
+            shape((1, MEM, D), F32),
+            shape((MEM, D // 4), F32),
+            shape((SEG, 3 * D), F32),
+            shape((SEG, D), F32),
+            shape((SEG, FF), F32),
+            shape((FF // 2, D), F32),
+            shape((1, D), F32),
+            shape((5, D), F32),
+        ),
+        in_specs=[
+            smem,
+            smem,
+            pair,
+            pair,
+            pl.BlockSpec((2, TAIL, D), lambda i: (0, SEG // TAIL - 1, 0)),
+            *grads,
+            whole(SMALL, D),
+        ],
+        out_specs=(
+            pair_out,
+            pair_out,
+            whole(1, MEM, D),
+            whole(MEM, D // 4),
+            *grads,
+            whole(1, D),
+            whole(5, D),
+        ),
+        compiler_params=pltpu.CompilerParams(vmem_limit_bytes=62 * 2**20),
+    )(counts, lasts, tops, backs, tops, *rest)
+
+
 def from_partner(x, axis, bit):
     return lax.ppermute(x, axis, [(i, i ^ 1 << bit) for i in range(lax.axis_size(axis))])
 
@@ -971,7 +1211,8 @@
     )
 
 
-def sum_grads(member, xs, ctxs, hids, acts, gps, gbs, gus, gds, vecg, memg):
+def sum_grads(member, operands):
+    xs, ctxs, hids, acts, gps, gbs, gus, gds, vecg, memg = operands
     def halves(left, right):
         size = left.shape[-1] // 2
         mine = lax.dynamic_slice_in_dim(left, member * size, size, 2)
@@ -994,7 +1235,7 @@
     mine_small = jnp.concatenate([vec_mine, memg], 0)
     small = mine_small + from_partner(jnp.concatenate([vec_theirs, memg], 0), "pipe", 0)
     *grads, small = lax.psum((*sums, small), "items")
-    return grads, small
+    return (*grads, small)
 
 
 def per_device(
@@ -1011,60 +1252,31 @@
     text_cot,
     memory_cot,
 ):
-    place = lax.axis_index("pipe")
-    first = place < 2
-    member = place % 2
+    member = lax.axis_index("pipe") % 2
     pad = ((0, 0), (0, SEG - TEXT), (0, 0))
-
-    count = counts[place]
-    lengths = jnp.stack([jnp.where(count > 1, TEXT, last_lengths[place]), last_lengths[place]])
-    two = count > 1
-    valid = jnp.stack([jnp.bool_(True), two])
-    shown = (jnp.arange(TEXT)[None, :] < lengths[:, None]) & valid[:, None]
     x_own = jnp.pad(text_in[0], pad)
-    c_own = jnp.pad(jnp.where(shown[:, :, None], text_cot[0], jnp.zeros_like(text_cot[0])), pad)
-    memory_full = lax.all_gather(memory, "pipe", axis=1, tiled=True)
-    mem0 = jnp.pad(jnp.concatenate([memory_full, memory_full], 0), ((TAIL - 2 * MEM, 0), (0, 0)))
-    placed = jnp.pad(memory_cot[0].astype(F32), ((TAIL - MEM, 0), (0, 0)))
-    mc_own = jnp.stack([jnp.where(two, placed, 0.0), jnp.where(two, 0.0, placed)])
-    pair_counts = jnp.stack([counts[member], counts[member + 2]])
-    pair_last = jnp.stack([last_lengths[member], last_lengths[member + 2]])
-    flags = jnp.broadcast_to((pair_counts > 1).astype(F32)[:, None, None], (2, 1, D))
-    unit_lengths = jnp.concatenate([jnp.where(pair_counts > 1, TEXT, pair_last), pair_last])
-    rows = jnp.arange(SEG)
-    keep = (rows[None, :] >= TEXT) | (rows[None, :] < unit_lengths[:, None])
-    kmask = jnp.where(keep, 0.0, MASKED).astype(F32)[:, None, :]
+    c_own = jnp.pad(text_cot[0], pad)
+    mem_own = jnp.pad(memory, ((0, 16 - MEM), (0, 2 * LANE - memory.shape[1])))
+    mcot_own = jnp.pad(memory_cot[0], ((TAIL - MEM, 0), (0, 0)))
     vec_own = jnp.concatenate(
         [gains[None], biases.reshape(5, D), jnp.zeros((2, D), gains.dtype)], 0
     ).astype(F32)
-
-    xs, ctxs, hids, acts, tops, gds, gus, gbs, gps, backs, vecg, memg = relay(
-        (x_own, c_own, mem0, mc_own, flags, kmask, w_qkv, w_o, w_in, w_out, vec_own)
+    xs, ctxs, hids, acts, own_top, gds, gus, gbs, gps, own_back, _, vecg, memg = relay(
+        (x_own, c_own, mem_own, mcot_own, counts, last_lengths, w_qkv, w_o, w_in, w_out, vec_own)
     )
-
-    outgoing = jnp.where(first, backs[1::2], tops[0::2])
-    returned = from_partner(outgoing, "pipe", 1)
-    if lax.axis_size("items") == 8:
-        *grads, small = reduce_grads((xs, ctxs, hids, acts, gps, gbs, gus, gds, vecg, memg))
-        grads = [grad.astype(F32) for grad in grads]
-    else:
-        grads, small = sum_grads(member, xs, ctxs, hids, acts, gps, gbs, gus, gds, vecg, memg)
-    own_top = jnp.where(first, returned, tops[1::2])
-    own_back = jnp.where(first, backs[0::2], returned)
-    final_text = jnp.where(shown[:, :, None], own_top[:, :TEXT].astype(F32), 0.0)[None]
-    text_grad = own_back[:, :TEXT].astype(F32)[None]
-    ends = own_top[:, SEG - MEM :].astype(F32)
-    final_memory = jnp.where(two, ends[1], ends[0])[None]
-    width = D // 4
-    memory_grad = lax.dynamic_slice(small, (SMALL - MEM, place * width), (MEM, width))
+    sum_all = reduce_grads if lax.axis_size("items") == 8 else functools.partial(sum_grads, member)
+    sums = sum_all((xs, ctxs, hids, acts, gps, gbs, gus, gds, vecg, memg))
+    text, text_grad, last_memory, memory_grad, *grads, gains_grad, biases_grad = finish(
+        (counts, last_lengths, own_top, own_back, *sums)
+    )
     return (
-        final_text,
-        final_memory,
-        text_grad,
+        text.transpose(1, 0, 2)[None],
+        last_memory,
+        text_grad.transpose(1, 0, 2)[None],
         memory_grad,
         *grads,
-        small[0],
-        small[1:6].reshape(5 * D),
+        gains_grad.reshape(D),
+        biases_grad.reshape(5 * D),
     )
 
 

time: 449 us -> 415 us (0.924)
  other arithmetic: 23.6 us -> 1.97 us
  local copies, waits for them, and re-layouts: 20.3 us -> 10.7 us
  Pallas kernels: 393 us -> 401 us
  blocking collectives: 6.42 us -> 0 us
    pallas_call x0 -> x1, Pallas kernels: none -> 12.1 us  [finish(): pl.pallas_call(finish_kernel, grid=(steps,), out_shape=(shape((TEXT, 2, D...]
    convert_element_type x6 -> x0, other arithmetic: 11 us -> none  [the longest x4 9.61 us: per_device(): grads = [grad.astype(F32) for grad in grads]]
    all_gather x1 -> x0, blocking collectives: 6.42 us -> none  [per_device(): memory_full = lax.all_gather(memory, 'pipe', axis=1, tiled=True)]
    unnamed x13 -> x5, local copies, waits for them, and re-layouts: 9.09 us -> 2.92 us
    select_n x5 -> x0, other arithmetic: 4.94 us -> none  [the longest x1 2.66 us: per_device(): jnp.where(pair_counts > 1, TEXT, pair_last)]
  transfers between devices with their start and end apart: 1 -> 0, of which waited for: 0 -> 0; matrix products, arithmetic and copies ran while one was open for 3% -> 0% of each run, Pallas kernels for 38% -> 0%
where the time goes in v3:
time: 415 us; the launch traced here: 414 us
  Pallas kernels  401 us (97%)
  local copies, waits for them, and re-layouts  10.7 us (3%)
    pallas_call x1, Pallas kernels, relay(): pl.pallas_call(relay_kernel, out_shape=results, in_specs=in_specs, out_sp...  218 us
    pallas_call x1, Pallas kernels, reduce_grads(): pl.pallas_call(reduce_kernel, out_shape=(shape((SEG, 3 * D), BF), shape((...  171 us
    pallas_call x1, Pallas kernels, finish(): pl.pallas_call(finish_kernel, grid=(steps,), out_shape=(shape((TEXT, 2, D...  12.1 us

profile of v3, /device:TPU:0, one launch (start us, length us, event | category | flops | bytes accessed | tf_op | source)
XLA Modules:
  0.0 414.5 jit_solution(512661826619341451)
XLA Ops:
  0.7 0.1 pad.21.clone
  0.7 0.0 copy-start
  0.7 0.8 broadcast_in_dim.12
  1.5 1.3 pad.17.mem_own
  2.8 0.7 reshape.29
  3.5 0.7 maximum_convert_fusion.vec_own
  4.2 1.4 pad.18.mcot_own
  5.6 1.4 copy.28
  6.9 1.1 pad.15.x_own
  8.0 0.0 copy-done
  8.0 0.1 copy.27
  8.2 1.1 pad.16.c_own
  9.2 217.7 %shard_map.195 = (bf16[4,384,768]{2,1,0:T(8,128)(2,1)}, bf16[4,384,768]{2,1,0:T(8,128)(2,1)}, bf16[4,384,768]{2,1,0:T(8,128)(2,1)}, bf16[4,1536,768]{2,1,0:T(8,1...) custom-call(bf16[2,384,768]{2,1,0:T(8,128)(2,1)} %pad.15.x_own, ...), custom_call_target="tpu_custom_call" | custom-call | flops 80000000000 | bytes 83886080 | tf_op jit(solution)/shard_map/pallas_call | solution.py:803
  227.0 171.3 %shard_map.196 = (bf16[384,2304]{1,0:T(8,128)(2,1)}, bf16[384,768]{1,0:T(8,128)(2,1)}, bf16[384,3072]{1,0:T(8,128)(2,1)}, bf16[1536,768]{1,0:T(8,128)(2,1)}, f32[40,768]{1,0:T(8,128)}) custom-call(bf16[4,384,768]{2,1,0:T(8,128)(2,1)} %get-tuple-element.39.xs, bf16[4,384,768]{2,1,0:T(8,128)(2,1)} %get-tuple-element.40.ctxs, ...), custom_call_target="tpu_custom_call" | custom-call | flops 22000001024 | bytes 67108864 | tf_op jit(solution)/shard_map/pallas_call | solution.py:1079
  398.3 12.1 %shard_map.197 = (f32[364,2,768]{2,1,0:T(2,128)}, f32[364,2,768]{2,1,0:T(2,128)}, f32[1,10,768]{2,1,0:T(8,128)}, f32[10,192]{1,0:T(8,128)}, f32[384,2304]{1,0:T(...) custom-call(s32[4]{0:T(128)} %counts.3, s32[4]{0:T(128)} %lasts.3, ...), custom_call_target="tpu_custom_call" | custom-call | tf_op jit(solution)/shard_map/pallas_call | solution.py:1167
  410.4 1.3 reduce
  411.7 1.3 reshape.31
  413.0 1.4 copy.24
  (1 shorter events, 0.0 us)
Async XLA Ops:
  0.7 7.3 %copy-start = (bf16[1,2,364,768]{3,1,2,0:T(2,128)(2,1)S(1)}, bf16[1,2,364,768]{3,1,2,0:T(2,128)(2,1)}, u32[]{:S(2)}) copy-start(bf16[1,2,364,768]{3,1,2,0:T(2,128)(2,1)} %param.22) | copy-start | bytes 3354628

commit v4 on v3

--- a/solution.py
+++ b/solution.py
@@ -329,10 +329,6 @@
             for copy in x_home:
                 copy.wait()
 
-        @pl.when(first & (member == 1) & (u == 0))
-        def _():
-            pl.semaphore_wait(lag, 1)
-
         @pl.when(first & (u == 1))
         def _():
             x_away[0].wait_recv()
@@ -401,10 +397,6 @@
                 big[b * 2 * SEG : b * 2 * SEG + SEG, :], stv[b]
             ).astype(BF)
         pltpu.make_async_copy(ctx.at[u], ctxs.at[u], ctx_sem.at[u]).start()
-
-        @pl.when(first & (member == 0) & (u == 0))
-        def _():
-            pl.semaphore_signal(lag, inc=1, device_id=twin, device_id_type=MESH)
 
         @pl.when(u == 0)
         def _():
@@ -814,8 +806,12 @@
 
 
 BLOCKS_G = 12
-CHUNK = SEG // 8
-STAGES = 15
+PARTS = 4
+CHUNK = SEG // PARTS
+PIECES = BLOCKS_G * PARTS
+STAGES = 8
+SLACK = 4
+PATH_BLOCKS = (0, 3, 6, 9)
 SMALL = 8 + TAIL
 
 
@@ -841,17 +837,22 @@
     own,
     sent,
     tw,
-    ring0,
-    ring,
+    low_rx,
+    high_rx,
     fin,
+    acc,
     sm_tw,
     sm_rx,
     sm_tx,
     load_sem,
     tw_send,
     tw_recv,
-    ring_send,
-    ring_recv,
+    up_send,
+    low_recv,
+    high_recv,
+    rung_recv,
+    down_send,
+    down_recv,
     fin_sem,
     sm_send,
     sm_recv,
@@ -861,27 +862,29 @@
     member = lax.rem(place, 2)
     twin = {"pipe": place + 1 - 2 * member}
     x_at, z_at = lax.rem(item, 2), item // 2
-    at = x_at * (7 - z_at) + (1 - x_at) * z_at
-    turn = 1 - 2 * member
-    logical = (1 - member) * at + member * (7 - at)
-
-    def item_of(position):
-        p = lax.rem(position + 8, 8)
-        up = p // 4
-        return up * (2 * (7 - p) + 1) + (1 - up) * 2 * p
-
-    ahead = {"items": item_of(at + turn)}
-    behind = {"items": item_of(at - turn)}
-    rounds = [
-        {"items": item + 1 - 2 * x_at},
-        {"items": item + 2 - 4 * lax.rem(z_at, 2)},
-        {"items": item + 4 - 8 * (z_at // 2)},
-    ]
+    rung = {"items": item + 1 - 2 * x_at}
+    above = {"items": lax.rem(item + 2, 8)}
+    below = {"items": lax.rem(item + 6, 8)}
+    pair = {"items": item + 2 - 4 * lax.rem(z_at, 2)}
+    far = {"items": item + 4 - 8 * (z_at // 2)}
+    rounds = [rung, pair, far]
+    has_above, has_below = z_at < 3, z_at > 0
 
     barrier = pltpu.get_barrier_semaphore()
-    for to in [twin, ahead, behind, *rounds]:
+
+    def greet(to):
         pl.semaphore_signal(barrier, inc=1, device_id=to, device_id_type=MESH)
-    pl.semaphore_wait(barrier, 6)
+
+    for to in (twin, rung, far):
+        greet(to)
+
+    @pl.when(has_above)
+    def _():
+        greet(above)
+
+    @pl.when(has_below)
+    def _():
+        greet(below)
 
     def remote(src, dst, send, recv, to):
         return pltpu.make_async_remote_copy(
@@ -935,15 +938,6 @@
     def twin_copy(b, slot):
         return remote(sent.at[slot], tw.at[b], tw_send.at[slot], tw_recv.at[b], twin)
 
-    def rows_of(c):
-        return pl.ds(pl.multiple_of(c * CHUNK, 16), CHUNK)
-
-    def ring_copy(b, s, src, dst):
-        return remote(src, dst, ring_send.at[b, s], ring_recv.at[b, s], ahead)
-
-    def ring_wait(b, s):
-        ring_copy(b, s, ring0.at[b], ring0.at[b]).wait_recv()
-
     def out_copy(b, go):
         @pl.when(b < 4)
         def _():
@@ -961,38 +955,126 @@
         def _():
             go(f_qkv.at[:, aligned((b - 9) * D, D)])
 
-    def stage(b, s):
-        c = lax.rem(logical - s + 16, 8)
-        rows = rows_of(c)
-
-        def part():
-            return own[b, rows, :] + tw[b, rows, :].astype(F32)
-
-        @pl.when(s == 0)
-        def _():
-            twin_copy(b, 0).wait_recv()
-            ring0[b] = part().astype(BF)
-            ring_copy(b, 0, ring0.at[b], ring.at[b, 0]).start()
-
-        @pl.when(s > 0)
-        def _():
-            ring_wait(b, s - 1)
-
-        @pl.when((s > 0) & (s < 7))
-        def _():
-            total = ring[b, s - 1].astype(F32) + part()
-            ring[b, s - 1] = total.astype(BF)
-            ring_copy(b, s, ring.at[b, s - 1], ring.at[b, s]).start()
-
-        @pl.when(s == 7)
-        def _():
-            fin[b, rows, :] = (ring[b, 6].astype(F32) + part()).astype(BF)
-
-        @pl.when((s >= 7) & (s < STAGES - 1))
-        def _():
-            ring_copy(b, s, fin.at[b, rows], fin.at[b, rows]).start()
-
-        @pl.when(s == STAGES - 1)
+    def piece(j):
+        b, k = j // PARTS, lax.rem(j, PARTS)
+        path = b == PATH_BLOCKS[0]
+        for other_block in PATH_BLOCKS[1:]:
+            path = path | (b == other_block)
+        row = jnp.where(path, jnp.where(k < 4, k, k + 2 - PARTS // 2 - PARTS // 4), 1 + lax.rem(k // 2, 2))
+        root = row + member * (3 - 2 * row)
+        chain = path | (x_at == lax.rem(k + member, 2))
+        away = jnp.abs(z_at - root)
+        rows = pl.ds(pl.multiple_of(k * CHUNK, 16), CHUNK)
+        return b, k, rows, path, root, chain, away
+
+    def low_copy(j):
+        return remote(low_rx.at[j], low_rx.at[j], up_send.at[j], low_recv.at[j], above)
+
+    def high_copy(j):
+        return remote(low_rx.at[j], high_rx.at[j], up_send.at[j], high_recv.at[j], below)
+
+    def rung_up(j, b, rows):
+        return remote(low_rx.at[j], fin.at[b, rows], up_send.at[j], rung_recv.at[j], rung)
+
+    def rung_down(j, b, rows):
+        return remote(fin.at[b, rows], fin.at[b, rows], down_send.at[2, j], rung_recv.at[j], rung)
+
+    def below_down(j, b, rows):
+        return remote(fin.at[b, rows], fin.at[b, rows], down_send.at[0, j], down_recv.at[j], below)
+
+    def above_down(j, b, rows):
+        return remote(fin.at[b, rows], fin.at[b, rows], down_send.at[1, j], down_recv.at[j], above)
+
+    def spread(j, act):
+        b, k, rows, path, root, chain, away = piece(j)
+
+        @pl.when(chain & has_below & (z_at <= root))
+        def _():
+            act(below_down(j, b, rows))
+
+        @pl.when(chain & has_above & (z_at >= root))
+        def _():
+            act(above_down(j, b, rows))
+
+        @pl.when(chain & jnp.logical_not(path))
+        def _():
+            act(rung_down(j, b, rows))
+
+    def gather(j):
+        b, k, rows, path, root, chain, away = piece(j)
+        acc[...] = own[b, rows, :] + tw[b, rows, :].astype(F32)
+
+        @pl.when(chain & jnp.logical_not(path))
+        def _():
+            rung_down(j, b, rows).wait_recv()
+            acc[...] += fin[b, rows, :].astype(F32)
+
+        @pl.when(chain & has_below & (z_at <= root))
+        def _():
+            low_copy(j).wait_recv()
+            acc[...] += low_rx[j].astype(F32)
+
+        @pl.when(chain & has_above & (z_at >= root))
+        def _():
+            high_copy(j).wait_recv()
+            acc[...] += high_rx[j].astype(F32)
+
+        here = chain & (away == 0)
+
+        @pl.when(here & jnp.logical_not(path))
+        def _():
+            fin[b, rows, :] = acc[...].astype(BF)
+            spread(j, lambda copy: copy.start())
+
+        @pl.when(jnp.logical_not(here & jnp.logical_not(path)))
+        def _():
+            low_rx[j] = acc[...].astype(BF)
+
+        @pl.when(jnp.logical_not(chain) | (here & path))
+        def _():
+            rung_up(j, b, rows).start()
+
+        @pl.when(chain & (z_at < root))
+        def _():
+            low_copy(j).start()
+
+        @pl.when(chain & (z_at > root))
+        def _():
+            high_copy(j).start()
+
+    def settle(j):
+        b, k, rows, path, root, chain, away = piece(j)
+
+        @pl.when(jnp.logical_not(chain) | (away == 0))
+        def _():
+            rung_down(j, b, rows).wait_recv()
+
+        @pl.when(chain & (away == 0))
+        def _():
+            fin[b, rows, :] = (low_rx[j].astype(F32) + fin[b, rows, :].astype(F32)).astype(BF)
+
+        @pl.when(chain & (away > 0))
+        def _():
+            below_down(j, b, rows).wait_recv()
+
+        @pl.when(chain)
+        def _():
+            spread(j, lambda copy: copy.start())
+
+    def stage(j, t):
+        b, k, rows, path, root, chain, away = piece(j)
+
+        @pl.when(t == jnp.where(chain, 3 - away, 0))
+        def _():
+            gather(j)
+
+        later = jnp.where(path | jnp.logical_not(chain), 4 + away, 3 + away)
+
+        @pl.when((t == later) & jnp.logical_not(chain & (away == 0) & jnp.logical_not(path)))
+        def _():
+            settle(j)
+
+        @pl.when((t == STAGES - 1) & (k == PARTS - 1))
         def _():
             out_copy(b, lambda dst: pltpu.make_async_copy(fin.at[b], dst, fin_sem.at[b]).start())
 
@@ -1003,6 +1085,16 @@
         return remote(small, sm_rx.at[k], sm_send.at[k + 1], sm_recv.at[k + 1], rounds[k])
 
     start_loads(0, 0)
+
+    def product(slot, left):
+        return tn(left[slot].reshape(UNITS * SEG, SEG), gg[slot].reshape(UNITS * SEG, D))
+
+    wait_loads(0)
+    start_loads(1, 1)
+    sent[0] = product(0, xt).astype(BF)
+    ends = z_at * (3 - z_at)
+    pl.semaphore_wait(barrier, 4 + ends // 2)
+    twin_copy(0, 0).start()
     eight = pl.ds(pl.multiple_of((1 - member) * 8, 8), 8)
     mine8 = pl.ds(pl.multiple_of(member * 8, 8), 8)
     sm_tx[0, :8, :] = vecg[eight, :]
@@ -1012,28 +1104,36 @@
     small_twin().start()
 
     def step(i, carry):
-        slot = lax.rem(i, 2)
-
-        @pl.when(i < BLOCKS_G)
-        def _():
-            wait_loads(slot)
-
-            @pl.when(i + 1 < BLOCKS_G)
+        now = i // PARTS
+        fresh = lax.rem(i, PARTS) == 0
+        slot = lax.rem(now, 2)
+
+        @pl.when(fresh & (now < BLOCKS_G))
+        def _():
+            @pl.when(now > 0)
             def _():
-                start_loads(i + 1, 1 - slot)
-
-            @pl.when(i >= 2)
-            def _():
-                twin_copy(i - 2, slot).wait_send()
-
-            right = gg[slot].reshape(UNITS * SEG, D)
-            sent[slot] = tn(xt[slot].reshape(UNITS * SEG, SEG), right).astype(BF)
-            twin_copy(i, slot).start()
-            own[i] = tn(xm[slot].reshape(UNITS * SEG, SEG), right)
+                wait_loads(slot)
+
+                @pl.when(now + 1 < BLOCKS_G)
+                def _():
+                    start_loads(now + 1, 1 - slot)
+
+                @pl.when(now >= 2)
+                def _():
+                    twin_copy(now - 2, slot).wait_send()
+
+                sent[slot] = product(slot, xt).astype(BF)
+                twin_copy(now, slot).start()
+
+            own[now] = product(slot, xm)
+
+        @pl.when(fresh & (now > 0) & (now <= BLOCKS_G))
+        def _():
+            twin_copy(now - 1, 0).wait_recv()
 
         for k in range(4):
 
-            @pl.when(i == 2 * k + 2)
+            @pl.when(i == 4 * k + 4)
             def _():
                 if k == 0:
                     small_twin().wait()
@@ -1044,31 +1144,39 @@
                 if k < 3:
                     small_round(k).start()
 
-        first_b = jnp.maximum(i - STAGES, 0)
-        last_b = jnp.minimum(i, BLOCKS_G)
-
-        def serve(b, inner):
-            stage(b, i - 1 - b)
+        def serve(t, inner):
+            j = i - PARTS - SLACK * t
+
+            @pl.when((j >= 0) & (j < PIECES))
+            def _():
+                stage(j, t)
+
             return inner
 
-        lax.fori_loop(first_b, last_b, serve, 0)
+        lax.fori_loop(0, STAGES, serve, 0)
         return carry
 
-    lax.fori_loop(0, BLOCKS_G + STAGES, step, 0)
+    lax.fori_loop(0, PARTS + PIECES + SLACK * (STAGES - 1), step, 0)
 
     twin_copy(0, 0).wait_send()
     twin_copy(1, 1).wait_send()
 
-    def drain(b, carry):
-        def one(s, inner):
-            ring_copy(b, s, ring0.at[b], ring0.at[b]).wait_send()
-            return inner
-
-        lax.fori_loop(0, STAGES - 1, one, 0)
-        out_copy(b, lambda dst: pltpu.make_async_copy(fin.at[b], dst, fin_sem.at[b]).wait())
+    def drain(j, carry):
+        b, k, rows, path, root, chain, away = piece(j)
+
+        @pl.when(jnp.logical_not(chain & (away == 0) & jnp.logical_not(path)))
+        def _():
+            low_copy(j).wait_send()
+
+        spread(j, lambda copy: copy.wait_send())
+
+        @pl.when(k == 0)
+        def _():
+            out_copy(b, lambda dst: pltpu.make_async_copy(fin.at[b], dst, fin_sem.at[b]).wait())
+
         return carry
 
-    lax.fori_loop(0, BLOCKS_G, drain, 0)
+    lax.fori_loop(0, PIECES, drain, 0)
 
 
 def reduce_grads(operands):
@@ -1094,17 +1202,22 @@
             pltpu.VMEM((BLOCKS_G, SEG, D), F32),
             pltpu.VMEM((2, SEG, D), BF),
             pltpu.VMEM((BLOCKS_G, SEG, D), BF),
-            pltpu.VMEM((BLOCKS_G, CHUNK, D), BF),
-            pltpu.VMEM((BLOCKS_G, 7, CHUNK, D), BF),
+            pltpu.VMEM((PIECES, CHUNK, D), BF),
+            pltpu.VMEM((PIECES, CHUNK, D), BF),
             pltpu.VMEM((BLOCKS_G, SEG, D), BF),
+            pltpu.VMEM((CHUNK, D), F32),
             pltpu.VMEM((SMALL, D), F32),
             pltpu.VMEM((3, SMALL, D), F32),
             pltpu.VMEM((1, SMALL, D), F32),
             dma((2, 3)),
             dma((2,)),
             dma((BLOCKS_G,)),
-            dma((BLOCKS_G, STAGES - 1)),
-            dma((BLOCKS_G, STAGES - 1)),
+            dma((PIECES,)),
+            dma((PIECES,)),
+            dma((PIECES,)),
+            dma((PIECES,)),
+            dma((3, PIECES)),
+            dma((PIECES,)),
             dma((BLOCKS_G,)),
             dma((4,)),
             dma((4,)),

time: 415 us -> 393 us (0.947)
  Pallas kernels: 401 us -> 376 us
    pallas_call x1, Pallas kernels: 171 us -> 149 us  [reduce_grads(): pl.pallas_call(reduce_kernel, out_shape=(shape((SEG, 3 * D), BF), shape((...]
where the time goes in v4:
time: 393 us; the launch traced here: 390 us
  Pallas kernels  376 us (96%)
  local copies, waits for them, and re-layouts  10.7 us (3%)
    pallas_call x1, Pallas kernels, relay(): pl.pallas_call(relay_kernel, out_shape=results, in_specs=in_specs, out_sp...  215 us
    pallas_call x1, Pallas kernels, reduce_grads(): pl.pallas_call(reduce_kernel, out_shape=(shape((SEG, 3 * D), BF), shape((...  149 us
    pallas_call x1, Pallas kernels, finish(): pl.pallas_call(finish_kernel, grid=(steps,), out_shape=(shape((TEXT, 2, D...  12.1 us

profile of v4, /device:TPU:0, one launch (start us, length us, event | category | flops | bytes accessed | tf_op | source)
XLA Modules:
  0.0 389.8 jit_solution(9388618813805593157)
XLA Ops:
  0.7 0.1 pad.21.clone
  0.7 0.0 copy-start
  0.7 0.8 broadcast_in_dim.12
  1.5 1.3 pad.17.mem_own
  2.8 0.7 reshape.29
  3.5 0.7 maximum_convert_fusion.vec_own
  4.2 1.4 pad.18.mcot_own
  5.6 1.4 copy.28
  6.9 1.1 pad.15.x_own
  8.0 0.0 copy-done
  8.0 0.1 copy.27
  8.2 1.1 pad.16.c_own
  9.2 215.1 %shard_map.195 = (bf16[4,384,768]{2,1,0:T(8,128)(2,1)}, bf16[4,384,768]{2,1,0:T(8,128)(2,1)}, bf16[4,384,768]{2,1,0:T(8,128)(2,1)}, bf16[4,1536,768]{2,1,0:T(8,1...) custom-call(bf16[2,384,768]{2,1,0:T(8,128)(2,1)} %pad.15.x_own, ...), custom_call_target="tpu_custom_call" | custom-call | flops 80000000000 | bytes 83886080 | tf_op jit(solution)/shard_map/pallas_call | solution.py:795
  224.3 149.3 %shard_map.196 = (bf16[384,2304]{1,0:T(8,128)(2,1)}, bf16[384,768]{1,0:T(8,128)(2,1)}, bf16[384,3072]{1,0:T(8,128)(2,1)}, bf16[1536,768]{1,0:T(8,128)(2,1)}, f32[40,768]{1,0:T(8,128)}) custom-call(bf16[4,384,768]{2,1,0:T(8,128)(2,1)} %get-tuple-element.39.xs, bf16[4,384,768]{2,1,0:T(8,128)(2,1)} %get-tuple-element.40.ctxs, ...), custom_call_target="tpu_custom_call" | custom-call | flops 22000001024 | bytes 67108864 | tf_op jit(solution)/shard_map/pallas_call | solution.py:1187
  373.6 12.1 %shard_map.197 = (f32[364,2,768]{2,1,0:T(2,128)}, f32[364,2,768]{2,1,0:T(2,128)}, f32[1,10,768]{2,1,0:T(8,128)}, f32[10,192]{1,0:T(8,128)}, f32[384,2304]{1,0:T(...) custom-call(s32[4]{0:T(128)} %counts.3, s32[4]{0:T(128)} %lasts.3, ...), custom_call_target="tpu_custom_call" | custom-call | tf_op jit(solution)/shard_map/pallas_call | solution.py:1280
  385.7 1.3 reduce
  387.0 1.3 reshape.31
  388.3 1.4 copy.24
  (1 shorter events, 0.0 us)
Async XLA Ops:
  0.7 7.3 %copy-start = (bf16[1,2,364,768]{3,1,2,0:T(2,128)(2,1)S(1)}, bf16[1,2,364,768]{3,1,2,0:T(2,128)(2,1)}, u32[]{:S(2)}) copy-start(bf16[1,2,364,768]{3,1,2,0:T(2,128)(2,1)} %param.22) | copy-start | bytes 3354628

commit v5 on v4

--- a/solution.py
+++ b/solution.py
@@ -87,8 +87,8 @@
 def relay_kernel(
     x_own,
     c_own,
-    mem_own,
-    mcot_own,
+    mem_raw,
+    mcot_raw,
     counts,
     lasts,
     w_qkv,
@@ -118,6 +118,8 @@
     gsl,
     mcs,
     mem_rx,
+    mem_own,
+    mcot_own,
     mem0,
     trx,
     packed,
@@ -175,16 +177,6 @@
     across = {"pipe": 3 - place}
     second = jnp.logical_not(first)
 
-    barrier = pltpu.get_barrier_semaphore()
-    for to in (twin, other, across):
-        pl.semaphore_signal(barrier, inc=1, device_id=to, device_id_type=MESH)
-    pl.semaphore_wait(barrier, 3)
-
-    def remote(src, dst, send, recv, to):
-        return pltpu.make_async_remote_copy(
-            src_ref=src, dst_ref=dst, send_sem=send, recv_sem=recv, device_id=to, device_id_type=MESH
-        )
-
     halves = (
         (vec_own, vec, 8),
         (w_qkv, wq, D // 2),
@@ -192,14 +184,47 @@
         (w_in, wi, D // 2),
         (w_out, wd, FF // 2),
     )
-    locals_, sends, recvs = [], [], []
-    for index, (src, dst, rows) in enumerate(halves):
-        mine = dst.at[pl.ds(pl.multiple_of(member * rows, rows), rows)]
-        theirs = dst.at[pl.ds(pl.multiple_of((1 - member) * rows, rows), rows)]
-        locals_.append(pltpu.make_async_copy(src, mine, w_local.at[index]))
+
+    def weight_rows(index, who):
+        src, dst, rows = halves[index]
+        return dst.at[pl.ds(pl.multiple_of(who * rows, rows), rows)]
+
+    def local_weight(index):
+        return pltpu.make_async_copy(
+            halves[index][0], weight_rows(index, member), w_local.at[index]
+        )
+
+    def x_here(k):
+        return pltpu.make_async_copy(x_own.at[k], xin.at[2 * k], e_local.at[k])
+
+    barrier = pltpu.get_barrier_semaphore()
+    for to in (twin, other, across):
+        pl.semaphore_signal(barrier, inc=1, device_id=to, device_id_type=MESH)
+    mem_own[...] = jnp.zeros_like(mem_own)
+    mem_own[:MEM, : D // 4] = mem_raw[...]
+    mcot_own[...] = jnp.zeros_like(mcot_own)
+    mcot_own[TAIL - MEM :, :] = mcot_raw[:, 0, :].astype(BF)
+    for index in (0, 1):
+        local_weight(index).start()
+
+    @pl.when(first)
+    def _():
+        for k in range(2):
+            x_here(k).start()
+
+    pl.semaphore_wait(barrier, 3)
+
+    def remote(src, dst, send, recv, to):
+        return pltpu.make_async_remote_copy(
+            src_ref=src, dst_ref=dst, send_sem=send, recv_sem=recv, device_id=to, device_id_type=MESH
+        )
+
+    sends, recvs = [], []
+    for index, (src, _, _) in enumerate(halves):
+        mine, theirs = weight_rows(index, member), weight_rows(index, 1 - member)
         sends.append(remote(src, mine, w_send.at[index], w_recv.at[index], twin))
         recvs.append(remote(src, theirs, w_send.at[index], w_recv.at[index], twin))
-    x_home = [pltpu.make_async_copy(x_own.at[k], xin.at[2 * k], e_local.at[k]) for k in range(2)]
+    x_home = [x_here(k) for k in range(2)]
     x_away = [
         remote(x_own.at[k], xin.at[2 * k + 1], e_send.at[k], e_recv.at[k], other) for k in range(2)
     ]
@@ -216,11 +241,10 @@
     mem_across = remote(mem_own, mem_rx.at[place], mem_send.at[1], mem_recv.at[place], across)
 
     def start_weights(index):
-        locals_[index].start()
         sends[index].start()
 
     def wait_weights(index):
-        locals_[index].wait()
+        local_weight(index).wait()
         recvs[index].wait_recv()
 
     start_weights(0)
@@ -228,8 +252,6 @@
 
     @pl.when(first)
     def _():
-        for copy in x_home:
-            copy.start()
         mem_twin.start()
 
     @pl.when(second)
@@ -322,6 +344,7 @@
             wait_weights(0)
             wait_weights(1)
             for index in (2, 3, 4):
+                local_weight(index).start()
                 start_weights(index)
 
         @pl.when(first & (u == 0))
@@ -519,10 +542,10 @@
         m_home.wait()
 
     def gd_copy(u):
-        return pltpu.make_async_copy(gdb.at[0], gds.at[u], gd_sem.at[0])
+        return pltpu.make_async_copy(hid, gds.at[u], gd_sem.at[0])
 
     def gb_copy(u):
-        return pltpu.make_async_copy(gdb.at[1], gbs.at[u], gd_sem.at[1])
+        return pltpu.make_async_copy(gdb, gbs.at[u], gd_sem.at[1])
 
     def gu_copy(u):
         return pltpu.make_async_copy(gub, gus.at[u], gu_sem)
@@ -578,13 +601,13 @@
             second_grad = norm_back(grad, normed, st[u, rows, 13:14], v(G2))
             sc[0, rows, :] = second_grad
             down = second_grad.astype(BF)
-            gdb[0, rows, :] = down
+            hid[rows, :] = down
             vecg[G2 : G2 + 1, :] += row_sum(grad * normed)
             vecg[N2 : N2 + 1, :] += row_sum(grad)
             vecg[BD : BD + 1, :] += row_sum(down.astype(F32))
         gd_copy(u).start()
         for j in range(4):
-            sd[j % 2] = nt(gdb[0], wd[j * D : (j + 1) * D, :])
+            sd[j % 2] = nt(hid[...], wd[j * D : (j + 1) * D, :])
             for rows in BLOCKS:
                 cols = slice(j * D, (j + 1) * D)
                 lifted = (sd[j % 2, rows, :] * dgf[rows, cols]).astype(BF)
@@ -602,13 +625,13 @@
             normed = n1s[u, rows, :]
             first_grad = norm_back(grad, normed, st[u, rows, 12:13], v(G1))
             branch = first_grad.astype(BF)
-            gdb[1, rows, :] = branch
+            gdb[rows, :] = branch
             vecg[G1 : G1 + 1, :] += row_sum(grad * normed)
             vecg[N1 : N1 + 1, :] += row_sum(grad)
             vecg[BO : BO + 1, :] += row_sum(branch.astype(F32))
             n1s[u, rows, :] = first_grad
         gb_copy(u).start()
-        grad_ctx = nt(gdb[1], wo[...]).astype(BF)
+        grad_ctx = nt(gdb[...], wo[...]).astype(BF)
         ctx[u] = grad_ctx
         mask = key_mask(length)
 
@@ -766,6 +789,8 @@
         pltpu.VMEM(rows, BF),
         pltpu.VMEM((2, TAIL, D), BF),
         pltpu.VMEM((4, 16, 2 * LANE), BF),
+        pltpu.VMEM((16, 2 * LANE), BF),
+        pltpu.VMEM((TAIL, D), BF),
         pltpu.VMEM((TAIL, D), BF),
         pltpu.VMEM((UNITS, TAIL, D), BF),
         pltpu.VMEM((UNITS, SEG, 3 * D), BF),
@@ -783,7 +808,7 @@
         pltpu.VMEM((2, 2 * SEG, 2 * LANE), BF),
         pltpu.VMEM((SEG, D), BF),
         pltpu.VMEM((2, SEG, D), BF),
-        pltpu.VMEM((2, SEG, D), BF),
+        pltpu.VMEM((SEG, D), BF),
         pltpu.VMEM((2, 2, SEG, LANE), F32),
         pltpu.VMEM((2, SEG, 4 * LANE), BF),
     ]
@@ -813,6 +838,7 @@
 SLACK = 4
 PATH_BLOCKS = (0, 3, 6, 9)
 SMALL = 8 + TAIL
+FINISH = 62
 
 
 def reduce_kernel(
@@ -826,13 +852,9 @@
     gds,
     vecg,
     mem_part,
-    f_qkv,
-    f_o,
-    f_in,
-    f_out,
+    sums,
     small,
-    xt,
-    xm,
+    xb,
     gg,
     own,
     sent,
@@ -895,8 +917,12 @@
         rows_t, col_t = theirs_rows
         rows_m, col_m = mine_rows
         return [
-            pltpu.make_async_copy(left.at[:, rows_t, col_t], xt.at[slot], load_sem.at[slot, 0]),
-            pltpu.make_async_copy(left.at[:, rows_m, col_m], xm.at[slot], load_sem.at[slot, 1]),
+            pltpu.make_async_copy(
+                left.at[:, rows_t, col_t], xb.at[slot, :, :, pl.ds(0, SEG)], load_sem.at[slot, 0]
+            ),
+            pltpu.make_async_copy(
+                left.at[:, rows_m, col_m], xb.at[slot, :, :, pl.ds(SEG, SEG)], load_sem.at[slot, 1]
+            ),
             pltpu.make_async_copy(right.at[:, :, cols], gg.at[slot], load_sem.at[slot, 2]),
         ]
 
@@ -937,23 +963,6 @@
 
     def twin_copy(b, slot):
         return remote(sent.at[slot], tw.at[b], tw_send.at[slot], tw_recv.at[b], twin)
-
-    def out_copy(b, go):
-        @pl.when(b < 4)
-        def _():
-            go(f_out.at[aligned(b * SEG, SEG)])
-
-        @pl.when((b >= 4) & (b < 8))
-        def _():
-            go(f_in.at[:, aligned((b - 4) * D, D)])
-
-        @pl.when(b == 8)
-        def _():
-            go(f_o.at[...])
-
-        @pl.when(b >= 9)
-        def _():
-            go(f_qkv.at[:, aligned((b - 9) * D, D)])
 
     def piece(j):
         b, k = j // PARTS, lax.rem(j, PARTS)
@@ -1076,7 +1085,7 @@
 
         @pl.when((t == STAGES - 1) & (k == PARTS - 1))
         def _():
-            out_copy(b, lambda dst: pltpu.make_async_copy(fin.at[b], dst, fin_sem.at[b]).start())
+            pltpu.make_async_copy(fin.at[b], sums.at[b], fin_sem.at[b]).start()
 
     def small_twin():
         return remote(sm_tx.at[0], sm_tw, sm_send.at[0], sm_recv.at[0], twin)
@@ -1086,12 +1095,14 @@
 
     start_loads(0, 0)
 
-    def product(slot, left):
-        return tn(left[slot].reshape(UNITS * SEG, SEG), gg[slot].reshape(UNITS * SEG, D))
+    def product(b, slot):
+        both = tn(xb[slot].reshape(UNITS * SEG, D), gg[slot].reshape(UNITS * SEG, D))
+        sent[slot] = both[:SEG].astype(BF)
+        own[b] = both[SEG:]
 
     wait_loads(0)
     start_loads(1, 1)
-    sent[0] = product(0, xt).astype(BF)
+    product(0, 0)
     ends = z_at * (3 - z_at)
     pl.semaphore_wait(barrier, 4 + ends // 2)
     twin_copy(0, 0).start()
@@ -1122,10 +1133,8 @@
                 def _():
                     twin_copy(now - 2, slot).wait_send()
 
-                sent[slot] = product(slot, xt).astype(BF)
+                product(now, slot)
                 twin_copy(now, slot).start()
-
-            own[now] = product(slot, xm)
 
         @pl.when(fresh & (now > 0) & (now <= BLOCKS_G))
         def _():
@@ -1172,7 +1181,7 @@
 
         @pl.when(k == 0)
         def _():
-            out_copy(b, lambda dst: pltpu.make_async_copy(fin.at[b], dst, fin_sem.at[b]).wait())
+            pltpu.make_async_copy(fin.at[b], sums.at[b], fin_sem.at[b]).wait()
 
         return carry
 
@@ -1187,17 +1196,13 @@
     return pl.pallas_call(
         reduce_kernel,
         out_shape=(
-            shape((SEG, 3 * D), BF),
-            shape((SEG, D), BF),
-            shape((SEG, FF), BF),
-            shape((FF // 2, D), BF),
+            shape((BLOCKS_G, SEG, D), BF),
             shape((SMALL, D), F32),
         ),
         in_specs=[hbm] * 8 + [vmem, vmem],
-        out_specs=(hbm, hbm, hbm, hbm, vmem),
+        out_specs=(hbm, vmem),
         scratch_shapes=[
-            pltpu.VMEM((2, UNITS, SEG, SEG), BF),
-            pltpu.VMEM((2, UNITS, SEG, SEG), BF),
+            pltpu.VMEM((2, UNITS, SEG, D), BF),
             pltpu.VMEM((2, UNITS, SEG, D), BF),
             pltpu.VMEM((BLOCKS_G, SEG, D), F32),
             pltpu.VMEM((2, SEG, D), BF),
@@ -1223,14 +1228,30 @@
             dma((4,)),
         ],
         compiler_params=pltpu.CompilerParams(
-            collective_id=1, has_side_effects=True, vmem_limit_bytes=60 * 2**20
+            collective_id=1, has_side_effects=True, vmem_limit_bytes=62 * 2**20
         ),
         cost_estimate=pl.CostEstimate(flops=22 * 10**9, bytes_accessed=64 * 2**20, transcendentals=0),
     )(*operands)
 
 
 def finish_kernel(
-    counts, lasts, tops, backs, tail, f_qkv, f_o, f_in, f_out, small, text, text_g, memory, mem_g, qkv_g, o_g, in_g, out_g, gains_g, biases_g
+    counts,
+    lasts,
+    tops,
+    backs,
+    tail,
+    sums,
+    small,
+    text,
+    text_g,
+    memory,
+    mem_g,
+    qkv_g,
+    o_g,
+    in_g,
+    out_g,
+    gains_g,
+    biases_g,
 ):
     step = pl.program_id(0)
     place = lax.axis_index("pipe")
@@ -1241,15 +1262,17 @@
         limit = jnp.where(count > 1, TEXT if k == 0 else last, last if k == 0 else 0)
         text[:, k, :] = jnp.where(row < limit, tops[k].astype(F32), 0.0)
         text_g[:, k, :] = backs[k].astype(F32)
-    qkv_g[...] = f_qkv[...].astype(F32)
-    o_g[...] = f_o[...].astype(F32)
-    in_g[...] = f_in[...].astype(F32)
-    out_g[...] = f_out[...].astype(F32)
+    out_g[...] = sums[:4].astype(F32)
+    for j in range(4):
+        in_g[:, j * D : (j + 1) * D] = sums[4 + j].astype(F32)
+    o_g[...] = sums[8].astype(F32)
+    for j in range(3):
+        qkv_g[:, j * D : (j + 1) * D] = sums[9 + j].astype(F32)
 
     @pl.when(step == 0)
     def _():
         ends = tail[...].astype(F32)
-        memory[0] = jnp.where(count > 1, ends[1], ends[0])[TAIL - MEM :, :]
+        memory[:, 0, :] = jnp.where(count > 1, ends[1], ends[0])[TAIL - MEM :, :]
         width = D // 4
         for index in range(4):
 
@@ -1257,14 +1280,15 @@
             def _():
                 mem_g[...] = small[SMALL - MEM :, index * width : (index + 1) * width]
 
-        gains_g[...] = small[0:1, :]
-        biases_g[...] = small[1:6, :]
+        gains_g[...] = small[0]
+        for index in range(5):
+            biases_g[index * D : (index + 1) * D] = small[1 + index]
 
 
 def finish(operands):
     shape = jax.ShapeDtypeStruct
     smem = pl.BlockSpec(memory_space=pltpu.SMEM)
-    steps = 8
+    steps = 4
     row = SEG // steps
 
     def split(rows, cols):
@@ -1275,7 +1299,8 @@
 
     pair = pl.BlockSpec((2, row, D), lambda i: (0, i, 0))
     pair_out = pl.BlockSpec((row, 2, D), lambda i: (i, 0, 0))
-    grads = [split(row, 3 * D), split(row, D), split(row, FF), split(4 * row, D)]
+    out_spec = pl.BlockSpec((4, row, D), lambda i: (0, i, 0))
+    grads = [split(row, 3 * D), split(row, D), split(row, FF), out_spec]
     counts, lasts, tops, backs, *rest = operands
     return pl.pallas_call(
         finish_kernel,
@@ -1283,14 +1308,14 @@
         out_shape=(
             shape((TEXT, 2, D), F32),
             shape((TEXT, 2, D), F32),
-            shape((1, MEM, D), F32),
+            shape((MEM, 1, D), F32),
             shape((MEM, D // 4), F32),
             shape((SEG, 3 * D), F32),
             shape((SEG, D), F32),
             shape((SEG, FF), F32),
-            shape((FF // 2, D), F32),
-            shape((1, D), F32),
-            shape((5, D), F32),
+            shape((4, SEG, D), F32),
+            shape((D,), F32),
+            shape((5 * D,), F32),
         ),
         in_specs=[
             smem,
@@ -1298,19 +1323,19 @@
             pair,
             pair,
             pl.BlockSpec((2, TAIL, D), lambda i: (0, SEG // TAIL - 1, 0)),
-            *grads,
+            pl.BlockSpec((BLOCKS_G, row, D), lambda i: (0, i, 0)),
             whole(SMALL, D),
         ],
         out_specs=(
             pair_out,
             pair_out,
-            whole(1, MEM, D),
+            whole(MEM, 1, D),
             whole(MEM, D // 4),
             *grads,
-            whole(1, D),
-            whole(5, D),
+            whole(D),
+            whole(5 * D),
         ),
-        compiler_params=pltpu.CompilerParams(vmem_limit_bytes=62 * 2**20),
+        compiler_params=pltpu.CompilerParams(vmem_limit_bytes=FINISH * 2**20),
     )(counts, lasts, tops, backs, tops, *rest)
 
 
@@ -1348,7 +1373,10 @@
     mine_small = jnp.concatenate([vec_mine, memg], 0)
     small = mine_small + from_partner(jnp.concatenate([vec_theirs, memg], 0), "pipe", 0)
     *grads, small = lax.psum((*sums, small), "items")
-    return (*grads, small)
+    qkv, out_proj, up, down = grads
+    columns = [up[:, j * D : (j + 1) * D] for j in range(4)] + [out_proj]
+    columns += [qkv[:, j * D : (j + 1) * D] for j in range(3)]
+    return jnp.concatenate([down.reshape(4, SEG, D), jnp.stack(columns)], 0), small
 
 
 def per_device(
@@ -1369,27 +1397,25 @@
     pad = ((0, 0), (0, SEG - TEXT), (0, 0))
     x_own = jnp.pad(text_in[0], pad)
     c_own = jnp.pad(text_cot[0], pad)
-    mem_own = jnp.pad(memory, ((0, 16 - MEM), (0, 2 * LANE - memory.shape[1])))
-    mcot_own = jnp.pad(memory_cot[0], ((TAIL - MEM, 0), (0, 0)))
-    vec_own = jnp.concatenate(
-        [gains[None], biases.reshape(5, D), jnp.zeros((2, D), gains.dtype)], 0
-    ).astype(F32)
+    mcot = memory_cot.astype(F32).transpose(1, 0, 2)
+    vec_own = jnp.concatenate([gains, biases, jnp.zeros(2 * D, gains.dtype)]).reshape(8, D).astype(F32)
     xs, ctxs, hids, acts, own_top, gds, gus, gbs, gps, own_back, _, vecg, memg = relay(
-        (x_own, c_own, mem_own, mcot_own, counts, last_lengths, w_qkv, w_o, w_in, w_out, vec_own)
+        (x_own, c_own, memory, mcot, counts, last_lengths, w_qkv, w_o, w_in, w_out, vec_own)
     )
     sum_all = reduce_grads if lax.axis_size("items") == 8 else functools.partial(sum_grads, member)
     sums = sum_all((xs, ctxs, hids, acts, gps, gbs, gus, gds, vecg, memg))
-    text, text_grad, last_memory, memory_grad, *grads, gains_grad, biases_grad = finish(
+    text, text_grad, last_memory, memory_grad, *grads, down, gains_grad, biases_grad = finish(
         (counts, last_lengths, own_top, own_back, *sums)
     )
     return (
         text.transpose(1, 0, 2)[None],
-        last_memory,
+        last_memory.transpose(1, 0, 2),
         text_grad.transpose(1, 0, 2)[None],
         memory_grad,
         *grads,
-        gains_grad.reshape(D),
-        biases_grad.reshape(5 * D),
+        down.reshape(FF // 2, D),
+        gains_grad,
+        biases_grad,
     )
 
 

time: 393 us -> 388 us (0.987)
  local copies, waits for them, and re-layouts: 10.7 us -> 4.28 us
where the time goes in v5:
time: 388 us; the launch traced here: 385 us
  Pallas kernels  378 us (97%)
  local copies, waits for them, and re-layouts  4.28 us (1%)
    pallas_call x1, Pallas kernels, relay(): pl.pallas_call(relay_kernel, out_shape=results, in_specs=in_specs, out_sp...  218 us
    pallas_call x1, Pallas kernels, reduce_grads(): pl.pallas_call(reduce_kernel, out_shape=(shape((BLOCKS_G, SEG, D), BF), s...  149 us
    pallas_call x1, Pallas kernels, finish(): pl.pallas_call(finish_kernel, grid=(steps,), out_shape=(shape((TEXT, 2, D...  10.9 us

profile of v5, /device:TPU:0, one launch (start us, length us, event | category | flops | bytes accessed | tf_op | source)
XLA Modules:
  0.0 384.9 jit_solution(13125555275923167771)
XLA Ops:
  0.6 0.0 copy-start
  0.7 0.8 maximum_convert_fusion
  1.5 0.6 reshape.28.vec_own
  2.1 1.4 bitcast_convert_fusion.mcot_raw
  3.4 1.4 copy.29
  4.8 1.1 pad.7.x_own
  5.9 0.0 copy-done
  5.9 0.1 copy.28
  6.0 1.1 pad.8.c_own
  7.1 218.0 %shard_map.195 = (bf16[4,384,768]{2,1,0:T(8,128)(2,1)}, bf16[4,384,768]{2,1,0:T(8,128)(2,1)}, bf16[4,384,768]{2,1,0:T(8,128)(2,1)}, bf16[4,1536,768]{2,1,0:T(8,1...) custom-call(bf16[2,384,768]{2,1,0:T(8,128)(2,1)} %pad.7.x_own, ...), custom_call_target="tpu_custom_call" | custom-call | flops 80000000000 | bytes 83886080 | tf_op jit(solution)/shard_map/pallas_call | solution.py:820
  225.2 148.6 %shard_map.196 = (bf16[12,384,768]{2,1,0:T(8,128)(2,1)}, f32[40,768]{1,0:T(8,128)}) custom-call(bf16[4,384,768]{2,1,0:T(8,128)(2,1)} %get-tuple-element.36.xs, bf16[4,384,768]{2,1,0:T(8,128)(2,1)} %get-tuple-element.37.ctxs, bf16[4,384,768]{2,1,0:T(8,128)(2,1)} %get-tuple-element.38.hids, bf16[4,1536,768]{2,1,0:T(8,128)(2,1)} %get-tuple-element.39.acts, ...), custom_call_target="tpu_custom_call" | custom-call | flops 22000001024 | bytes 67108864 | tf_op jit(solution)/shard_map/pallas_call | solution.py:1196
  373.8 10.9 %shard_map.197 = (f32[364,2,768]{2,1,0:T(2,128)}, f32[364,2,768]{2,1,0:T(2,128)}, f32[10,1,768]{2,1,0:T(1,128)}, f32[10,192]{1,0:T(8,128)}, f32[384,2304]{1,0:T(...) custom-call(s32[4]{0:T(128)} %counts.3, s32[4]{0:T(128)} %lasts.3, ...), custom_call_target="tpu_custom_call" | custom-call | tf_op jit(solution)/shard_map/pallas_call | solution.py:1305
  (1 shorter events, 0.0 us)
Async XLA Ops:
  0.6 5.3 %copy-start = (bf16[1,2,364,768]{3,1,2,0:T(2,128)(2,1)S(1)}, bf16[1,2,364,768]{3,1,2,0:T(2,128)(2,1)}, u32[]{:S(2)}) copy-start(bf16[1,2,364,768]{3,1,2,0:T(2,128)(2,1)} %param.22) | copy-start | bytes 3354628

commit v6 on v5

--- a/solution.py
+++ b/solution.py
@@ -139,7 +139,7 @@
     outb,
     gdb,
     delta,
-    parts,
+    rest,
     w_local,
     w_send,
     w_recv,
@@ -264,7 +264,6 @@
         m_home.start()
 
     rhs[...] = jnp.zeros_like(rhs)
-    ones = jnp.ones((2 * LANE, LANE), BF)
     vecg[...] = jnp.zeros_like(vecg)
     memg[...] = jnp.zeros_like(memg)
     low = lax.broadcasted_iota(jnp.int32, (SEG, LANE), 1) < 64
@@ -416,9 +415,10 @@
                         raised * (1.0 / total)
                     ).astype(BF)
                     st[u, rows, 2 * p + h : 2 * p + h + 1] = top + jnp.log2(total)
-            ctx[u, :, p * LANE : (p + 1) * LANE] = nn(
-                big[b * 2 * SEG : b * 2 * SEG + SEG, :], stv[b]
-            ).astype(BF)
+            mixed = nn(big[b * 2 * SEG : b * 2 * SEG + SEG, :], stv[b])
+            rounded = mixed.astype(BF)
+            ctx[u, :, p * LANE : (p + 1) * LANE] = rounded
+            rest[u, :, p * LANE : (p + 1) * LANE] = (mixed - rounded.astype(F32)).astype(BF)
         pltpu.make_async_copy(ctx.at[u], ctxs.at[u], ctx_sem.at[u]).start()
 
         @pl.when(u == 0)
@@ -631,7 +631,12 @@
             vecg[BO : BO + 1, :] += row_sum(branch.astype(F32))
             n1s[u, rows, :] = first_grad
         gb_copy(u).start()
+        head = lax.broadcasted_iota(jnp.int32, (D, LANE), 0) // 64
+        heads = (head == lax.broadcasted_iota(jnp.int32, (D, LANE), 1)).astype(F32).astype(BF)
         grad_ctx = nt(gdb[...], wo[...]).astype(BF)
+        product = grad_ctx.astype(F32) * (ctx[u].astype(F32) + rest[u].astype(F32))
+        high = product.astype(BF)
+        delta[...] = nn(high, heads) + nn((product - high.astype(F32)).astype(BF), heads)
         ctx[u] = grad_ctx
         mask = key_mask(length)
 
@@ -658,22 +663,9 @@
                     one = slice(2 * p + h, 2 * p + h + 1)
                     probs = jnp.exp2(sc[b, rows, cols] * LOG2E + mask - st[u, rows, one])
                     big[base + rows.start : base + rows.stop, cols] = probs.astype(BF)
-                    sc[b, rows, cols] = probs
-                    product = probs * sd[b, rows, cols]
-                    third = product[:, :LANE] + product[:, LANE : 2 * LANE] + product[:, 2 * LANE :]
-                    high = third.astype(BF)
-                    at = 2 * h * LANE
-                    parts[b, rows, at : at + LANE] = high
-                    parts[b, rows, at + LANE : at + 2 * LANE] = (third - high.astype(F32)).astype(BF)
-            for h in range(2):
-                delta[b, h] = nn(parts[b, :, 2 * h * LANE : 2 * (h + 1) * LANE], ones)
-            for rows in BLOCKS:
-                for h in range(2):
-                    for third in range(3):
-                        cols = slice(h * SEG + third * LANE, h * SEG + (third + 1) * LANE)
-                        big[base + SEG + rows.start : base + SEG + rows.stop, cols] = (
-                            sc[b, rows, cols] * (sd[b, rows, cols] - delta[b, h, rows, :])
-                        ).astype(BF)
+                    big[base + SEG + rows.start : base + SEG + rows.stop, cols] = (
+                        probs * (sd[b, rows, cols] - delta[rows, one])
+                    ).astype(BF)
             packed[u, :, p * LANE : (p + 1) * LANE] = (
                 nn(big[base + SEG : base + 2 * SEG, :], stk[b]) * 0.125
             ).astype(BF)
@@ -809,8 +801,8 @@
         pltpu.VMEM((SEG, D), BF),
         pltpu.VMEM((2, SEG, D), BF),
         pltpu.VMEM((SEG, D), BF),
-        pltpu.VMEM((2, 2, SEG, LANE), F32),
-        pltpu.VMEM((2, SEG, 4 * LANE), BF),
+        pltpu.VMEM((SEG, LANE), F32),
+        pltpu.VMEM(rows, BF),
     ]
     counts = [5, 5, 5, 3, 3, 3, 2, 4, 4, 4, 2, 4, 4, 4, 0, 4, 0, 0, 2, 2, 2, 4, 1, 2, 1, 2, 2]
     scratch += [pltpu.SemaphoreType.DMA((n,)) if n else pltpu.SemaphoreType.DMA for n in counts]

time: 388 us -> 382 us (0.985)
  Pallas kernels: 378 us -> 372 us
    pallas_call x1, Pallas kernels: 218 us -> 213 us  [relay(): pl.pallas_call(relay_kernel, out_shape=results, in_specs=in_specs, out_sp...]
where the time goes in v6:
time: 382 us; the launch traced here: 380 us
  Pallas kernels  372 us (97%)
  local copies, waits for them, and re-layouts  4.28 us (1%)
    pallas_call x1, Pallas kernels, relay(): pl.pallas_call(relay_kernel, out_shape=results, in_specs=in_specs, out_sp...  213 us
    pallas_call x1, Pallas kernels, reduce_grads(): pl.pallas_call(reduce_kernel, out_shape=(shape((BLOCKS_G, SEG, D), BF), s...  149 us
    pallas_call x1, Pallas kernels, finish(): pl.pallas_call(finish_kernel, grid=(steps,), out_shape=(shape((TEXT, 2, D...  10.9 us

profile of v6, /device:TPU:0, one launch (start us, length us, event | category | flops | bytes accessed | tf_op | source)
XLA Modules:
  0.0 379.5 jit_solution(16757615408827939961)
XLA Ops:
  0.6 0.0 copy-start
  0.7 0.8 maximum_convert_fusion
  1.5 0.6 reshape.28.vec_own
  2.1 1.4 bitcast_convert_fusion.mcot_raw
  3.4 1.4 copy.29
  4.8 1.1 pad.7.x_own
  5.9 0.0 copy-done
  5.9 0.1 copy.28
  6.0 1.1 pad.8.c_own
  7.1 212.6 %shard_map.195 = (bf16[4,384,768]{2,1,0:T(8,128)(2,1)}, bf16[4,384,768]{2,1,0:T(8,128)(2,1)}, bf16[4,384,768]{2,1,0:T(8,128)(2,1)}, bf16[4,1536,768]{2,1,0:T(8,1...) custom-call(bf16[2,384,768]{2,1,0:T(8,128)(2,1)} %pad.7.x_own, ...), custom_call_target="tpu_custom_call" | custom-call | flops 80000000000 | bytes 83886080 | tf_op jit(solution)/shard_map/pallas_call | solution.py:812
  219.7 148.7 %shard_map.196 = (bf16[12,384,768]{2,1,0:T(8,128)(2,1)}, f32[40,768]{1,0:T(8,128)}) custom-call(bf16[4,384,768]{2,1,0:T(8,128)(2,1)} %get-tuple-element.36.xs, bf16[4,384,768]{2,1,0:T(8,128)(2,1)} %get-tuple-element.37.ctxs, bf16[4,384,768]{2,1,0:T(8,128)(2,1)} %get-tuple-element.38.hids, bf16[4,1536,768]{2,1,0:T(8,128)(2,1)} %get-tuple-element.39.acts, ...), custom_call_target="tpu_custom_call" | custom-call | flops 22000001024 | bytes 67108864 | tf_op jit(solution)/shard_map/pallas_call | solution.py:1188
  368.4 10.9 %shard_map.197 = (f32[364,2,768]{2,1,0:T(2,128)}, f32[364,2,768]{2,1,0:T(2,128)}, f32[10,1,768]{2,1,0:T(1,128)}, f32[10,192]{1,0:T(8,128)}, f32[384,2304]{1,0:T(...) custom-call(s32[4]{0:T(128)} %counts.3, s32[4]{0:T(128)} %lasts.3, ...), custom_call_target="tpu_custom_call" | custom-call | tf_op jit(solution)/shard_map/pallas_call | solution.py:1297
  (1 shorter events, 0.0 us)
Async XLA Ops:
  0.6 5.3 %copy-start = (bf16[1,2,364,768]{3,1,2,0:T(2,128)(2,1)S(1)}, bf16[1,2,364,768]{3,1,2,0:T(2,128)(2,1)}, u32[]{:S(2)}) copy-start(bf16[1,2,364,768]{3,1,2,0:T(2,128)(2,1)} %param.22) | copy-start | bytes 3354628
